TPU v7x, 32 devices: a whole 2x2x4 slice. The times are simulated.
32 devices in a mesh: blk: 16 (over z, y, core), dp: 2 (over x).
Axes of the slice: x: 2, y: 2, z: 4, core: 2. Of those that a mesh axis runs over, the one named last changes fastest.
Arguments:
- tokens: bfloat16 [16, 768, 576], P('blk', 'dp'), may hold values from -6 to 6
- cotangent: bfloat16 [16, 768, 576], P('blk', 'dp'), may hold values from -0.59765625 to 0.59765625
- w_gate: bfloat16 [16, 576, 1536], P('blk'), may hold values from -0.25 to 0.25
- w_up: bfloat16 [16, 576, 1536], P('blk'), may hold values from -0.25 to 0.25
- w_down: bfloat16 [16, 1536, 576], P('blk'), may hold values from -0.15625 to 0.15625
Outputs:
- d_tokens: bfloat16 [16, 768, 576], P('blk', 'dp')
- grad_gate: bfloat16 [16, 576, 1536], P('blk')
- grad_up: bfloat16 [16, 576, 1536], P('blk')
- grad_down: bfloat16 [16, 1536, 576], P('blk')
All inputs are finite; a program needn't handle non-finite values.
Results may differ from a plain program's by a relative error of at most 0.027.
Values may be sent and summed in bfloat16 or wider, within the bound.
No kernel may reach another device: no remote copies, remote signals or barrier semaphores. Data moves between devices by JAX's collectives and lax.ppermute only.
A program may use at most 64 MiB of HBM per device.

v0:
```python
import jax
import jax.numpy as jnp
from jax import lax
from jax.sharding import PartitionSpec as P


def from_behind(x, axis, by):
    length = lax.axis_size(axis)
    return lax.ppermute(x, axis, [(i, (i + by) % length) for i in range(length)])


def sublayer_saved(vector, w_first, w_second):
    vf = vector.astype(jnp.float32)
    inverse = lax.rsqrt(jnp.mean(vf * vf, axis=-1, keepdims=True) + 1e-05)
    normed = vf * inverse
    zed = normed.astype(jnp.bfloat16)
    pre_g = jnp.dot(zed, w_first, preferred_element_type=jnp.float32)
    pre_u = jnp.dot(zed, w_second, preferred_element_type=jnp.float32)
    active = (jax.nn.silu(pre_g) * pre_u).astype(jnp.bfloat16)
    return (inverse, normed, zed, pre_g, pre_u, active)


def sublayer_fwd(vector, w_first, w_second, w_lower):
    saved = sublayer_saved(vector, w_first, w_second)
    output = (
        vector.astype(jnp.float32) + jnp.dot(saved[5], w_lower, preferred_element_type=jnp.float32)
    ).astype(jnp.bfloat16)
    return (output, saved)


def sublayer_bwd(incoming, saved, w_first, w_second, w_lower):
    inverse, normed, zed, pre_g, pre_u, active = saved
    d_lower = jnp.dot(active.T, incoming, preferred_element_type=jnp.float32)
    d_active = jnp.dot(incoming, w_lower.T, preferred_element_type=jnp.float32)
    sigma = jax.nn.sigmoid(pre_g)
    d_gate = (d_active * pre_u * sigma * (1.0 + pre_g * (1.0 - sigma))).astype(jnp.bfloat16)
    d_upper = (d_active * pre_g * sigma).astype(jnp.bfloat16)
    g_first = jnp.dot(zed.T, d_gate, preferred_element_type=jnp.float32)
    g_second = jnp.dot(zed.T, d_upper, preferred_element_type=jnp.float32)
    d_zed = jnp.dot(d_gate, w_first.T, preferred_element_type=jnp.float32) + jnp.dot(
        d_upper, w_second.T, preferred_element_type=jnp.float32
    )
    inner = jnp.mean(d_zed * normed, axis=-1, keepdims=True)
    d_vector = (incoming.astype(jnp.float32) + inverse * (d_zed - normed * inner)).astype(
        jnp.bfloat16
    )
    return (
        d_vector,
        g_first.astype(jnp.bfloat16),
        g_second.astype(jnp.bfloat16),
        d_lower.astype(jnp.bfloat16),
    )


def local(tokens, cotangent, w_gate, w_up, w_down):
    inputs = tokens[0]
    grads_in = cotangent[0]
    gate_own = w_gate[0]
    up_own = w_up[0]
    down_own = w_down[0]
    middle, saved_a = sublayer_fwd(inputs, gate_own, up_own, down_own)
    gate_prev, up_prev, down_prev = from_behind((gate_own, up_own, down_own), "blk", 1)
    saved_b = sublayer_saved(middle, gate_prev, up_prev)
    d_middle, b_gate, b_up, b_down = sublayer_bwd(grads_in, saved_b, gate_prev, up_prev, down_prev)
    b_gate, b_up, b_down = from_behind((b_gate, b_up, b_down), "blk", -1)
    d_inputs, a_gate, a_up, a_down = sublayer_bwd(d_middle, saved_a, gate_own, up_own, down_own)
    part_gate = (a_gate.astype(jnp.float32) + b_gate.astype(jnp.float32)).astype(jnp.bfloat16)
    part_up = (a_up.astype(jnp.float32) + b_up.astype(jnp.float32)).astype(jnp.bfloat16)
    part_down = (a_down.astype(jnp.float32) + b_down.astype(jnp.float32)).astype(jnp.bfloat16)
    sum_gate, sum_up, sum_down = (
        lax.psum(part_gate, "dp").astype(jnp.float32),
        lax.psum(part_up, "dp").astype(jnp.float32),
        lax.psum(part_down, "dp").astype(jnp.float32),
    )
    return (
        d_inputs[None],
        sum_gate.astype(jnp.bfloat16)[None],
        sum_up.astype(jnp.bfloat16)[None],
        sum_down.astype(jnp.bfloat16)[None],
    )


def solution(mesh):
    in_specs = (
        P("blk", "dp", None),
        P("blk", "dp", None),
        P("blk", None, None),
        P("blk", None, None),
        P("blk", None, None),
    )
    out_specs = (
        P("blk", "dp", None),
        P("blk", None, None),
        P("blk", None, None),
        P("blk", None, None),
    )
    return jax.shard_map(local, mesh=mesh, in_specs=in_specs, out_specs=out_specs, check_vma=False)
```

profile of v0, /device:TPU:0, one launch (start us, length us, event | category | flops | bytes accessed | tf_op | source)
XLA Modules:
  0.0 291.2 jit_solution(16881681200773526938)
XLA Ops:
  7.2 0.0 all-reduce.3.cloned.1.call-start
  7.2 0.5 collective-permute-start
  7.7 2.6 collective-permute-start.1
  10.3 0.1 collective-permute-start.2
  10.4 1.1 fusion.15
  11.6 0.0 copy-start
  11.6 0.0 copy-start.5
  11.6 2.9 fusion.24
  14.5 0.0 copy-done
  14.5 0.0 copy-done.5
  14.5 0.0 copy-start.4
  14.5 1.4 multiply_convert_fusion.5
  15.9 0.1 copy-done.4
  16.0 1.1 multiply_reduce_fusion.1
  17.1 0.1 multiply_convert_fusion.7
  17.2 53.9 %collective-permute-done.2 = bf16[576,1536]{1,0:T(8,128)(2,1)S(1)} collective-permute-done((bf16[576,1536]{1,0:T(8,128)(2,1)}, bf16[576,1536]{1,0:T(8,128)(2,1)S(1)}, u32[]{:S(2)}, u32[]{:S(2)}) %collective-permute-start.2) | collective-permute-done | bytes 1769504 | tf_op jit(solution)/shard_map/ppermute | solution.py:9
  71.0 1.1 fusion.38
  72.2 0.0 copy-start.3
  72.2 0.0 collective-permute-done.1
  72.2 1.1 fusion.37
  73.3 0.0 copy-done.3
  73.3 1.2 convolution_convert_fusion
  74.5 0.0 collective-permute-done
  74.5 1.9 multiply_convert_fusion.4
  76.4 1.1 convolution_convert_fusion.4
  77.5 1.1 convolution_convert_fusion.2
  78.6 0.1 collective-permute-start.4
  78.6 2.4 collective-permute-start.3
  81.0 0.1 collective-permute-start.5
  81.1 1.1 fusion.39
  82.2 1.2 multiply_reduce_fusion
  83.4 0.2 add_convert_fusion.3
  83.6 1.8 multiply_convert_fusion.1
  85.4 51.2 %collective-permute-done.5 = bf16[1536,576]{0,1:T(8,128)(2,1)S(1)} collective-permute-done((bf16[1536,576]{0,1:T(8,128)(2,1)S(1)}, bf16[1536,576]{0,1:T(8,128)(2,1)S(1)}, u32[]{:S(2)}, u32[]{:S(2)}) %collective-permute-start.5) | collective-permute-done | bytes 1769504 | tf_op jit(solution)/shard_map/ppermute | solution.py:9
  136.6 2.3 fusion.2
  138.9 0.0 collective-permute-done.4
  138.9 2.3 fusion.1
  141.2 0.0 collective-permute-done.3
  141.2 2.3 fusion
  143.5 0.0 all-reduce.3.cloned.1.call-update
  143.5 0.0 copy-start.6
  143.5 2.7 fusion.33
  146.2 0.0 copy-done.6
  146.2 1.1 fusion.10
  147.4 1.0 fusion.18
  148.4 129.7 %all-reduce.3.cloned.1.call-done = (bf16[1,576,1536]{2,1,0:T(8,128)(2,1)}, bf16[1,576,1536]{2,1,0:T(8,128)(2,1)}, bf16[1,1536,576]{1,2,0:T(8,128)(2,1)}) async-done(((bf16[1,576,1536]{2,1,0:T(8,128)(2,1)}, bf16[1,576,1536]{2,1,0:T(8,128)(2,1)}, bf16[1,1536,576]{1,2,0:T(8,128)(2,1)}), (bf16[1,576,1536]{2,1,0:T(8,128)(2,1)}, bf16[1,576,1536]{2,1,0:T(8,128)(2,1)}, ...) | async-done | bytes 5308432 | tf_op jit(solution)/shard_map/psum | solution.py:71
  278.1 0.0 copy-start.2
  278.1 2.9 %copy.12 = bf16[1,576,1536]{2,1,0:T(8,128)(2,1)} copy(bf16[1,576,1536]{2,1,0:T(8,128)(2,1)} %get-tuple-element.20) | data formatting | bytes 3538944
  281.0 0.0 copy-done.2
  281.0 0.0 copy-start.1
  281.0 1.2 copy.13
  282.2 0.9 copy-done.1
  283.1 1.2 copy.14
  (4 shorter events, 0.0 us)
Async XLA Ops:
  7.2 270.9 %all-reduce.3.cloned.1.call-start = ((), (), s32[]{:S(2)}) async-start(), calls=%async_computation | async-start | bytes 10616832 | tf_op jit(solution)/shard_map/psum | solution.py:71
  7.2 67.3 %collective-permute-start = (bf16[1536,576]{0,1:T(8,128)(2,1)}, bf16[1536,576]{0,1:T(8,128)(2,1)S(1)}, u32[]{:S(2)}, u32[]{:S(2)}) collective-permute-start(bf16[1536,576]{0,1:T(8,128)(2,1)} %bitcast.96), channel_id=1, source_target_pairs={{0,2},{2,4},{4,6},{6,8},{8,10},{10,12},{12,14},{14,16},{16,18},{18... | collective-permute-start | bytes 5308424 | tf_op jit(solution)/shard_map/ppermute | solution.py:9
  7.7 64.5 %collective-permute-start.1 = (bf16[576,1536]{1,0:T(8,128)(2,1)}, bf16[576,1536]{1,0:T(8,128)(2,1)S(1)}, u32[]{:S(2)}, u32[]{:S(2)}) collective-permute-start(bf16[576,1536]{1,0:T(8,128)(2,1)} %bitcast.98), channel_id=1, source_target_pairs={{0,2},{2,4},{4,6},{6,8},{8,10},{10,12},{12,14},{14,16},{16,18},{18... | collective-permute-start | bytes 5308424 | tf_op jit(solution)/shard_map/ppermute | solution.py:9
  10.3 60.7 %collective-permute-start.2 = (bf16[576,1536]{1,0:T(8,128)(2,1)}, bf16[576,1536]{1,0:T(8,128)(2,1)S(1)}, u32[]{:S(2)}, u32[]{:S(2)}) collective-permute-start(bf16[576,1536]{1,0:T(8,128)(2,1)} %bitcast.97), channel_id=1, source_target_pairs={{0,2},{2,4},{4,6},{6,8},{8,10},{10,12},{12,14},{14,16},{16,18},{18... | collective-permute-start | bytes 5308424 | tf_op jit(solution)/shard_map/ppermute | solution.py:9
  11.6 2.9 copy-start
  11.6 2.9 copy-start.5
  14.5 1.5 copy-start.4
  72.2 1.1 copy-start.3
  78.6 60.3 %collective-permute-start.4 = (bf16[576,1536]{1,0:T(8,128)(2,1)S(1)}, bf16[576,1536]{1,0:T(8,128)(2,1)S(1)}, u32[]{:S(2)}, u32[]{:S(2)}) collective-permute-start(bf16[576,1536]{1,0:T(8,128)(2,1)S(1)} %convolution_convert_fusion.2), channel_id=1, source_target_pairs={{0,30},{2,0},{4,2},{6,4},{8,6},{10,8},{12,10},{14,12},{16,14},{18,... | collective-permute-start | bytes 5308424 | tf_op jit(solution)/shard_map/ppermute | solution.py:9
  78.6 62.5 %collective-permute-start.3 = (bf16[576,1536]{1,0:T(8,128)(2,1)S(1)}, bf16[576,1536]{1,0:T(8,128)(2,1)S(1)}, u32[]{:S(2)}, u32[]{:S(2)}) collective-permute-start(bf16[576,1536]{1,0:T(8,128)(2,1)S(1)} %convolution_convert_fusion.4), channel_id=1, source_target_pairs={{0,30},{2,0},{4,2},{6,4},{8,6},{10,8},{12,10},{14,12},{16,14},{18,... | collective-permute-start | bytes 5308424 | tf_op jit(solution)/shard_map/ppermute | solution.py:9
  81.0 55.6 %collective-permute-start.5 = (bf16[1536,576]{0,1:T(8,128)(2,1)S(1)}, bf16[1536,576]{0,1:T(8,128)(2,1)S(1)}, u32[]{:S(2)}, u32[]{:S(2)}) collective-permute-start(bf16[1536,576]{0,1:T(8,128)(2,1)S(1)} %convolution_convert_fusion), channel_id=1, source_target_pairs={{0,30},{2,0},{4,2},{6,4},{8,6},{10,8},{12,10},{14,12},{16,14},{18,... | collective-permute-start | bytes 5308424 | tf_op jit(solution)/shard_map/ppermute | solution.py:9
  143.5 2.7 copy-start.6
  278.1 2.9 %copy-start.2 = (bf16[1,576,1536]{2,1,0:T(8,128)(2,1)S(1)}, bf16[1,576,1536]{2,1,0:T(8,128)(2,1)}, u32[]{:S(2)}) copy-start(bf16[1,576,1536]{2,1,0:T(8,128)(2,1)} %get-tuple-element.21) | copy-start | bytes 5308420
  281.0 2.1 copy-start.1
Sparse Core Ops, SparseCore 0:
  143.6 134.4 all-reduce.2
where the time goes:
time: 291 us
  waiting for transfers between devices  235 us (81%)
  matrix products  27.6 us (9%)
  between operations  14.2 us (5%)
  local copies, waits for them, and re-layouts  6.36 us (2%)
  starting transfers between devices  5.76 us (2%)
    psum x1, waiting for transfers between devices, local(): lax.psum(part_gate, 'dp').astype(jnp.float32)  130 us
    ppermute x6, waiting for transfers between devices, from_behind(): lax.ppermute(x, axis, [(i, (i + by) % length) for i in range(length)])  105 us
    unnamed x17, local copies, waits for them, and re-layouts  6.36 us
  transfers between devices with their start and end apart: 7, of which 3 were waited for; matrix products, arithmetic and copies ran while one was open for 8% of the time, Pallas kernels for 0%

commit v1 on v0

v1 whole, which is shorter than its diff:
```python
import jax
import jax.numpy as jnp
from jax import lax
from jax.sharding import PartitionSpec as P

F32 = jnp.float32
BF16 = jnp.bfloat16


def shift(x, by, flip=False):
    blk, dp = lax.axis_size("blk"), lax.axis_size("dp")
    pairs = []
    for i in range(blk):
        for r in range(dp):
            to = (dp - 1 - r) if flip else r
            pairs.append((i * dp + r, ((i + by) % blk) * dp + to))
    return lax.ppermute(x, ("blk", "dp"), pairs)


def dot(a, b, dims=((1,), (0,))):
    return lax.dot_general(a, b, (dims, ((), ())), preferred_element_type=F32)


def normalize(v):
    vf = v.astype(F32)
    inverse = lax.rsqrt(jnp.mean(vf * vf, axis=-1, keepdims=True) + 1e-05)
    return inverse, vf * inverse


def gates(zed, gate, up):
    pre_g = dot(zed, gate)
    pre_u = dot(zed, up)
    s = jax.nn.sigmoid(pre_g)
    q = pre_g * s
    p = pre_u * s * (1.0 + pre_g * (1.0 - s))
    return (q * pre_u).astype(BF16), p, q


def forward(v, gate, up, down):
    inverse, normed = normalize(v)
    zed = normed.astype(BF16)
    active, p, q = gates(zed, gate, up)
    out = (v.astype(F32) + dot(active, down)).astype(BF16)
    return out, (inverse, normed, zed, active, p, q)


def backward_hidden(c, saved, down):
    da = dot(c, down, ((1,), (1,)))
    return (da * saved[4]).astype(BF16), (da * saved[5]).astype(BF16)


def backward_input(c, saved, dgate, dup, gate, up):
    inverse, normed = saved[0], saved[1]
    dz = dot(dgate, gate, ((1,), (1,))) + dot(dup, up, ((1,), (1,)))
    inner = jnp.mean(dz * normed, axis=-1, keepdims=True)
    return (c.astype(F32) + inverse * (dz - normed * inner)).astype(BF16)


def second(v, c, gate, up, down):
    inverse, normed = normalize(v)
    zed = normed.astype(BF16)
    active, p, q = gates(zed, gate, up)
    saved = (inverse, normed, zed, active, p, q)
    dgate, dup = backward_hidden(c, saved, down)
    dv = backward_input(c, saved, dgate, dup, gate, up)
    return dv, (zed, active, dgate, dup, c)


def grads(terms):
    zed, active, dgate, dup, c = (jnp.concatenate(t, axis=0) for t in zip(*terms))
    tn = ((0,), (0,))
    return dot(zed, dgate, tn).astype(BF16), dot(zed, dup, tn).astype(BF16), dot(active, c, tn).astype(BF16)


def local_pair(tokens, cotangent, w_gate, w_up, w_down):
    x, g = tokens[0], cotangent[0]
    w = (w_gate[0], w_up[0], w_down[0])
    x_o = shift(x, 0, True)
    g_b = shift(g, -1)
    g_bo = shift(g, -1, True)
    h, saved = forward(x, *w)
    h_b = shift(h, -1)
    h_o, saved_o = forward(x_o, *w)
    h_bo = shift(h_o, -1)
    d_b, terms_b = second(h_b, g_b, *w)
    d = shift(d_b, 1)
    d_bo, terms_bo = second(h_bo, g_bo, *w)
    d_o = shift(d_bo, 1)
    dgate, dup = backward_hidden(d, saved, w[2])
    dx = backward_input(d, saved, dgate, dup, w[0], w[1])
    terms_a = (saved[2], saved[3], dgate, dup, d)
    dgate_o, dup_o = backward_hidden(d_o, saved_o, w[2])
    terms_ao = (saved_o[2], saved_o[3], dgate_o, dup_o, d_o)
    gg, gu, gd = grads((terms_b, terms_bo, terms_a, terms_ao))
    return dx[None], gg[None], gu[None], gd[None]


def local_many(tokens, cotangent, w_gate, w_up, w_down):
    x, g = tokens[0], cotangent[0]
    w = (w_gate[0], w_up[0], w_down[0])
    g_b = shift(g, -1)
    h, saved = forward(x, *w)
    h_b = shift(h, -1)
    d_b, terms_b = second(h_b, g_b, *w)
    d = shift(d_b, 1)
    dgate, dup = backward_hidden(d, saved, w[2])
    dx = backward_input(d, saved, dgate, dup, w[0], w[1])
    terms_a = (saved[2], saved[3], dgate, dup, d)
    gg, gu, gd = lax.psum(grads((terms_b, terms_a)), "dp")
    return dx[None], gg[None], gu[None], gd[None]


def solution(mesh):
    rows = P("blk", "dp", None)
    blocks = P("blk", None, None)
    body = local_pair if mesh.shape["dp"] == 2 else local_many
    return jax.shard_map(
        body,
        mesh=mesh,
        in_specs=(rows, rows, blocks, blocks, blocks),
        out_specs=(rows, blocks, blocks, blocks),
        check_vma=False,
    )
```

time: 291 us -> 77.4 us (0.27)
  waiting for transfers between devices: 235 us -> 15.6 us
  between operations: 14.2 us -> 0.86 us
  matrix products: 27.6 us -> 40.5 us
  starting transfers between devices: 5.76 us -> 16.7 us
  local copies, waits for them, and re-layouts: 6.36 us -> 0.06 us
    psum x1 -> x0, waiting for transfers between devices: 130 us -> none  [local(): lax.psum(part_gate, 'dp').astype(jnp.float32)]
    ppermute x6 -> x7, waiting for transfers between devices: 105 us -> 15.6 us  [shift(): return lax.ppermute(x, ('blk', 'dp'), pairs)]
    dot_general x17 -> x23, matrix products: 27.6 us -> 40.5 us  [dot(): return lax.dot_general(a, b, (dims, ((), ())), preferred_element_type=F32)]
    ppermute x6 -> x7, starting transfers between devices: 5.72 us -> 16.7 us  [shift(): return lax.ppermute(x, ('blk', 'dp'), pairs)]
    unnamed x17 -> x8, local copies, waits for them, and re-layouts: 6.36 us -> 0.06 us
  transfers between devices with their start and end apart: 7 -> 7, of which waited for: 3 -> 3; matrix products, arithmetic and copies ran while one was open for 8% -> 31% of each run, Pallas kernels for 0% -> 0%
where the time goes in v1:
time: 77.4 us; the launch traced here: 77.2 us
  matrix products  40.5 us (52%)
  starting transfers between devices  16.7 us (22%)
  waiting for transfers between devices  15.6 us (20%)
  other arithmetic  3.44 us (4%)
  between operations  0.86 us (1%)
    dot_general x23, matrix products, dot(): return lax.dot_general(a, b, (dims, ((), ())), preferred_element_type=F32)  40.5 us
    ppermute x7, starting transfers between devices, shift(): return lax.ppermute(x, ('blk', 'dp'), pairs)  16.7 us
    ppermute x7, waiting for transfers between devices, shift(): return lax.ppermute(x, ('blk', 'dp'), pairs)  15.6 us
    reduce_sum x4, other arithmetic, normalize(): inverse = lax.rsqrt(jnp.mean(vf * vf, axis=-1, keepdims=True) + 1e-05)  1.58 us
  transfers between devices with their start and end apart: 7, of which 3 were waited for; matrix products, arithmetic and copies ran while one was open for 31% of the time, Pallas kernels for 0%

profile of v1, /device:TPU:0, one launch (start us, length us, event | category | flops | bytes accessed | tf_op | source)
XLA Modules:
  0.0 77.2 jit_solution(12084076782909302170)
XLA Ops:
  0.6 0.0 copy-start
  0.6 6.4 %collective-permute-start.5 = (bf16[384,576]{0,1:T(8,128)(2,1)}, bf16[384,576]{0,1:T(8,128)(2,1)S(1)}, u32[]{:S(2)}, u32[]{:S(2)}) collective-permute-start(bf16[384,576]{0,1:T(8,128)(2,1)} %bitcast.115), channel_id=1, source_target_pairs={{0,31},{1,30},{2,1},{3,0},{4,3},{5,2},{6,5},{7,4},{8,7},{9,6},{10,... | collective-permute-start | bytes 1327112 | tf_op jit(solution)/shard_map/ppermute | solution.py:17
  7.1 0.8 %collective-permute-start = (bf16[384,576]{0,1:T(8,128)(2,1)}, bf16[384,576]{0,1:T(8,128)(2,1)S(1)}, u32[]{:S(2)}, u32[]{:S(2)}) collective-permute-start(bf16[384,576]{0,1:T(8,128)(2,1)} %bitcast.116), channel_id=1, source_target_pairs={{0,30},{1,31},{2,0},{3,1},{4,2},{5,3},{6,4},{7,5},{8,6},{9,7},{10,... | collective-permute-start | bytes 1327112 | tf_op jit(solution)/shard_map/ppermute | solution.py:17
  7.9 0.5 collective-permute-start.3
  8.5 1.2 %fusion.138 = f32[384]{0:T(512)S(1)} fusion(bf16[1,384,576]{1,2,0:T(8,128)(2,1)} %param.5), kind=kLoop, calls=%fused_computation.139 | loop fusion | flops 663168 | bytes 443904 | tf_op jit(solution)/shard_map/reduce_sum | solution.py:26
  9.6 0.0 copy-start.1
  9.6 2.8 %fusion.91 = f32[384,1536]{1,0:T(8,128)S(1)} fusion(bf16[1,576,1536]{2,1,0:T(8,128)(2,1)} %param.7, bf16[1,384,576]{1,2,0:T(8,128)(2,1)} %param.5, f32[384]{0:T(512)S(1)} %add_rsqrt_fusion.3), kind=kOutput, calls=%fused_computation.96 | convolution fusion | flops 680140800 | bytes 4572672 | tf_op jit(solution)/shard_map/dot_general | solution.py:21
  12.4 0.0 copy-done
  12.4 0.0 copy-done.1
  12.4 0.0 copy-start.3
  12.5 1.4 %multiply_convert_fusion.11 = (bf16[384,1536]{1,0:T(8,128)(2,1)S(1)}, f32[384,1536]{1,0:T(8,128)S(1)}) fusion(f32[384,1536]{1,0:T(8,128)S(1)} %fusion.91, bf16[1,576,1536]{2,1,0:T(8,128)(2,1)S(1)} %copy-done, bf16[1,384,576]{1,2,0:T(8,128)(2,1)S(1)} %copy-done.1, f32[384]{0:T(512)S(1)} %add_rsqrt_fusion.3), kind=kOutput, calls=%fused_computation.47 | convolution fusion | flops 683679744 | bytes 8111616 | tf_op jit(solution)/shard_map/dot_general | solution.py:21
  13.9 0.0 copy-done.3
  13.9 0.0 copy-start.2
  13.9 1.1 %fusion.106 = bf16[384,576]{0,1:T(8,128)(2,1)S(1)} fusion(bf16[384,1536]{1,0:T(8,128)(2,1)S(1)} %get-tuple-element.16, bf16[1,1536,576]{1,2,0:T(8,128)(2,1)S(1)} %copy-done.3, bf16[1,384,576]{1,2,0:T(8,128)(2,1)S(1)} %copy-done.1), kind=kOutput, calls=%fused_computation.107 | convolution fusion | flops 680140800 | bytes 3833856 | tf_op jit(solution)/shard_map/dot_general | solution.py:21
  15.0 0.1 collective-permute-start.1
  15.1 6.5 %collective-permute-done.3 = bf16[384,576]{0,1:T(8,128)(2,1)S(1)} collective-permute-done((bf16[384,576]{0,1:T(8,128)(2,1)}, bf16[384,576]{0,1:T(8,128)(2,1)S(1)}, u32[]{:S(2)}, u32[]{:S(2)}) %collective-permute-start.3) | collective-permute-done | bytes 442400 | tf_op jit(solution)/shard_map/ppermute | solution.py:17
  21.6 0.1 fusion.139
  21.7 0.1 fusion.140
  21.8 0.0 copy-done.2
  21.8 1.1 %fusion.83 = f32[384,1536]{1,0:T(8,128)S(1)} fusion(bf16[384,576]{0,1:T(8,128)(2,1)S(1)} %fusion.140, bf16[1,576,1536]{2,1,0:T(8,128)(2,1)S(1)} %copy-done.2), kind=kOutput, calls=%fused_computation.88 | convolution fusion | flops 679477248 | bytes 4571136 | tf_op jit(solution)/shard_map/dot_general | solution.py:21
  23.0 0.0 collective-permute-done.1
  23.0 0.1 fusion.126
  23.1 0.1 fusion.120
  23.2 1.1 %fusion.89 = f32[384,1536]{1,0:T(8,128)S(1)} fusion(bf16[384,576]{0,1:T(8,128)(2,1)S(1)} %fusion.120, bf16[1,576,1536]{2,1,0:T(8,128)(2,1)S(1)} %copy-done.2), kind=kOutput, calls=%fused_computation.94 | convolution fusion | flops 679477248 | bytes 4571136 | tf_op jit(solution)/shard_map/dot_general | solution.py:21
  24.3 0.0 collective-permute-done
  24.3 1.1 %fusion.61 = f32[384,1536]{1,0:T(8,128)S(1)} fusion(bf16[384,576]{0,1:T(8,128)(2,1)S(1)} %collective-permute-done, bf16[1,1536,576]{1,2,0:T(8,128)(2,1)S(1)} %copy-done.3), kind=kOutput, calls=%fused_computation.66 | convolution fusion | flops 679477248 | bytes 4571136 | tf_op jit(solution)/shard_map/dot_general | solution.py:21
  25.4 2.1 %multiply_convert_fusion.1 = (bf16[384,1536]{1,0:T(8,128)(2,1)S(1)}, bf16[384,1536]{1,0:T(8,128)(2,1)S(1)}, bf16[384,1536]{1,0:T(8,128)(2,1)S(1)}) fusion(f32[384,1536]{1,0:T(8,128)S(1)} %fusion.89, f32[384,1536]{1,0:T(8,128)S(1)} %fusion.61, bf16[384,576]{0,1:T(8,128)(2,1)S(1)} %fusion.120, bf16[1,576,1536]{2,1,0:T(8,128)(2,1)S(1)} %copy-done), kind=kOutput, calls=%fused_computation.31 | convolution fusion | flops 688324608 | bytes 10469376 | tf_op jit(solution)/shard_map/dot_general | solution.py:21
  27.5 1.1 %fusion.73 = f32[384,576]{0,1:T(8,128)S(1)} fusion(bf16[384,1536]{1,0:T(8,128)(2,1)S(1)} %get-tuple-element.6, bf16[1,576,1536]{2,1,0:T(8,128)(2,1)S(1)} %copy-done), kind=kOutput, calls=%fused_computation.78 | convolution fusion | flops 679477248 | bytes 3833856 | tf_op jit(solution)/shard_map/dot_general | solution.py:21
  28.6 1.1 %fusion.121 = (f32[384]{0:T(512)S(1)}, f32[384,576]{0,1:T(8,128)S(1)}) fusion(bf16[384,576]{0,1:T(8,128)(2,1)S(1)} %collective-permute-done.1, f32[384]{0:T(512)S(1)} %add_rsqrt_fusion.2, f32[384,576]{0,1:T(8,128)S(1)} %fusion.73, bf16[384,1536]{1,0:T(8,128)(2,1)S(1)} %get-tuple-element.5, bf16[1,576,1536]{2,1,0:T(8,128)(2,1)S(1)} %copy-done.2), kind=kOutput, calls=%fused_computation.122 | convolution fusion | flops 680582784 | bytes 5164032 | tf_op jit(solution)/shard_map/dot_general | solution.py:21
  29.8 0.3 fusion.125
  30.0 2.0 %collective-permute-start.2 = (bf16[384,576]{0,1:T(8,128)(2,1)S(1)}, bf16[384,576]{0,1:T(8,128)(2,1)S(1)}, u32[]{:S(2)}, u32[]{:S(2)}) collective-permute-start(bf16[384,576]{0,1:T(8,128)(2,1)S(1)} %fusion.125), channel_id=1, source_target_pairs={{0,2},{1,3},{2,4},{3,5},{4,6},{5,7},{6,8},{7,9},{8,10},{9,11},{10,... | collective-permute-start | bytes 1327112 | tf_op jit(solution)/shard_map/ppermute | solution.py:17
  32.0 1.4 %multiply_convert_fusion.6 = (bf16[384,1536]{1,0:T(8,128)(2,1)S(1)}, f32[384,1536]{1,0:T(8,128)S(1)}) fusion(f32[384,1536]{1,0:T(8,128)S(1)} %fusion.83, bf16[384,576]{0,1:T(8,128)(2,1)S(1)} %fusion.140, bf16[1,576,1536]{2,1,0:T(8,128)(2,1)S(1)} %copy-done), kind=kOutput, calls=%fused_computation.38 | convolution fusion | flops 683016192 | bytes 8110080 | tf_op jit(solution)/shard_map/dot_general | solution.py:21
  33.4 1.1 %fusion.109 = bf16[384,576]{0,1:T(8,128)(2,1)S(1)} fusion(bf16[384,1536]{1,0:T(8,128)(2,1)S(1)} %get-tuple-element.22, bf16[1,1536,576]{1,2,0:T(8,128)(2,1)S(1)} %copy-done.3, bf16[384,576]{0,1:T(8,128)(2,1)S(1)} %collective-permute-done.3), kind=kOutput, calls=%fused_computation.108 | convolution fusion | flops 680140800 | bytes 3833856 | tf_op jit(solution)/shard_map/dot_general | solution.py:21
  34.5 5.3 %collective-permute-start.4 = (bf16[384,576]{0,1:T(8,128)(2,1)S(1)}, bf16[384,576]{0,1:T(8,128)(2,1)S(1)}, u32[]{:S(2)}, u32[]{:S(2)}) collective-permute-start(bf16[384,576]{0,1:T(8,128)(2,1)S(1)} %fusion.109), channel_id=1, source_target_pairs={{0,30},{1,31},{2,0},{3,1},{4,2},{5,3},{6,4},{7,5},{8,6},{9,7},{10,... | collective-permute-start | bytes 1327112 | tf_op jit(solution)/shard_map/ppermute | solution.py:17
  39.8 0.0 collective-permute-done.5
  39.8 1.1 %fusion.55 = f32[384,1536]{1,0:T(8,128)S(1)} fusion(bf16[384,576]{0,1:T(8,128)(2,1)S(1)} %collective-permute-done.5, bf16[1,1536,576]{1,2,0:T(8,128)(2,1)S(1)} %copy-done.3), kind=kOutput, calls=%fused_computation.60 | convolution fusion | flops 679477248 | bytes 4571136 | tf_op jit(solution)/shard_map/dot_general | solution.py:21
  40.9 2.2 %collective-permute-done.2 = bf16[384,576]{0,1:T(8,128)(2,1)S(1)} collective-permute-done((bf16[384,576]{0,1:T(8,128)(2,1)S(1)}, bf16[384,576]{0,1:T(8,128)(2,1)S(1)}, u32[]{:S(2)}, u32[]{:S(2)}) %collective-permute-start.2) | collective-permute-done | bytes 442400 | tf_op jit(solution)/shard_map/ppermute | solution.py:17
  43.1 2.0 %multiply_convert_fusion.8 = (bf16[384,1536]{1,0:T(8,128)(2,1)S(1)}, bf16[384,1536]{1,0:T(8,128)(2,1)S(1)}) fusion(f32[384,1536]{1,0:T(8,128)S(1)} %fusion.91, f32[384,1536]{1,0:T(8,128)S(1)} %get-tuple-element.17, bf16[384,576]{0,1:T(8,128)(2,1)S(1)} %collective-permute-done.2, bf16[1,1536,576]{1,2,0:T(8,128)(2,1)S(1)} %copy-done.3), kind=kOutput, calls=%fused_computation.42 | convolution fusion | flops 687144960 | bytes 9289728 | tf_op jit(solution)/shard_map/dot_general | solution.py:21
  45.1 1.1 %fusion.71 = f32[384,576]{0,1:T(8,128)S(1)} fusion(bf16[384,1536]{1,0:T(8,128)(2,1)S(1)} %get-tuple-element.13, bf16[1,576,1536]{2,1,0:T(8,128)(2,1)S(1)} %copy-done), kind=kOutput, calls=%fused_computation.76 | convolution fusion | flops 679477248 | bytes 3833856 | tf_op jit(solution)/shard_map/dot_general | solution.py:21
  46.2 0.0 collective-permute-done.4
  46.2 0.1 fusion.132
  46.4 0.1 fusion.117
  46.5 1.1 %fusion.81 = f32[384,1536]{1,0:T(8,128)S(1)} fusion(bf16[384,576]{0,1:T(8,128)(2,1)S(1)} %fusion.117, bf16[1,576,1536]{2,1,0:T(8,128)(2,1)S(1)} %copy-done.2), kind=kOutput, calls=%fused_computation.86 | convolution fusion | flops 679477248 | bytes 4571136 | tf_op jit(solution)/shard_map/dot_general | solution.py:21
  47.6 2.1 %multiply_convert_fusion = (bf16[384,1536]{1,0:T(8,128)(2,1)S(1)}, bf16[384,1536]{1,0:T(8,128)(2,1)S(1)}, bf16[384,1536]{1,0:T(8,128)(2,1)S(1)}) fusion(f32[384,1536]{1,0:T(8,128)S(1)} %fusion.81, f32[384,1536]{1,0:T(8,128)S(1)} %fusion.55, bf16[384,576]{0,1:T(8,128)(2,1)S(1)} %fusion.117, bf16[1,576,1536]{2,1,0:T(8,128)(2,1)S(1)} %copy-done), kind=kOutput, calls=%fused_computation.30 | convolution fusion | flops 688324608 | bytes 10469376 | tf_op jit(solution)/shard_map/dot_general | solution.py:21
  49.7 1.1 %fusion.65 = f32[384,576]{0,1:T(8,128)S(1)} fusion(bf16[384,1536]{1,0:T(8,128)(2,1)S(1)} %get-tuple-element.9, bf16[1,576,1536]{2,1,0:T(8,128)(2,1)S(1)} %copy-done), kind=kOutput, calls=%fused_computation.70 | convolution fusion | flops 679477248 | bytes 3833856 | tf_op jit(solution)/shard_map/dot_general | solution.py:21
  50.8 1.1 %fusion.127 = (f32[384]{0:T(512)S(1)}, f32[384,576]{0,1:T(8,128)S(1)}) fusion(bf16[384,576]{0,1:T(8,128)(2,1)S(1)} %collective-permute-done.4, f32[384]{0:T(512)S(1)} %add_rsqrt_fusion, f32[384,576]{0,1:T(8,128)S(1)} %fusion.65, bf16[384,1536]{1,0:T(8,128)(2,1)S(1)} %get-tuple-element.8, bf16[1,576,1536]{2,1,0:T(8,128)(2,1)S(1)} %copy-done.2), kind=kOutput, calls=%fused_computation.128 | convolution fusion | flops 680582784 | bytes 5164032 | tf_op jit(solution)/shard_map/dot_general | solution.py:21
  51.9 0.3 fusion.131
  52.2 1.6 %collective-permute-start.6 = (bf16[384,576]{0,1:T(8,128)(2,1)S(1)}, bf16[384,576]{0,1:T(8,128)(2,1)S(1)}, u32[]{:S(2)}, u32[]{:S(2)}) collective-permute-start(bf16[384,576]{0,1:T(8,128)(2,1)S(1)} %fusion.131), channel_id=1, source_target_pairs={{0,2},{1,3},{2,4},{3,5},{4,6},{5,7},{6,8},{7,9},{8,10},{9,11},{10,... | collective-permute-start | bytes 1327112 | tf_op jit(solution)/shard_map/ppermute | solution.py:17
  53.8 1.1 %fusion.133 = (f32[384]{0:T(512)S(1)}, f32[384,576]{0,1:T(8,128)S(1)}) fusion(f32[384]{0:T(512)S(1)} %add_rsqrt_fusion.3, bf16[1,384,576]{1,2,0:T(8,128)(2,1)S(1)} %copy-done.1, f32[384,576]{0,1:T(8,128)S(1)} %fusion.71, bf16[384,1536]{1,0:T(8,128)(2,1)S(1)} %get-tuple-element.12, bf16[1,576,1536]{2,1,0:T(8,128)(2,1)S(1)} %copy-done.2), kind=kOutput, calls=%fused_computation.134 | convolution fusion | flops 680582784 | bytes 5164032 | tf_op jit(solution)/shard_map/dot_general | solution.py:21
  54.9 1.0 %fusion.112 = (bf16[384,576]{0,1:T(8,128)(2,1)S(1)}, bf16[1,384,576]{1,2,0:T(8,128)(2,1)}) fusion(f32[384]{0:T(512)S(1)} %add_rsqrt_fusion.3, bf16[1,384,576]{1,2,0:T(8,128)(2,1)S(1)} %copy-done.1, f32[384,576]{0,1:T(8,128)S(1)} %get-tuple-element.21, f32[384]{0:T(512)S(1)} %broadcast_multiply_fusion.1, bf16[384,576]{0,1:T(8,128)(2,1)S(1)} %collective-permute-done.2), kind=kLoop, calls=%fused_computation.109 | loop fusion | flops 1990656 | bytes 2657280 | tf_op jit(solution)/shard_map/convert_element_type | solution.py:41
  56.0 6.9 %collective-permute-done.6 = bf16[384,576]{0,1:T(8,128)(2,1)S(1)} collective-permute-done((bf16[384,576]{0,1:T(8,128)(2,1)S(1)}, bf16[384,576]{0,1:T(8,128)(2,1)S(1)}, u32[]{:S(2)}, u32[]{:S(2)}) %collective-permute-start.6) | collective-permute-done | bytes 442400 | tf_op jit(solution)/shard_map/ppermute | solution.py:17
  62.9 2.0 %multiply_convert_fusion.2 = (bf16[384,1536]{1,0:T(8,128)(2,1)S(1)}, bf16[384,1536]{1,0:T(8,128)(2,1)S(1)}) fusion(f32[384,1536]{1,0:T(8,128)S(1)} %fusion.83, f32[384,1536]{1,0:T(8,128)S(1)} %get-tuple-element.23, bf16[384,576]{0,1:T(8,128)(2,1)S(1)} %collective-permute-done.6, bf16[1,1536,576]{1,2,0:T(8,128)(2,1)S(1)} %copy-done.3), kind=kOutput, calls=%fused_computation.32 | convolution fusion | flops 687144960 | bytes 9289728 | tf_op jit(solution)/shard_map/dot_general | solution.py:21
  64.8 4.1 %fusion.33 = bf16[1,576,1536]{2,1,0:T(8,128)(2,1)} fusion(bf16[384,1536]{1,0:T(8,128)(2,1)S(1)} %get-tuple-element.11, bf16[384,1536]{1,0:T(8,128)(2,1)S(1)} %get-tuple-element.12, bf16[384,1536]{1,0:T(8,128)(2,1)S(1)} %get-tuple-element.8, bf16[384,1536]{1,0:T(8,128)(2,1)S(1)} %get-tuple-element.5, bf16[384,576]{0,1:T(8,128)(2,1)S(1)} %fusion.140, ...), kind=kOutput, calls=%fused_computation.27 | convolution fusion | flops 2744745984 | bytes 8257536 | tf_op jit(solution)/shard_map/dot_general | solution.py:21
  69.0 4.1 %fusion.36 = bf16[1,576,1536]{2,1,0:T(8,128)(2,1)} fusion(bf16[384,1536]{1,0:T(8,128)(2,1)S(1)} %get-tuple-element.10, bf16[384,1536]{1,0:T(8,128)(2,1)S(1)} %get-tuple-element.13, bf16[384,1536]{1,0:T(8,128)(2,1)S(1)} %get-tuple-element.9, bf16[384,1536]{1,0:T(8,128)(2,1)S(1)} %get-tuple-element.6, bf16[384,576]{0,1:T(8,128)(2,1)S(1)} %fusion.140, ...), kind=kOutput, calls=%fused_computation.28 | convolution fusion | flops 2744745984 | bytes 8257536 | tf_op jit(solution)/shard_map/dot_general | solution.py:21
  73.1 4.1 %fusion.39 = bf16[1,1536,576]{1,2,0:T(8,128)(2,1)} fusion(bf16[384,1536]{1,0:T(8,128)(2,1)S(1)} %get-tuple-element.22, bf16[384,1536]{1,0:T(8,128)(2,1)S(1)} %get-tuple-element.16, bf16[384,1536]{1,0:T(8,128)(2,1)S(1)} %get-tuple-element.7, bf16[384,1536]{1,0:T(8,128)(2,1)S(1)} %get-tuple-element.4, bf16[384,576]{0,1:T(8,128)(2,1)S(1)} %collective-permute-done.6, ...), kind=kOutput, calls=%fused_computation.29 | convolution fusion | flops 2744745984 | bytes 8257536 | tf_op jit(solution)/shard_map/dot_general | solution.py:21
  (7 shorter events, 0.0 us)
Async XLA Ops:
  0.6 11.8 %copy-start = (bf16[1,576,1536]{2,1,0:T(8,128)(2,1)S(1)}, bf16[1,576,1536]{2,1,0:T(8,128)(2,1)}, u32[]{:S(2)}) copy-start(bf16[1,576,1536]{2,1,0:T(8,128)(2,1)} %param.8) | copy-start | bytes 5308420
  0.6 39.2 %collective-permute-start.5 = (bf16[384,576]{0,1:T(8,128)(2,1)}, bf16[384,576]{0,1:T(8,128)(2,1)S(1)}, u32[]{:S(2)}, u32[]{:S(2)}) collective-permute-start(bf16[384,576]{0,1:T(8,128)(2,1)} %bitcast.115), channel_id=1, source_target_pairs={{0,31},{1,30},{2,1},{3,0},{4,3},{5,2},{6,5},{7,4},{8,7},{9,6},{10,... | collective-permute-start | bytes 1327112 | tf_op jit(solution)/shard_map/ppermute | solution.py:17
  7.1 17.2 %collective-permute-start = (bf16[384,576]{0,1:T(8,128)(2,1)}, bf16[384,576]{0,1:T(8,128)(2,1)S(1)}, u32[]{:S(2)}, u32[]{:S(2)}) collective-permute-start(bf16[384,576]{0,1:T(8,128)(2,1)} %bitcast.116), channel_id=1, source_target_pairs={{0,30},{1,31},{2,0},{3,1},{4,2},{5,3},{6,4},{7,5},{8,6},{9,7},{10,... | collective-permute-start | bytes 1327112 | tf_op jit(solution)/shard_map/ppermute | solution.py:17
  7.9 13.7 %collective-permute-start.3 = (bf16[384,576]{0,1:T(8,128)(2,1)}, bf16[384,576]{0,1:T(8,128)(2,1)S(1)}, u32[]{:S(2)}, u32[]{:S(2)}) collective-permute-start(bf16[384,576]{0,1:T(8,128)(2,1)} %bitcast.114), channel_id=1, source_target_pairs={{0,1},{1,0},{2,3},{3,2},{4,5},{5,4},{6,7},{7,6},{8,9},{9,8},{10,11... | collective-permute-start | bytes 1327112 | tf_op jit(solution)/shard_map/ppermute | solution.py:17
  9.6 2.8 %copy-start.1 = (bf16[1,384,576]{1,2,0:T(8,128)(2,1)S(1)}, bf16[1,384,576]{1,2,0:T(8,128)(2,1)}, u32[]{:S(2)}) copy-start(bf16[1,384,576]{1,2,0:T(8,128)(2,1)} %param.5) | copy-start | bytes 1327108
  12.4 1.5 %copy-start.3 = (bf16[1,1536,576]{1,2,0:T(8,128)(2,1)S(1)}, bf16[1,1536,576]{1,2,0:T(8,128)(2,1)}, u32[]{:S(2)}) copy-start(bf16[1,1536,576]{1,2,0:T(8,128)(2,1)} %param.9) | copy-start | bytes 5308420
  13.9 7.9 %copy-start.2 = (bf16[1,576,1536]{2,1,0:T(8,128)(2,1)S(1)}, bf16[1,576,1536]{2,1,0:T(8,128)(2,1)}, u32[]{:S(2)}) copy-start(bf16[1,576,1536]{2,1,0:T(8,128)(2,1)} %param.7) | copy-start | bytes 5308420
  15.0 7.9 %collective-permute-start.1 = (bf16[384,576]{0,1:T(8,128)(2,1)S(1)}, bf16[384,576]{0,1:T(8,128)(2,1)S(1)}, u32[]{:S(2)}, u32[]{:S(2)}) collective-permute-start(bf16[384,576]{0,1:T(8,128)(2,1)S(1)} %fusion.106), channel_id=1, source_target_pairs={{0,30},{1,31},{2,0},{3,1},{4,2},{5,3},{6,4},{7,5},{8,6},{9,7},{10,... | collective-permute-start | bytes 1327112 | tf_op jit(solution)/shard_map/ppermute | solution.py:17
  30.0 13.1 %collective-permute-start.2 = (bf16[384,576]{0,1:T(8,128)(2,1)S(1)}, bf16[384,576]{0,1:T(8,128)(2,1)S(1)}, u32[]{:S(2)}, u32[]{:S(2)}) collective-permute-start(bf16[384,576]{0,1:T(8,128)(2,1)S(1)} %fusion.125), channel_id=1, source_target_pairs={{0,2},{1,3},{2,4},{3,5},{4,6},{5,7},{6,8},{7,9},{8,10},{9,11},{10,... | collective-permute-start | bytes 1327112 | tf_op jit(solution)/shard_map/ppermute | solution.py:17
  34.5 11.7 %collective-permute-start.4 = (bf16[384,576]{0,1:T(8,128)(2,1)S(1)}, bf16[384,576]{0,1:T(8,128)(2,1)S(1)}, u32[]{:S(2)}, u32[]{:S(2)}) collective-permute-start(bf16[384,576]{0,1:T(8,128)(2,1)S(1)} %fusion.109), channel_id=1, source_target_pairs={{0,30},{1,31},{2,0},{3,1},{4,2},{5,3},{6,4},{7,5},{8,6},{9,7},{10,... | collective-permute-start | bytes 1327112 | tf_op jit(solution)/shard_map/ppermute | solution.py:17
  52.2 10.7 %collective-permute-start.6 = (bf16[384,576]{0,1:T(8,128)(2,1)S(1)}, bf16[384,576]{0,1:T(8,128)(2,1)S(1)}, u32[]{:S(2)}, u32[]{:S(2)}) collective-permute-start(bf16[384,576]{0,1:T(8,128)(2,1)S(1)} %fusion.131), channel_id=1, source_target_pairs={{0,2},{1,3},{2,4},{3,5},{4,6},{5,7},{6,8},{7,9},{8,10},{9,11},{10,... | collective-permute-start | bytes 1327112 | tf_op jit(solution)/shard_map/ppermute | solution.py:17

commit v2 on v1

v2 whole, which is shorter than its diff:
```python
import functools

import jax
import jax.numpy as jnp
from jax import lax
from jax.experimental import pallas as pl
from jax.experimental.pallas import tpu as pltpu
from jax.sharding import PartitionSpec as P

F32 = jnp.float32
BF16 = jnp.bfloat16
EPS = 1e-05


def shift(x, by, flip=False):
    blk, dp = lax.axis_size("blk"), lax.axis_size("dp")
    pairs = []
    for i in range(blk):
        for r in range(dp):
            to = (dp - 1 - r) if flip else r
            pairs.append((i * dp + r, ((i + by) % blk) * dp + to))
    return lax.ppermute(x, ("blk", "dp"), pairs)


def dot(a, b, dims=((1,), (0,))):
    return lax.dot_general(a, b, (dims, ((), ())), preferred_element_type=F32)


def after(x, y):
    return lax.optimization_barrier((x, y))[0]


def normalize(v):
    inverse = lax.rsqrt(jnp.mean(v * v, axis=0, keepdims=True) + EPS)
    return inverse, v * inverse


def chunks(size):
    step = 512 if size % 512 == 0 else (256 if size % 256 == 0 else size)
    return [slice(k, k + step) for k in range(0, size, step)]


def gate_values(pre_g, pre_u):
    s = 0.5 * jnp.tanh(0.5 * pre_g) + 0.5
    q = pre_g * s
    p = pre_u * (s + q * (1.0 - s))
    return q * pre_u, p, q


def input_cotangent(c, dz, inverse, normed):
    inner = jnp.mean(dz * normed, axis=0, keepdims=True)
    return (c + inverse * (dz - normed * inner)).astype(BF16)


def forward_kernel(x_ref, gate_ref, up_ref, down_ref, h_ref, z_ref, act_ref, p_ref, q_ref):
    x = x_ref[...].astype(F32)
    _, normed = normalize(x)
    zed = normed.astype(BF16)
    z_ref[...] = zed
    zt = zed.T
    total = x
    for hc in chunks(gate_ref.shape[1]):
        pre_g = dot(zt, gate_ref[:, hc])
        pre_u = dot(zt, up_ref[:, hc])
        active, p, q = gate_values(pre_g, pre_u)
        active = active.astype(BF16)
        act_ref[:, hc] = active
        p_ref[:, hc] = p.astype(BF16)
        q_ref[:, hc] = q.astype(BF16)
        total += dot(down_ref[:, hc], active, ((1,), (1,)))
    h_ref[...] = total.astype(BF16)


def second_kernel(h_ref, c_ref, gate_ref, up_ref, down_ref, d_ref, z_ref, act_ref, dg_ref, du_ref):
    inverse, normed = normalize(h_ref[...].astype(F32))
    zed = normed.astype(BF16)
    z_ref[...] = zed
    zt = zed.T
    ct = c_ref[...].T
    dz = jnp.zeros(c_ref.shape, F32)
    for hc in chunks(gate_ref.shape[1]):
        pre_g = dot(zt, gate_ref[:, hc])
        pre_u = dot(zt, up_ref[:, hc])
        da = dot(ct, down_ref[:, hc])
        active, p, q = gate_values(pre_g, pre_u)
        act_ref[:, hc] = active.astype(BF16)
        dgate = (da * p).astype(BF16)
        dup = (da * q).astype(BF16)
        dg_ref[:, hc] = dgate
        du_ref[:, hc] = dup
        dz += dot(gate_ref[:, hc], dgate, ((1,), (1,)))
        dz += dot(up_ref[:, hc], dup, ((1,), (1,)))
    d_ref[...] = input_cotangent(c_ref[...].astype(F32), dz, inverse, normed)


def first_back_kernel(x_ref, c_ref, p_ref, q_ref, gate_ref, up_ref, down_ref, d_ref, dg_ref, du_ref):
    inverse, normed = normalize(x_ref[...].astype(F32))
    ct = c_ref[...].T
    dz = jnp.zeros(c_ref.shape, F32)
    for hc in chunks(gate_ref.shape[1]):
        da = dot(ct, down_ref[:, hc])
        dgate = (da * p_ref[:, hc].astype(F32)).astype(BF16)
        dup = (da * q_ref[:, hc].astype(F32)).astype(BF16)
        dg_ref[:, hc] = dgate
        du_ref[:, hc] = dup
        dz += dot(gate_ref[:, hc], dgate, ((1,), (1,)))
        dz += dot(up_ref[:, hc], dup, ((1,), (1,)))
    d_ref[...] = input_cotangent(c_ref[...].astype(F32), dz, inverse, normed)


def grads_kernel(
    p_ref, q_ref, down_ref,
    z0, z1, z2, z3, c0, c1, c2, c3, act0, act1, act2, act3, dg0, dg1, dg2, du0, du1, du2,
    gg_ref, gu_ref, gd_ref,
):
    da = dot(c3[...].T, down_ref[...])
    dg3 = (da * p_ref[...].astype(F32)).astype(BF16)
    du3 = (da * q_ref[...].astype(F32)).astype(BF16)
    z = jnp.concatenate([z0[...], z1[...], z2[...], z3[...]], axis=1)
    dg = jnp.concatenate([dg0[...], dg1[...], dg2[...], dg3], axis=0)
    du = jnp.concatenate([du0[...], du1[...], du2[...], du3], axis=0)
    c = jnp.concatenate([c0[...], c1[...], c2[...], c3[...]], axis=1)
    act = jnp.concatenate([act0[...], act1[...], act2[...], act3[...]], axis=0)
    gd_ref[...] = dot(c, act).astype(BF16)
    gg_ref[...] = dot(z, dg).astype(BF16)
    gu_ref[...] = dot(z, du).astype(BF16)


PARAMS = pltpu.CompilerParams(vmem_limit_bytes=20 * 1024 * 1024)


def in_vmem(x):
    return pltpu.with_memory_space_constraint(x, pltpu.VMEM)


def whole(kernel, args, out_shapes, name):
    spec = pl.BlockSpec(memory_space=pltpu.VMEM)
    return pl.pallas_call(
        kernel,
        in_specs=[spec] * len(args),
        out_specs=[spec] * len(out_shapes),
        out_shape=[pltpu.VMEM(s, BF16) for s in out_shapes],
        compiler_params=PARAMS,
        name=name,
    )(*(in_vmem(a) for a in args))


def first(x, w, name):
    d, t = x.shape
    h = w[0].shape[1]
    return whole(forward_kernel, (x, *w), [(d, t), (d, t), (t, h), (t, h), (t, h)], name)


def second(v, c, w, name):
    d, t = v.shape
    h = w[0].shape[1]
    return whole(second_kernel, (v, c, *w), [(d, t), (d, t), (t, h), (t, h), (t, h)], name)


def first_back(x, c, p, q, w, name):
    d, t = x.shape
    h = w[0].shape[1]
    return whole(first_back_kernel, (x, c, p, q, *w), [(d, t), (t, h), (t, h)], name)


def grads(p, q, down, zs, cs, acts, dgs, dus):
    d, t = zs[0].shape
    h = down.shape[1]
    step = 512
    full = pl.BlockSpec(memory_space=pltpu.VMEM)
    tile = pl.BlockSpec((t, step), lambda k: (0, k))
    wide = pl.BlockSpec((d, step), lambda k: (0, k))
    return pl.pallas_call(
        grads_kernel,
        grid=(h // step,),
        in_specs=[tile, tile, wide] + [full] * 8 + [tile] * 10,
        out_specs=[wide] * 3,
        out_shape=[jax.ShapeDtypeStruct((d, h), BF16)] * 3,
        compiler_params=PARAMS,
        name="grads",
    )(p, q, down, *(in_vmem(a) for a in (*zs, *cs)), *acts, *dgs, *dus)


def local_pair(tokens, cotangent, w_gate, w_up, w_down):
    x, g = tokens[0].T, cotangent[0].T
    w = (w_gate[0], w_up[0], w_down[0].T)
    x_o = shift(x, 0, True)
    g_b = shift(g, -1)
    h, z2, act2, p2, q2 = first(x, w, "first_own")
    h_b = shift(h, -1)
    g_bo = shift(after(g_b, x_o), 0, True)
    d_b, z0, act0, dg0, du0 = second(h_b, g_b, w, "second_own")
    d = shift(d_b, 1)
    h_o, z3, act3, p3, q3 = first(x_o, w, "first_other")
    h_bo = shift(h_o, -1)
    dx, dg2, du2 = first_back(x, d, p2, q2, w, "first_back_own")
    d_bo, z1, act1, dg1, du1 = second(h_bo, g_bo, w, "second_other")
    d_o = shift(d_bo, 1)
    gg, gu, gd = grads(
        p3, q3, w[2], (z0, z1, z2, z3), (g_b, g_bo, d, d_o), (act0, act1, act2, act3), (dg0, dg1, dg2), (du0, du1, du2)
    )
    return dx.T[None], gg[None], gu[None], gd.T[None]


def many_gates(v, gate, up):
    vf = v.astype(F32)
    inverse = lax.rsqrt(jnp.mean(vf * vf, axis=-1, keepdims=True) + EPS)
    normed = vf * inverse
    zed = normed.astype(BF16)
    active, p, q = gate_values(dot(zed, gate), dot(zed, up))
    return inverse, normed, zed, active.astype(BF16), p, q


def many_back(c, saved, gate, up, down):
    inverse, normed, _, _, p, q = saved
    da = dot(c, down, ((1,), (1,)))
    dgate, dup = (da * p).astype(BF16), (da * q).astype(BF16)
    dz = dot(dgate, gate, ((1,), (1,))) + dot(dup, up, ((1,), (1,)))
    inner = jnp.mean(dz * normed, axis=-1, keepdims=True)
    return (c.astype(F32) + inverse * (dz - normed * inner)).astype(BF16), dgate, dup


def local_many(tokens, cotangent, w_gate, w_up, w_down):
    x, g = tokens[0], cotangent[0]
    gate, up, down = w_gate[0], w_up[0], w_down[0]
    g_b = shift(g, -1)
    saved = many_gates(x, gate, up)
    h = (x.astype(F32) + dot(saved[3], down)).astype(BF16)
    saved_b = many_gates(shift(h, -1), gate, up)
    d_b, dg_b, du_b = many_back(g_b, saved_b, gate, up, down)
    d = shift(d_b, 1)
    dx, dg, du = many_back(d, saved, gate, up, down)
    tn = ((0,), (0,))
    zed = jnp.concatenate([saved_b[2], saved[2]])
    parts = (
        dot(zed, jnp.concatenate([dg_b, dg]), tn),
        dot(zed, jnp.concatenate([du_b, du]), tn),
        dot(jnp.concatenate([saved_b[3], saved[3]]), jnp.concatenate([g_b, d]), tn),
    )
    gg, gu, gd = lax.psum(tuple(a.astype(BF16) for a in parts), "dp")
    return dx[None], gg[None], gu[None], gd[None]


def solution(mesh):
    rows = P("blk", "dp", None)
    blocks = P("blk", None, None)
    body = local_pair if mesh.shape["dp"] == 2 else local_many
    return jax.shard_map(
        body,
        mesh=mesh,
        in_specs=(rows, rows, blocks, blocks, blocks),
        out_specs=(rows, blocks, blocks, blocks),
        check_vma=False,
    )
```

time: 77.4 us -> 61.8 us (0.80)
  matrix products: 40.5 us -> 0 us
  Pallas kernels: 0 us -> 34 us
  starting transfers between devices: 16.7 us -> 9.72 us
  local copies, waits for them, and re-layouts: 0.06 us -> 6.21 us
  waiting for transfers between devices: 15.6 us -> 11 us
  other arithmetic: 3.44 us -> 0 us
    dot_general x23 -> x0, matrix products: 40.5 us -> none  [dot(): return lax.dot_general(a, b, (dims, ((), ())), preferred_element_type=F32)]
    pallas_call x0 -> x6, Pallas kernels: none -> 34 us  [the longest x5 21.9 us: whole(): pl.pallas_call(kernel, in_specs=[spec] * len(args), out_specs=[spec] * le...]
    ppermute x7, starting transfers between devices: 16.7 us -> 9.72 us  [shift(): return lax.ppermute(x, ('blk', 'dp'), pairs)]
    unnamed x8 -> x13, local copies, waits for them, and re-layouts: 0.06 us -> 6.21 us
    ppermute x7, waiting for transfers between devices: 15.6 us -> 11 us  [shift(): return lax.ppermute(x, ('blk', 'dp'), pairs)]
    convert_element_type x6 -> x0, other arithmetic: 1.82 us -> none  [the longest x2 1.13 us: forward(): zed = normed.astype(BF16)]
    reduce_sum x4 -> x0, other arithmetic: 1.58 us -> none  [normalize(): inverse = lax.rsqrt(jnp.mean(vf * vf, axis=-1, keepdims=True) + 1e-05)]
  transfers between devices with their start and end apart: 7 -> 7, of which waited for: 3 -> 4; matrix products, arithmetic and copies ran while one was open for 31% -> 1% of each run, Pallas kernels for 0% -> 36%
where the time goes in v2:
time: 61.8 us; the launch traced here: 61.6 us
  Pallas kernels  34 us (55%)
  waiting for transfers between devices  11 us (18%)
  starting transfers between devices  9.72 us (16%)
  local copies, waits for them, and re-layouts  6.21 us (10%)
  between operations  0.7 us (1%)
    pallas_call x5, Pallas kernels, whole(): pl.pallas_call(kernel, in_specs=[spec] * len(args), out_specs=[spec] * le...  21.9 us
    pallas_call x1, Pallas kernels, grads(): pl.pallas_call(grads_kernel, grid=(h // step,), in_specs=[tile, tile, wid...  12.1 us
    ppermute x7, waiting for transfers between devices, shift(): return lax.ppermute(x, ('blk', 'dp'), pairs)  11 us
    ppermute x7, starting transfers between devices, shift(): return lax.ppermute(x, ('blk', 'dp'), pairs)  9.72 us
    unnamed x13, local copies, waits for them, and re-layouts  6.21 us
  transfers between devices with their start and end apart: 7, of which 4 were waited for; matrix products, arithmetic and copies ran while one was open for 1% of the time, Pallas kernels for 36%

profile of v2, /device:TPU:0, one launch (start us, length us, event | category | flops | bytes accessed | tf_op | source)
XLA Modules:
  0.0 61.6 jit_solution(8246798145063325556)
XLA Ops:
  0.6 3.0 %collective-permute-start.3 = (bf16[576,384]{1,0:T(8,128)(2,1)}, bf16[576,384]{1,0:T(8,128)(2,1)S(1)}, u32[]{:S(2)}, u32[]{:S(2)}) collective-permute-start(bf16[576,384]{1,0:T(8,128)(2,1)} %bitcast.36), channel_id=1, source_target_pairs={{0,1},{1,0},{2,3},{3,2},{4,5},{5,4},{6,7},{7,6},{8,9},{9,8},{10,11... | collective-permute-start | bytes 1327112 | tf_op jit(solution)/shard_map/ppermute | solution.py:22
  3.6 3.7 %collective-permute-start.1 = (bf16[576,384]{1,0:T(8,128)(2,1)}, bf16[576,384]{1,0:T(8,128)(2,1)S(1)}, u32[]{:S(2)}, u32[]{:S(2)}) collective-permute-start(bf16[576,384]{1,0:T(8,128)(2,1)} %bitcast.42), channel_id=1, source_target_pairs={{0,30},{1,31},{2,0},{3,1},{4,2},{5,3},{6,4},{7,5},{8,6},{9,7},{10,... | collective-permute-start | bytes 1327112 | tf_op jit(solution)/shard_map/ppermute | solution.py:22
  7.4 0.0 copy-start
  7.4 1.5 %copy-done = bf16[1,1536,576]{1,2,0:T(8,128)(2,1)S(1)} copy-done((bf16[1,1536,576]{1,2,0:T(8,128)(2,1)S(1)}, bf16[1,1536,576]{1,2,0:T(8,128)(2,1)}, u32[]{:S(2)}) %copy-start) | copy-done | bytes 1769496
  8.8 0.0 copy-start.2
  8.8 1.5 %copy-done.2 = bf16[1,576,1536]{2,1,0:T(8,128)(2,1)S(1)} copy-done((bf16[1,576,1536]{2,1,0:T(8,128)(2,1)S(1)}, bf16[1,576,1536]{2,1,0:T(8,128)(2,1)}, u32[]{:S(2)}) %copy-start.2) | copy-done | bytes 1769496
  10.3 0.0 copy-start.4
  10.3 1.5 %copy-done.4 = bf16[1,576,1536]{2,1,0:T(8,128)(2,1)S(1)} copy-done((bf16[1,576,1536]{2,1,0:T(8,128)(2,1)S(1)}, bf16[1,576,1536]{2,1,0:T(8,128)(2,1)}, u32[]{:S(2)}) %copy-start.4) | copy-done | bytes 1769496
  11.8 0.0 copy-start.5
  11.8 1.0 %copy-done.5 = bf16[1,384,576]{1,2,0:T(8,128)(2,1)S(1)} copy-done((bf16[1,384,576]{1,2,0:T(8,128)(2,1)S(1)}, bf16[1,384,576]{1,2,0:T(8,128)(2,1)}, u32[]{:S(2)}) %copy-start.5) | copy-done | bytes 442392
  12.8 0.0 copy-start.1
  12.8 0.0 copy-start.3
  12.8 3.4 %first_own.1 = (bf16[576,384]{1,0:T(8,128)(2,1)S(1)}, bf16[576,384]{1,0:T(8,128)(2,1)S(1)}, bf16[384,1536]{1,0:T(8,128)(2,1)S(1)}, bf16[384,1536]{1,0:T(8,128)(2,1)S(1)}, bf16[384,1536]{1,0:T(8,128)(2,1)S(1)}) custom-call(bf16[576,384]{1,0:T(8,128)(2,1)S(1)} %bitcast.37, bf16[576,1536]{1,0:T(8,128)(2,1)S(1)} %bitcast.26, bf16[576,1536]{1,0:T(8,128)(2,1)S(1)} %bitcast.31, ...), custom_call_target="tpu_custom_call" | custom-call | tf_op jit(solution)/shard_map/first_own/pallas_call | solution.py:138
  16.2 1.0 %collective-permute-start = (bf16[576,384]{1,0:T(8,128)(2,1)S(1)}, bf16[576,384]{1,0:T(8,128)(2,1)S(1)}, u32[]{:S(2)}, u32[]{:S(2)}) collective-permute-start(bf16[576,384]{1,0:T(8,128)(2,1)S(1)} %get-tuple-element.31), channel_id=1, source_target_pairs={{0,30},{1,31},{2,0},{3,1},{4,2},{5,3},{6,4},{7,5},{8,6},{9,7},{10,... | collective-permute-start | bytes 1327112 | tf_op jit(solution)/shard_map/ppermute | solution.py:22
  17.2 0.0 collective-permute-done.3.x_ref
  17.2 0.0 copy-done.1
  17.2 0.0 copy-done.3
  17.2 3.4 %first_other.1 = (bf16[576,384]{1,0:T(8,128)(2,1)S(1)}, bf16[576,384]{1,0:T(8,128)(2,1)S(1)}, bf16[384,1536]{1,0:T(8,128)(2,1)S(1)}, bf16[384,1536]{1,0:T(8,128)(2,1)S(1)}, bf16[384,1536]{1,0:T(8,128)(2,1)S(1)}) custom-call(bf16[576,384]{1,0:T(8,128)(2,1)S(1)} %collective-permute-done.3.x_ref, bf16[576,1536]{1,0:T(8,128)(2,1)S(1)} %bitcast.27, ...), custom_call_target="tpu_custom_call" | custom-call | tf_op jit(solution)/shard_map/first_other/pallas_call | solution.py:138
  20.7 0.2 collective-permute-start.4
  20.9 0.0 collective-permute-done.1.c_ref.c0
  20.9 1.5 %collective-permute-start.5 = (bf16[576,384]{1,0:T(8,128)(2,1)S(1)}, bf16[576,384]{1,0:T(8,128)(2,1)S(1)}, u32[]{:S(2)}, u32[]{:S(2)}) collective-permute-start(bf16[576,384]{1,0:T(8,128)(2,1)S(1)} %collective-permute-done.1.c_ref.c0), channel_id=1, source_target_pairs={{0,1},{1,0},{2,3},{3,2},{4,5},{5,4},{6,7},{7,6},{8,9},{9,8},{10,11... | collective-permute-start | bytes 1327112 | tf_op jit(solution)/shard_map/ppermute | solution.py:22
  22.4 0.7 %collective-permute-done.h_ref = bf16[576,384]{1,0:T(8,128)(2,1)S(1)} collective-permute-done((bf16[576,384]{1,0:T(8,128)(2,1)S(1)}, bf16[576,384]{1,0:T(8,128)(2,1)S(1)}, u32[]{:S(2)}, u32[]{:S(2)}) %collective-permute-start) | collective-permute-done | bytes 442400 | tf_op jit(solution)/shard_map/ppermute | solution.py:22
  23.1 5.7 %second_own.1 = (bf16[576,384]{1,0:T(8,128)(2,1)S(1)}, bf16[576,384]{1,0:T(8,128)(2,1)S(1)}, bf16[384,1536]{1,0:T(8,128)(2,1)S(1)}, bf16[384,1536]{1,0:T(8,128)(2,1)S(1)}, bf16[384,1536]{1,0:T(8,128)(2,1)S(1)}) custom-call(bf16[576,384]{1,0:T(8,128)(2,1)S(1)} %collective-permute-done.h_ref, bf16[576,384]{1,0:T(8,128)(2,1)S(1)} %collective-permute-done.1.c_ref.c0, ...), custom_call_target="tpu_custom_call" | custom-call | tf_op jit(solution)/shard_map/second_own/pallas_call | solution.py:138
  28.8 0.2 collective-permute-start.2
  29.0 0.0 collective-permute-done.4.h_ref
  29.0 4.3 %collective-permute-done.5.c_ref.c1 = bf16[576,384]{1,0:T(8,128)(2,1)S(1)} collective-permute-done((bf16[576,384]{1,0:T(8,128)(2,1)S(1)}, bf16[576,384]{1,0:T(8,128)(2,1)S(1)}, u32[]{:S(2)}, u32[]{:S(2)}) %collective-permute-start.5) | collective-permute-done | bytes 442400 | tf_op jit(solution)/shard_map/ppermute | solution.py:22
  33.3 5.7 %second_other.1 = (bf16[576,384]{1,0:T(8,128)(2,1)S(1)}, bf16[576,384]{1,0:T(8,128)(2,1)S(1)}, bf16[384,1536]{1,0:T(8,128)(2,1)S(1)}, bf16[384,1536]{1,0:T(8,128)(2,1)S(1)}, bf16[384,1536]{1,0:T(8,128)(2,1)S(1)}) custom-call(bf16[576,384]{1,0:T(8,128)(2,1)S(1)} %collective-permute-done.4.h_ref, bf16[576,384]{1,0:T(8,128)(2,1)S(1)} %collective-permute-done.5.c_ref.c1, ...), custom_call_target="tpu_custom_call" | custom-call | tf_op jit(solution)/shard_map/second_other/pallas_call | solution.py:138
  39.0 0.1 collective-permute-start.6
  39.1 0.5 collective-permute-done.2.c_ref.c2
  39.6 3.6 %first_back_own.1 = (bf16[576,384]{1,0:T(8,128)(2,1)S(1)}, bf16[384,1536]{1,0:T(8,128)(2,1)S(1)}, bf16[384,1536]{1,0:T(8,128)(2,1)S(1)}) custom-call(bf16[576,384]{1,0:T(8,128)(2,1)S(1)} %bitcast.38, bf16[576,384]{1,0:T(8,128)(2,1)S(1)} %collective-permute-done.2.c_ref.c2, bf16[384,1536]{1,0:T(8,128)(2,1)S(1)} %get-tuple-element.33.p_ref, ...), custom_call_target="tpu_custom_call" | custom-call | tf_op jit(solution)/shard_map/first_back_own/pallas_call | solution.py:138
  43.2 0.8 %copy.9 = bf16[1,384,576]{1,2,0:T(8,128)(2,1)} copy(bf16[1,384,576]{1,2,0:T(8,128)(2,1)S(1)} %bitcast.19) | data formatting | bytes 884736
  44.0 5.5 %collective-permute-done.6.c3 = bf16[576,384]{1,0:T(8,128)(2,1)S(1)} collective-permute-done((bf16[576,384]{1,0:T(8,128)(2,1)S(1)}, bf16[576,384]{1,0:T(8,128)(2,1)S(1)}, u32[]{:S(2)}, u32[]{:S(2)}) %collective-permute-start.6) | collective-permute-done | bytes 442400 | tf_op jit(solution)/shard_map/ppermute | solution.py:22
  49.5 12.1 %grads.1 = (bf16[576,1536]{1,0:T(8,128)(2,1)}, bf16[576,1536]{1,0:T(8,128)(2,1)}, bf16[576,1536]{1,0:T(8,128)(2,1)}) custom-call(bf16[384,1536]{1,0:T(8,128)(2,1)S(1)} %get-tuple-element.36.p_ref, bf16[384,1536]{1,0:T(8,128)(2,1)S(1)} %get-tuple-element.37.q_ref, bf16[576,1536]{1,0:T(8,128)(2,1)S(1)} %bitcast.25, bf16[576,384]{1,0:T(8,128)(2,1)S(1)} %get-tuple-element.38.z0, ...), custom_call_target="tpu_custom_call" | custom-call | tf_op jit(solution)/shard_map/grads/pallas_call | solution.py:173
Async XLA Ops:
  0.6 16.6 %collective-permute-start.3 = (bf16[576,384]{1,0:T(8,128)(2,1)}, bf16[576,384]{1,0:T(8,128)(2,1)S(1)}, u32[]{:S(2)}, u32[]{:S(2)}) collective-permute-start(bf16[576,384]{1,0:T(8,128)(2,1)} %bitcast.36), channel_id=1, source_target_pairs={{0,1},{1,0},{2,3},{3,2},{4,5},{5,4},{6,7},{7,6},{8,9},{9,8},{10,11... | collective-permute-start | bytes 1327112 | tf_op jit(solution)/shard_map/ppermute | solution.py:22
  3.6 17.2 %collective-permute-start.1 = (bf16[576,384]{1,0:T(8,128)(2,1)}, bf16[576,384]{1,0:T(8,128)(2,1)S(1)}, u32[]{:S(2)}, u32[]{:S(2)}) collective-permute-start(bf16[576,384]{1,0:T(8,128)(2,1)} %bitcast.42), channel_id=1, source_target_pairs={{0,30},{1,31},{2,0},{3,1},{4,2},{5,3},{6,4},{7,5},{8,6},{9,7},{10,... | collective-permute-start | bytes 1327112 | tf_op jit(solution)/shard_map/ppermute | solution.py:22
  7.4 1.5 %copy-start = (bf16[1,1536,576]{1,2,0:T(8,128)(2,1)S(1)}, bf16[1,1536,576]{1,2,0:T(8,128)(2,1)}, u32[]{:S(2)}) copy-start(bf16[1,1536,576]{1,2,0:T(8,128)(2,1)} %param.9) | copy-start | bytes 5308420
  8.8 1.5 %copy-start.2 = (bf16[1,576,1536]{2,1,0:T(8,128)(2,1)S(1)}, bf16[1,576,1536]{2,1,0:T(8,128)(2,1)}, u32[]{:S(2)}) copy-start(bf16[1,576,1536]{2,1,0:T(8,128)(2,1)} %param.7) | copy-start | bytes 5308420
  10.3 1.5 %copy-start.4 = (bf16[1,576,1536]{2,1,0:T(8,128)(2,1)S(1)}, bf16[1,576,1536]{2,1,0:T(8,128)(2,1)}, u32[]{:S(2)}) copy-start(bf16[1,576,1536]{2,1,0:T(8,128)(2,1)} %param.8) | copy-start | bytes 5308420
  11.8 1.0 %copy-start.5 = (bf16[1,384,576]{1,2,0:T(8,128)(2,1)S(1)}, bf16[1,384,576]{1,2,0:T(8,128)(2,1)}, u32[]{:S(2)}) copy-start(bf16[1,384,576]{1,2,0:T(8,128)(2,1)} %param.5) | copy-start | bytes 1327108
  12.8 4.4 %copy-start.1 = (bf16[1,1536,576]{1,2,0:T(8,128)(2,1)S(1)}, bf16[1,1536,576]{1,2,0:T(8,128)(2,1)}, u32[]{:S(2)}) copy-start(bf16[1,1536,576]{1,2,0:T(8,128)(2,1)} %param.9) | copy-start | bytes 5308420
  12.8 4.4 %copy-start.3 = (bf16[1,576,1536]{2,1,0:T(8,128)(2,1)S(1)}, bf16[1,576,1536]{2,1,0:T(8,128)(2,1)}, u32[]{:S(2)}) copy-start(bf16[1,576,1536]{2,1,0:T(8,128)(2,1)} %param.7) | copy-start | bytes 5308420
  16.2 6.8 %collective-permute-start = (bf16[576,384]{1,0:T(8,128)(2,1)S(1)}, bf16[576,384]{1,0:T(8,128)(2,1)S(1)}, u32[]{:S(2)}, u32[]{:S(2)}) collective-permute-start(bf16[576,384]{1,0:T(8,128)(2,1)S(1)} %get-tuple-element.31), channel_id=1, source_target_pairs={{0,30},{1,31},{2,0},{3,1},{4,2},{5,3},{6,4},{7,5},{8,6},{9,7},{10,... | collective-permute-start | bytes 1327112 | tf_op jit(solution)/shard_map/ppermute | solution.py:22
  20.7 8.3 %collective-permute-start.4 = (bf16[576,384]{1,0:T(8,128)(2,1)S(1)}, bf16[576,384]{1,0:T(8,128)(2,1)S(1)}, u32[]{:S(2)}, u32[]{:S(2)}) collective-permute-start(bf16[576,384]{1,0:T(8,128)(2,1)S(1)} %get-tuple-element.39), channel_id=1, source_target_pairs={{0,30},{1,31},{2,0},{3,1},{4,2},{5,3},{6,4},{7,5},{8,6},{9,7},{10,... | collective-permute-start | bytes 1327112 | tf_op jit(solution)/shard_map/ppermute | solution.py:22
  20.9 12.4 %collective-permute-start.5 = (bf16[576,384]{1,0:T(8,128)(2,1)S(1)}, bf16[576,384]{1,0:T(8,128)(2,1)S(1)}, u32[]{:S(2)}, u32[]{:S(2)}) collective-permute-start(bf16[576,384]{1,0:T(8,128)(2,1)S(1)} %collective-permute-done.1.c_ref.c0), channel_id=1, source_target_pairs={{0,1},{1,0},{2,3},{3,2},{4,5},{5,4},{6,7},{7,6},{8,9},{9,8},{10,11... | collective-permute-start | bytes 1327112 | tf_op jit(solution)/shard_map/ppermute | solution.py:22
  28.8 10.8 %collective-permute-start.2 = (bf16[576,384]{1,0:T(8,128)(2,1)S(1)}, bf16[576,384]{1,0:T(8,128)(2,1)S(1)}, u32[]{:S(2)}, u32[]{:S(2)}) collective-permute-start(bf16[576,384]{1,0:T(8,128)(2,1)S(1)} %get-tuple-element.32), channel_id=1, source_target_pairs={{0,2},{1,3},{2,4},{3,5},{4,6},{5,7},{6,8},{7,9},{8,10},{9,11},{10,... | collective-permute-start | bytes 1327112 | tf_op jit(solution)/shard_map/ppermute | solution.py:22
  39.0 10.5 %collective-permute-start.6 = (bf16[576,384]{1,0:T(8,128)(2,1)S(1)}, bf16[576,384]{1,0:T(8,128)(2,1)S(1)}, u32[]{:S(2)}, u32[]{:S(2)}) collective-permute-start(bf16[576,384]{1,0:T(8,128)(2,1)S(1)} %get-tuple-element.44), channel_id=1, source_target_pairs={{0,2},{1,3},{2,4},{3,5},{4,6},{5,7},{6,8},{7,9},{8,10},{9,11},{10,... | collective-permute-start | bytes 1327112 | tf_op jit(solution)/shard_map/ppermute | solution.py:22

commit v3 on v2

--- a/solution.py
+++ b/solution.py
@@ -52,6 +52,17 @@
     return (c + inverse * (dz - normed * inner)).astype(BF16)
 
 
+def forward_chunk(hc, zt, total, gate, up, down, act_ref, p_ref, q_ref):
+    pre_g = dot(zt, gate[:, hc])
+    pre_u = dot(zt, up[:, hc])
+    active, p, q = gate_values(pre_g, pre_u)
+    active = active.astype(BF16)
+    act_ref[:, hc] = active
+    p_ref[:, hc] = p.astype(BF16)
+    q_ref[:, hc] = q.astype(BF16)
+    return total + dot(down[:, hc], active, ((1,), (1,)))
+
+
 def forward_kernel(x_ref, gate_ref, up_ref, down_ref, h_ref, z_ref, act_ref, p_ref, q_ref):
     x = x_ref[...].astype(F32)
     _, normed = normalize(x)
@@ -60,14 +71,34 @@
     zt = zed.T
     total = x
     for hc in chunks(gate_ref.shape[1]):
-        pre_g = dot(zt, gate_ref[:, hc])
-        pre_u = dot(zt, up_ref[:, hc])
-        active, p, q = gate_values(pre_g, pre_u)
-        active = active.astype(BF16)
-        act_ref[:, hc] = active
-        p_ref[:, hc] = p.astype(BF16)
-        q_ref[:, hc] = q.astype(BF16)
-        total += dot(down_ref[:, hc], active, ((1,), (1,)))
+        total = forward_chunk(hc, zt, total, gate_ref, up_ref, down_ref, act_ref, p_ref, q_ref)
+    h_ref[...] = total.astype(BF16)
+
+
+def loading_forward_kernel(
+    x_hbm, gate_hbm, up_hbm, down_hbm, h_ref, z_ref, act_ref, p_ref, q_ref, x_ref, gate_ref, up_ref, down_ref, sem
+):
+    x_copy = pltpu.make_async_copy(x_hbm, x_ref, sem.at[0])
+    x_copy.start()
+    parts = chunks(gate_ref.shape[1])
+    copies = []
+    for k, hc in enumerate(parts):
+        copies.append([])
+        for m, (src, dst) in enumerate(((gate_hbm, gate_ref), (up_hbm, up_ref), (down_hbm, down_ref))):
+            copy = pltpu.make_async_copy(src.at[:, hc], dst.at[:, hc], sem.at[1 + 3 * k + m])
+            copy.start()
+            copies[-1].append(copy)
+    x_copy.wait()
+    x = x_ref[...].astype(F32)
+    _, normed = normalize(x)
+    zed = normed.astype(BF16)
+    z_ref[...] = zed
+    zt = zed.T
+    total = x
+    for k, hc in enumerate(parts):
+        for copy in copies[k]:
+            copy.wait()
+        total = forward_chunk(hc, zt, total, gate_ref, up_ref, down_ref, act_ref, p_ref, q_ref)
     h_ref[...] = total.astype(BF16)
 
 
@@ -108,22 +139,41 @@
     d_ref[...] = input_cotangent(c_ref[...].astype(F32), dz, inverse, normed)
 
 
-def grads_kernel(
-    p_ref, q_ref, down_ref,
-    z0, z1, z2, z3, c0, c1, c2, c3, act0, act1, act2, act3, dg0, dg1, dg2, du0, du1, du2,
-    gg_ref, gu_ref, gd_ref,
+def join(refs, hc, axis):
+    return jnp.concatenate([r[:, hc] for r in refs], axis=axis)
+
+
+def partial_kernel(*refs):
+    zs, cs, acts, dgs, dus = (refs[3 * k : 3 * k + 3] for k in range(5))
+    gg_ref, gu_ref, gd_ref = refs[15:]
+    z = join(zs, slice(None), 1)
+    c = join(cs, slice(None), 1)
+    for hc in chunks(gg_ref.shape[1]):
+        gd_ref[:, hc] = dot(c, join(acts, hc, 0)).astype(BF16)
+        gg_ref[:, hc] = dot(z, join(dgs, hc, 0)).astype(BF16)
+        gu_ref[:, hc] = dot(z, join(dus, hc, 0)).astype(BF16)
+
+
+def final_kernel(
+    c_ref, z_ref, act_ref, p_ref, q_ref, down_ref, pg_ref, pu_ref, pd_ref, dx_ref,
+    gg_hbm, gu_hbm, gd_hbm, dx_hbm, gg_ref, gu_ref, gd_ref, sem,
 ):
-    da = dot(c3[...].T, down_ref[...])
-    dg3 = (da * p_ref[...].astype(F32)).astype(BF16)
-    du3 = (da * q_ref[...].astype(F32)).astype(BF16)
-    z = jnp.concatenate([z0[...], z1[...], z2[...], z3[...]], axis=1)
-    dg = jnp.concatenate([dg0[...], dg1[...], dg2[...], dg3], axis=0)
-    du = jnp.concatenate([du0[...], du1[...], du2[...], du3], axis=0)
-    c = jnp.concatenate([c0[...], c1[...], c2[...], c3[...]], axis=1)
-    act = jnp.concatenate([act0[...], act1[...], act2[...], act3[...]], axis=0)
-    gd_ref[...] = dot(c, act).astype(BF16)
-    gg_ref[...] = dot(z, dg).astype(BF16)
-    gu_ref[...] = dot(z, du).astype(BF16)
+    copies = [pltpu.make_async_copy(dx_ref, dx_hbm, sem.at[0])]
+    copies[0].start()
+    ct = c_ref[...].T
+    c, z = c_ref[...], z_ref[...]
+    for k, hc in enumerate(chunks(gg_ref.shape[1])):
+        da = dot(ct, down_ref[:, hc])
+        gd_ref[:, hc] = (pd_ref[:, hc].astype(F32) + dot(c, act_ref[:, hc])).astype(BF16)
+        dgate = (da * p_ref[:, hc].astype(F32)).astype(BF16)
+        gg_ref[:, hc] = (pg_ref[:, hc].astype(F32) + dot(z, dgate)).astype(BF16)
+        dup = (da * q_ref[:, hc].astype(F32)).astype(BF16)
+        gu_ref[:, hc] = (pu_ref[:, hc].astype(F32) + dot(z, dup)).astype(BF16)
+        for m, (src, dst) in enumerate(((gg_ref, gg_hbm), (gu_ref, gu_hbm), (gd_ref, gd_hbm))):
+            copies.append(pltpu.make_async_copy(src.at[:, hc], dst.at[:, hc], sem.at[1 + 3 * k + m]))
+            copies[-1].start()
+    for copy in copies:
+        copy.wait()
 
 
 PARAMS = pltpu.CompilerParams(vmem_limit_bytes=20 * 1024 * 1024)
@@ -151,6 +201,21 @@
     return whole(forward_kernel, (x, *w), [(d, t), (d, t), (t, h), (t, h), (t, h)], name)
 
 
+def loading_first(x, w, name):
+    d, t = x.shape
+    h = w[0].shape[1]
+    shapes = [(d, t), (d, t), (t, h), (t, h), (t, h), (d, t), (d, h), (d, h), (d, h)]
+    return pl.pallas_call(
+        loading_forward_kernel,
+        in_specs=[pl.BlockSpec(memory_space=pltpu.HBM)] * 4,
+        out_specs=[pl.BlockSpec(memory_space=pltpu.VMEM)] * len(shapes),
+        out_shape=[pltpu.VMEM(s, BF16) for s in shapes],
+        scratch_shapes=[pltpu.SemaphoreType.DMA((1 + 3 * len(chunks(h)),))],
+        compiler_params=PARAMS,
+        name=name,
+    )(*(pltpu.with_memory_space_constraint(a, pltpu.HBM) for a in (x, *w)))
+
+
 def second(v, c, w, name):
     d, t = v.shape
     h = w[0].shape[1]
@@ -163,42 +228,43 @@
     return whole(first_back_kernel, (x, c, p, q, *w), [(d, t), (t, h), (t, h)], name)
 
 
-def grads(p, q, down, zs, cs, acts, dgs, dus):
-    d, t = zs[0].shape
+def partial(zs, cs, acts, dgs, dus):
+    d, h = zs[0].shape[0], acts[0].shape[1]
+    return whole(partial_kernel, (*zs, *cs, *acts, *dgs, *dus), [(d, h)] * 3, "partial")
+
+
+def final(c, z, act, p, q, down, parts, dx):
+    d, t = c.shape
     h = down.shape[1]
-    step = 512
-    full = pl.BlockSpec(memory_space=pltpu.VMEM)
-    tile = pl.BlockSpec((t, step), lambda k: (0, k))
-    wide = pl.BlockSpec((d, step), lambda k: (0, k))
+    args = (c, z, act, p, q, down, *parts, dx)
     return pl.pallas_call(
-        grads_kernel,
-        grid=(h // step,),
-        in_specs=[tile, tile, wide] + [full] * 8 + [tile] * 10,
-        out_specs=[wide] * 3,
-        out_shape=[jax.ShapeDtypeStruct((d, h), BF16)] * 3,
+        final_kernel,
+        in_specs=[pl.BlockSpec(memory_space=pltpu.VMEM)] * len(args),
+        out_specs=[pl.BlockSpec(memory_space=pltpu.HBM)] * 4,
+        out_shape=[pltpu.HBM(s, BF16) for s in ((d, h), (d, h), (d, h), (d, t))],
+        scratch_shapes=[pltpu.VMEM((d, h), BF16)] * 3 + [pltpu.SemaphoreType.DMA((1 + 3 * len(chunks(h)),))],
         compiler_params=PARAMS,
-        name="grads",
-    )(p, q, down, *(in_vmem(a) for a in (*zs, *cs)), *acts, *dgs, *dus)
+        name="final",
+    )(*(in_vmem(a) for a in args))
 
 
 def local_pair(tokens, cotangent, w_gate, w_up, w_down):
     x, g = tokens[0].T, cotangent[0].T
-    w = (w_gate[0], w_up[0], w_down[0].T)
     x_o = shift(x, 0, True)
     g_b = shift(g, -1)
-    h, z2, act2, p2, q2 = first(x, w, "first_own")
+    h, z2, act2, p2, q2, x, *w = loading_first(x, (w_gate[0], w_up[0], w_down[0].T), "first_own")
     h_b = shift(h, -1)
-    g_bo = shift(after(g_b, x_o), 0, True)
-    d_b, z0, act0, dg0, du0 = second(h_b, g_b, w, "second_own")
-    d = shift(d_b, 1)
+    g_bo = shift(after(g_b, h), 0, True)
+    x_o = after(x_o, g_b)
     h_o, z3, act3, p3, q3 = first(x_o, w, "first_other")
     h_bo = shift(h_o, -1)
-    dx, dg2, du2 = first_back(x, d, p2, q2, w, "first_back_own")
-    d_bo, z1, act1, dg1, du1 = second(h_bo, g_bo, w, "second_other")
+    d_b, z0, act0, dg0, du0 = second(after(h_b, h_o), g_b, w, "second_own")
+    d = shift(d_b, 1)
+    d_bo, z1, act1, dg1, du1 = second(after(h_bo, d_b), g_bo, w, "second_other")
     d_o = shift(d_bo, 1)
-    gg, gu, gd = grads(
-        p3, q3, w[2], (z0, z1, z2, z3), (g_b, g_bo, d, d_o), (act0, act1, act2, act3), (dg0, dg1, dg2), (du0, du1, du2)
-    )
+    dx, dg2, du2 = first_back(x, after(d, d_bo), p2, q2, w, "first_back_own")
+    parts = partial((z0, z1, z2), (g_b, g_bo, d), (act0, act1, act2), (dg0, dg1, dg2), (du0, du1, du2))
+    gg, gu, gd, dx = final(d_o, z3, act3, p3, q3, w[2], parts, dx)
     return dx.T[None], gg[None], gu[None], gd.T[None]
 
 

time: 61.8 us -> 54.8 us (0.89)
  local copies, waits for them, and re-layouts: 6.21 us -> 0 us
  waiting for transfers between devices: 11 us -> 5.17 us
  starting transfers between devices: 9.72 us -> 12.9 us
  Pallas kernels: 34 us -> 35.7 us
    unnamed x13 -> x0, local copies, waits for them, and re-layouts: 6.21 us -> none
    ppermute x7, waiting for transfers between devices: 11 us -> 5.17 us  [shift(): return lax.ppermute(x, ('blk', 'dp'), pairs)]
    pallas_call x5, Pallas kernels: 21.9 us -> 25.5 us  [whole(): pl.pallas_call(kernel, in_specs=[spec] * len(args), out_specs=[spec] * le...]
    ppermute x7, starting transfers between devices: 9.72 us -> 12.9 us  [shift(): return lax.ppermute(x, ('blk', 'dp'), pairs)]
    pallas_call x1 -> x2, Pallas kernels: 12.1 us -> 10.2 us  [the longest x1 5.1 us: loading_first(): pl.pallas_call(loading_forward_kernel, in_specs=[pl.BlockSpec(memory_spac...]
  transfers between devices with their start and end apart: 7 -> 7, of which waited for: 4 -> 3; matrix products, arithmetic and copies ran while one was open for 1% -> 0% of each run, Pallas kernels for 36% -> 56%
where the time goes in v3:
time: 54.8 us; the launch traced here: 54.7 us
  Pallas kernels  35.7 us (65%)
  starting transfers between devices  12.9 us (24%)
  waiting for transfers between devices  5.17 us (9%)
  between operations  0.87 us (2%)
    pallas_call x5, Pallas kernels, whole(): pl.pallas_call(kernel, in_specs=[spec] * len(args), out_specs=[spec] * le...  25.5 us
    ppermute x7, starting transfers between devices, shift(): return lax.ppermute(x, ('blk', 'dp'), pairs)  12.9 us
    ppermute x7, waiting for transfers between devices, shift(): return lax.ppermute(x, ('blk', 'dp'), pairs)  5.17 us
    pallas_call x1, Pallas kernels, loading_first(): pl.pallas_call(loading_forward_kernel, in_specs=[pl.BlockSpec(memory_spac...  5.1 us
    pallas_call x1, Pallas kernels, final(): pl.pallas_call(final_kernel, in_specs=[pl.BlockSpec(memory_space=pltpu.VM...  5.07 us
  transfers between devices with their start and end apart: 7, of which 3 were waited for; matrix products, arithmetic and copies ran while one was open for 0% of the time, Pallas kernels for 56%

profile of v3, /device:TPU:0, one launch (start us, length us, event | category | flops | bytes accessed | tf_op | source)
XLA Modules:
  0.0 54.7 jit_solution(12466668083566704437)
XLA Ops:
  0.6 3.0 %collective-permute-start = (bf16[576,384]{1,0:T(8,128)(2,1)}, bf16[576,384]{1,0:T(8,128)(2,1)S(1)}, u32[]{:S(2)}, u32[]{:S(2)}) collective-permute-start(bf16[576,384]{1,0:T(8,128)(2,1)} %bitcast.22), channel_id=1, source_target_pairs={{0,1},{1,0},{2,3},{3,2},{4,5},{5,4},{6,7},{7,6},{8,9},{9,8},{10,11... | collective-permute-start | bytes 1327112 | tf_op jit(solution)/shard_map/ppermute | solution.py:22
  3.6 3.7 %collective-permute-start.1 = (bf16[576,384]{1,0:T(8,128)(2,1)}, bf16[576,384]{1,0:T(8,128)(2,1)S(1)}, u32[]{:S(2)}, u32[]{:S(2)}) collective-permute-start(bf16[576,384]{1,0:T(8,128)(2,1)} %bitcast.27), channel_id=1, source_target_pairs={{0,30},{1,31},{2,0},{3,1},{4,2},{5,3},{6,4},{7,5},{8,6},{9,7},{10,... | collective-permute-start | bytes 1327112 | tf_op jit(solution)/shard_map/ppermute | solution.py:22
  7.4 5.1 %first_own.1 = (bf16[576,384]{1,0:T(8,128)(2,1)S(1)}, bf16[576,384]{1,0:T(8,128)(2,1)S(1)}, bf16[384,1536]{1,0:T(8,128)(2,1)S(1)}, bf16[384,1536]{1,0:T(8,128)(2...) custom-call(bf16[576,384]{1,0:T(8,128)(2,1)} %bitcast.23, ...), custom_call_target="tpu_custom_call" | custom-call | tf_op jit(solution)/shard_map/first_own/pallas_call | solution.py:208
  12.5 1.0 %collective-permute-start.3 = (bf16[576,384]{1,0:T(8,128)(2,1)S(1)}, bf16[576,384]{1,0:T(8,128)(2,1)S(1)}, u32[]{:S(2)}, u32[]{:S(2)}) collective-permute-start(bf16[576,384]{1,0:T(8,128)(2,1)S(1)} %get-tuple-element.48), channel_id=1, source_target_pairs={{0,30},{1,31},{2,0},{3,1},{4,2},{5,3},{6,4},{7,5},{8,6},{9,7},{10,... | collective-permute-start | bytes 1327112 | tf_op jit(solution)/shard_map/ppermute | solution.py:22
  13.5 0.5 collective-permute-done.x_ref
  14.0 0.0 collective-permute-done.1.c_ref.refs_3_
  14.0 3.4 %first_other.1 = (bf16[576,384]{1,0:T(8,128)(2,1)S(1)}, bf16[576,384]{1,0:T(8,128)(2,1)S(1)}, bf16[384,1536]{1,0:T(8,128)(2,1)S(1)}, bf16[384,1536]{1,0:T(8,128)(2,1)S(1)}, bf16[384,1536]{1,0:T(8,128)(2,1)S(1)}) custom-call(bf16[576,384]{1,0:T(8,128)(2,1)S(1)} %collective-permute-done.x_ref, bf16[576,1536]{1,0:T(8,128)(2,1)S(1)} %get-tuple-element.44.gate_ref, ...), custom_call_target="tpu_custom_call" | custom-call | tf_op jit(solution)/shard_map/first_other/pallas_call | solution.py:188
  17.4 4.0 %collective-permute-start.2 = (bf16[576,384]{1,0:T(8,128)(2,1)S(1)}, bf16[576,384]{1,0:T(8,128)(2,1)S(1)}, u32[]{:S(2)}, u32[]{:S(2)}) collective-permute-start(bf16[576,384]{1,0:T(8,128)(2,1)S(1)} %get-tuple-element.47), channel_id=1, source_target_pairs={{0,30},{1,31},{2,0},{3,1},{4,2},{5,3},{6,4},{7,5},{8,6},{9,7},{10,... | collective-permute-start | bytes 1327112 | tf_op jit(solution)/shard_map/ppermute | solution.py:22
  21.5 0.9 %collective-permute-start.4 = (bf16[576,384]{1,0:T(8,128)(2,1)S(1)}, bf16[576,384]{1,0:T(8,128)(2,1)S(1)}, u32[]{:S(2)}, u32[]{:S(2)}) collective-permute-start(bf16[576,384]{1,0:T(8,128)(2,1)S(1)} %collective-permute-done.1.c_ref.refs_3_), channel_id=1, source_target_pairs={{0,1},{1,0},{2,3},{3,2},{4,5},{5,4},{6,7},{7,6},{8,9},{9,8},{10,11... | collective-permute-start | bytes 1327112 | tf_op jit(solution)/shard_map/ppermute | solution.py:22
  22.4 0.0 collective-permute-done.3.h_ref
  22.4 5.7 %second_own.1 = (bf16[576,384]{1,0:T(8,128)(2,1)S(1)}, bf16[576,384]{1,0:T(8,128)(2,1)S(1)}, bf16[384,1536]{1,0:T(8,128)(2,1)S(1)}, bf16[384,1536]{1,0:T(8,128)(2,1)S(1)}, bf16[384,1536]{1,0:T(8,128)(2,1)S(1)}) custom-call(bf16[576,384]{1,0:T(8,128)(2,1)S(1)} %collective-permute-done.3.h_ref, bf16[576,384]{1,0:T(8,128)(2,1)S(1)} %collective-permute-done.1.c_ref.refs_3_, ...), custom_call_target="tpu_custom_call" | custom-call | tf_op jit(solution)/shard_map/second_own/pallas_call | solution.py:188
  28.1 0.2 collective-permute-start.6
  28.3 0.0 collective-permute-done.2.h_ref
  28.3 1.7 %collective-permute-done.4.c_ref.refs_4_ = bf16[576,384]{1,0:T(8,128)(2,1)S(1)} collective-permute-done((bf16[576,384]{1,0:T(8,128)(2,1)S(1)}, bf16[576,384]{1,0:T(8,128)(2,1)S(1)}, u32[]{:S(2)}, u32[]{:S(2)}) %collective-permute-start.4) | collective-permute-done | bytes 442400 | tf_op jit(solution)/shard_map/ppermute | solution.py:22
  30.1 5.7 %second_other.1 = (bf16[576,384]{1,0:T(8,128)(2,1)S(1)}, bf16[576,384]{1,0:T(8,128)(2,1)S(1)}, bf16[384,1536]{1,0:T(8,128)(2,1)S(1)}, bf16[384,1536]{1,0:T(8,128)(2,1)S(1)}, bf16[384,1536]{1,0:T(8,128)(2,1)S(1)}) custom-call(bf16[576,384]{1,0:T(8,128)(2,1)S(1)} %collective-permute-done.2.h_ref, bf16[576,384]{1,0:T(8,128)(2,1)S(1)} %collective-permute-done.4.c_ref.refs_4_, ...), custom_call_target="tpu_custom_call" | custom-call | tf_op jit(solution)/shard_map/second_other/pallas_call | solution.py:188
  35.8 0.1 collective-permute-start.5
  35.9 2.9 %collective-permute-done.6.c_ref.refs_5_ = bf16[576,384]{1,0:T(8,128)(2,1)S(1)} collective-permute-done((bf16[576,384]{1,0:T(8,128)(2,1)S(1)}, bf16[576,384]{1,0:T(8,128)(2,1)S(1)}, u32[]{:S(2)}, u32[]{:S(2)}) %collective-permute-start.6) | collective-permute-done | bytes 442400 | tf_op jit(solution)/shard_map/ppermute | solution.py:22
  38.7 3.6 %first_back_own.1 = (bf16[576,384]{1,0:T(8,128)(2,1)S(1)}, bf16[384,1536]{1,0:T(8,128)(2,1)S(1)}, bf16[384,1536]{1,0:T(8,128)(2,1)S(1)}) custom-call(bf16[576,384]{1,0:T(8,128)(2,1)S(1)} %get-tuple-element.66.x_ref, bf16[576,384]{1,0:T(8,128)(2,1)S(1)} %collective-permute-done.6.c_ref.refs_5_, bf16[384,1536]{1,0:T(8,128)(2,1)S(1)} %get-tuple-element.68.p_ref, ...), custom_call_target="tpu_custom_call" | custom-call | tf_op jit(solution)/shard_map/first_back_own/pallas_call | solution.py:188
  42.4 7.0 %partial.1 = (bf16[576,1536]{1,0:T(8,128)(2,1)S(1)}, bf16[576,1536]{1,0:T(8,128)(2,1)S(1)}, bf16[576,1536]{1,0:T(8,128)(2,1)S(1)}) custom-call(bf16[576,384]{1,0:T(8,128)(2,1)S(1)} %get-tuple-element.58.refs_0_, bf16[576,384]{1,0:T(8,128)(2,1)S(1)} %get-tuple-element.59.refs_1_, bf16[576,384]{1,0:T(8,128)(2,1)S(1)} %get-tuple-element.60.refs_2_, ...), custom_call_target="tpu_custom_call" | custom-call | tf_op jit(solution)/shard_map/partial/pallas_call | solution.py:188
  49.4 0.0 collective-permute-done.5.c_ref
  49.4 5.1 %final.1 = (bf16[576,1536]{1,0:T(8,128)(2,1)}, bf16[576,1536]{1,0:T(8,128)(2,1)}, bf16[576,1536]{1,0:T(8,128)(2,1)}, bf16[576,384]{1,0:T(8,128)(2,1)}) custom-call(bf16[576,384]{1,0:T(8,128)(2,1)S(1)} %collective-permute-done.5.c_ref, bf16[576,384]{1,0:T(8,128)(2,1)S(1)} %get-tuple-element.54.z_ref, bf16[384,1536]{1,0:T(8,128)(2,1)S(1)} %get-tuple-element.55.act_ref, ...), custom_call_target="tpu_custom_call" | custom-call | tf_op jit(solution)/shard_map/final/pallas_call | solution.py:240
Async XLA Ops:
  0.6 13.4 %collective-permute-start = (bf16[576,384]{1,0:T(8,128)(2,1)}, bf16[576,384]{1,0:T(8,128)(2,1)S(1)}, u32[]{:S(2)}, u32[]{:S(2)}) collective-permute-start(bf16[576,384]{1,0:T(8,128)(2,1)} %bitcast.22), channel_id=1, source_target_pairs={{0,1},{1,0},{2,3},{3,2},{4,5},{5,4},{6,7},{7,6},{8,9},{9,8},{10,11... | collective-permute-start | bytes 1327112 | tf_op jit(solution)/shard_map/ppermute | solution.py:22
  3.6 10.4 %collective-permute-start.1 = (bf16[576,384]{1,0:T(8,128)(2,1)}, bf16[576,384]{1,0:T(8,128)(2,1)S(1)}, u32[]{:S(2)}, u32[]{:S(2)}) collective-permute-start(bf16[576,384]{1,0:T(8,128)(2,1)} %bitcast.27), channel_id=1, source_target_pairs={{0,30},{1,31},{2,0},{3,1},{4,2},{5,3},{6,4},{7,5},{8,6},{9,7},{10,... | collective-permute-start | bytes 1327112 | tf_op jit(solution)/shard_map/ppermute | solution.py:22
  12.5 9.9 %collective-permute-start.3 = (bf16[576,384]{1,0:T(8,128)(2,1)S(1)}, bf16[576,384]{1,0:T(8,128)(2,1)S(1)}, u32[]{:S(2)}, u32[]{:S(2)}) collective-permute-start(bf16[576,384]{1,0:T(8,128)(2,1)S(1)} %get-tuple-element.48), channel_id=1, source_target_pairs={{0,30},{1,31},{2,0},{3,1},{4,2},{5,3},{6,4},{7,5},{8,6},{9,7},{10,... | collective-permute-start | bytes 1327112 | tf_op jit(solution)/shard_map/ppermute | solution.py:22
  17.4 10.9 %collective-permute-start.2 = (bf16[576,384]{1,0:T(8,128)(2,1)S(1)}, bf16[576,384]{1,0:T(8,128)(2,1)S(1)}, u32[]{:S(2)}, u32[]{:S(2)}) collective-permute-start(bf16[576,384]{1,0:T(8,128)(2,1)S(1)} %get-tuple-element.47), channel_id=1, source_target_pairs={{0,30},{1,31},{2,0},{3,1},{4,2},{5,3},{6,4},{7,5},{8,6},{9,7},{10,... | collective-permute-start | bytes 1327112 | tf_op jit(solution)/shard_map/ppermute | solution.py:22
  21.5 8.6 %collective-permute-start.4 = (bf16[576,384]{1,0:T(8,128)(2,1)S(1)}, bf16[576,384]{1,0:T(8,128)(2,1)S(1)}, u32[]{:S(2)}, u32[]{:S(2)}) collective-permute-start(bf16[576,384]{1,0:T(8,128)(2,1)S(1)} %collective-permute-done.1.c_ref.refs_3_), channel_id=1, source_target_pairs={{0,1},{1,0},{2,3},{3,2},{4,5},{5,4},{6,7},{7,6},{8,9},{9,8},{10,11... | collective-permute-start | bytes 1327112 | tf_op jit(solution)/shard_map/ppermute | solution.py:22
  28.1 10.7 %collective-permute-start.6 = (bf16[576,384]{1,0:T(8,128)(2,1)S(1)}, bf16[576,384]{1,0:T(8,128)(2,1)S(1)}, u32[]{:S(2)}, u32[]{:S(2)}) collective-permute-start(bf16[576,384]{1,0:T(8,128)(2,1)S(1)} %get-tuple-element.50), channel_id=1, source_target_pairs={{0,2},{1,3},{2,4},{3,5},{4,6},{5,7},{6,8},{7,9},{8,10},{9,11},{10,... | collective-permute-start | bytes 1327112 | tf_op jit(solution)/shard_map/ppermute | solution.py:22
  35.8 13.6 %collective-permute-start.5 = (bf16[576,384]{1,0:T(8,128)(2,1)S(1)}, bf16[576,384]{1,0:T(8,128)(2,1)S(1)}, u32[]{:S(2)}, u32[]{:S(2)}) collective-permute-start(bf16[576,384]{1,0:T(8,128)(2,1)S(1)} %get-tuple-element.53), channel_id=1, source_target_pairs={{0,2},{1,3},{2,4},{3,5},{4,6},{5,7},{6,8},{7,9},{8,10},{9,11},{10,... | collective-permute-start | bytes 1327112 | tf_op jit(solution)/shard_map/ppermute | solution.py:22

commit v4 on v3

--- a/solution.py
+++ b/solution.py
@@ -26,6 +26,9 @@
     return lax.dot_general(a, b, (dims, ((), ())), preferred_element_type=F32)
 
 
+NT = ((1,), (1,))
+
+
 def after(x, y):
     return lax.optimization_barrier((x, y))[0]
 
@@ -35,9 +38,17 @@
     return inverse, v * inverse
 
 
-def chunks(size):
-    step = 512 if size % 512 == 0 else (256 if size % 256 == 0 else size)
+def chunks(size, step=256):
+    step = step if size % step == 0 else size
     return [slice(k, k + step) for k in range(0, size, step)]
+
+
+def staggered(parts, ahead, use):
+    ready = ahead(parts[0])
+    for k, part in enumerate(parts):
+        following = ahead(parts[k + 1]) if k + 1 < len(parts) else None
+        use(part, ready)
+        ready = following
 
 
 def gate_values(pre_g, pre_u):
@@ -52,27 +63,32 @@
     return (c + inverse * (dz - normed * inner)).astype(BF16)
 
 
-def forward_chunk(hc, zt, total, gate, up, down, act_ref, p_ref, q_ref):
-    pre_g = dot(zt, gate[:, hc])
-    pre_u = dot(zt, up[:, hc])
-    active, p, q = gate_values(pre_g, pre_u)
-    active = active.astype(BF16)
-    act_ref[:, hc] = active
-    p_ref[:, hc] = p.astype(BF16)
-    q_ref[:, hc] = q.astype(BF16)
-    return total + dot(down[:, hc], active, ((1,), (1,)))
-
-
-def forward_kernel(x_ref, gate_ref, up_ref, down_ref, h_ref, z_ref, act_ref, p_ref, q_ref):
+def forward_body(x_ref, gate_ref, up_ref, down_ref, h_ref, z_ref, act_ref, p_ref, q_ref, arrived):
     x = x_ref[...].astype(F32)
     _, normed = normalize(x)
     zed = normed.astype(BF16)
     z_ref[...] = zed
     zt = zed.T
-    total = x
-    for hc in chunks(gate_ref.shape[1]):
-        total = forward_chunk(hc, zt, total, gate_ref, up_ref, down_ref, act_ref, p_ref, q_ref)
-    h_ref[...] = total.astype(BF16)
+    total = [x]
+
+    def ahead(hc):
+        arrived(hc)
+        return dot(zt, gate_ref[:, hc]), dot(zt, up_ref[:, hc])
+
+    def use(hc, ready):
+        active, p, q = gate_values(*ready)
+        active = active.astype(BF16)
+        act_ref[:, hc] = active
+        p_ref[:, hc] = p.astype(BF16)
+        q_ref[:, hc] = q.astype(BF16)
+        total[0] += dot(down_ref[:, hc], active, NT)
+
+    staggered(chunks(gate_ref.shape[1]), ahead, use)
+    h_ref[...] = total[0].astype(BF16)
+
+
+def forward_kernel(*refs):
+    forward_body(*refs, arrived=lambda hc: None)
 
 
 def loading_forward_kernel(
@@ -80,26 +96,20 @@
 ):
     x_copy = pltpu.make_async_copy(x_hbm, x_ref, sem.at[0])
     x_copy.start()
-    parts = chunks(gate_ref.shape[1])
-    copies = []
-    for k, hc in enumerate(parts):
-        copies.append([])
+    copies = {}
+    for k, hc in enumerate(chunks(gate_ref.shape[1])):
+        copies[hc.start] = []
         for m, (src, dst) in enumerate(((gate_hbm, gate_ref), (up_hbm, up_ref), (down_hbm, down_ref))):
             copy = pltpu.make_async_copy(src.at[:, hc], dst.at[:, hc], sem.at[1 + 3 * k + m])
             copy.start()
-            copies[-1].append(copy)
+            copies[hc.start].append(copy)
     x_copy.wait()
-    x = x_ref[...].astype(F32)
-    _, normed = normalize(x)
-    zed = normed.astype(BF16)
-    z_ref[...] = zed
-    zt = zed.T
-    total = x
-    for k, hc in enumerate(parts):
-        for copy in copies[k]:
+
+    def arrived(hc):
+        for copy in copies[hc.start]:
             copy.wait()
-        total = forward_chunk(hc, zt, total, gate_ref, up_ref, down_ref, act_ref, p_ref, q_ref)
-    h_ref[...] = total.astype(BF16)
+
+    forward_body(x_ref, gate_ref, up_ref, down_ref, h_ref, z_ref, act_ref, p_ref, q_ref, arrived)
 
 
 def second_kernel(h_ref, c_ref, gate_ref, up_ref, down_ref, d_ref, z_ref, act_ref, dg_ref, du_ref):
@@ -108,75 +118,98 @@
     z_ref[...] = zed
     zt = zed.T
     ct = c_ref[...].T
-    dz = jnp.zeros(c_ref.shape, F32)
-    for hc in chunks(gate_ref.shape[1]):
-        pre_g = dot(zt, gate_ref[:, hc])
-        pre_u = dot(zt, up_ref[:, hc])
-        da = dot(ct, down_ref[:, hc])
-        active, p, q = gate_values(pre_g, pre_u)
+    dz = [jnp.zeros(c_ref.shape, F32)]
+
+    def ahead(hc):
+        return dot(zt, gate_ref[:, hc]), dot(zt, up_ref[:, hc]), dot(ct, down_ref[:, hc])
+
+    def use(hc, ready):
+        active, p, q = gate_values(*ready[:2])
+        dgate = (ready[2] * p).astype(BF16)
+        dup = (ready[2] * q).astype(BF16)
         act_ref[:, hc] = active.astype(BF16)
-        dgate = (da * p).astype(BF16)
-        dup = (da * q).astype(BF16)
         dg_ref[:, hc] = dgate
         du_ref[:, hc] = dup
-        dz += dot(gate_ref[:, hc], dgate, ((1,), (1,)))
-        dz += dot(up_ref[:, hc], dup, ((1,), (1,)))
-    d_ref[...] = input_cotangent(c_ref[...].astype(F32), dz, inverse, normed)
+        dz[0] += dot(gate_ref[:, hc], dgate, NT) + dot(up_ref[:, hc], dup, NT)
+
+    staggered(chunks(gate_ref.shape[1]), ahead, use)
+    d_ref[...] = input_cotangent(c_ref[...].astype(F32), dz[0], inverse, normed)
 
 
 def first_back_kernel(x_ref, c_ref, p_ref, q_ref, gate_ref, up_ref, down_ref, d_ref, dg_ref, du_ref):
     inverse, normed = normalize(x_ref[...].astype(F32))
     ct = c_ref[...].T
-    dz = jnp.zeros(c_ref.shape, F32)
-    for hc in chunks(gate_ref.shape[1]):
-        da = dot(ct, down_ref[:, hc])
+    dz = [jnp.zeros(c_ref.shape, F32)]
+
+    def ahead(hc):
+        return dot(ct, down_ref[:, hc])
+
+    def use(hc, da):
         dgate = (da * p_ref[:, hc].astype(F32)).astype(BF16)
         dup = (da * q_ref[:, hc].astype(F32)).astype(BF16)
         dg_ref[:, hc] = dgate
         du_ref[:, hc] = dup
-        dz += dot(gate_ref[:, hc], dgate, ((1,), (1,)))
-        dz += dot(up_ref[:, hc], dup, ((1,), (1,)))
-    d_ref[...] = input_cotangent(c_ref[...].astype(F32), dz, inverse, normed)
-
-
-def join(refs, hc, axis):
-    return jnp.concatenate([r[:, hc] for r in refs], axis=axis)
+        dz[0] += dot(gate_ref[:, hc], dgate, NT) + dot(up_ref[:, hc], dup, NT)
+
+    staggered(chunks(gate_ref.shape[1]), ahead, use)
+    d_ref[...] = input_cotangent(c_ref[...].astype(F32), dz[0], inverse, normed)
+
+
+def split(tokens):
+    return (3 * tokens // 256) * 256 - 2 * tokens
 
 
 def partial_kernel(*refs):
     zs, cs, acts, dgs, dus = (refs[3 * k : 3 * k + 3] for k in range(5))
     gg_ref, gu_ref, gd_ref = refs[15:]
-    z = join(zs, slice(None), 1)
-    c = join(cs, slice(None), 1)
+    cut = split(acts[0].shape[0])
+    z = jnp.concatenate([zs[0][...], zs[1][...], zs[2][:, :cut]], axis=1)
+    c = jnp.concatenate([cs[0][...], cs[1][...], cs[2][:, :cut]], axis=1)
+
+    def join(three, hc):
+        return jnp.concatenate([three[0][:, hc], three[1][:, hc], three[2][:cut, hc]], axis=0)
+
     for hc in chunks(gg_ref.shape[1]):
-        gd_ref[:, hc] = dot(c, join(acts, hc, 0)).astype(BF16)
-        gg_ref[:, hc] = dot(z, join(dgs, hc, 0)).astype(BF16)
-        gu_ref[:, hc] = dot(z, join(dus, hc, 0)).astype(BF16)
+        gd_ref[:, hc] = dot(c, join(acts, hc)).astype(BF16)
+        gg_ref[:, hc] = dot(z, join(dgs, hc)).astype(BF16)
+        gu_ref[:, hc] = dot(z, join(dus, hc)).astype(BF16)
 
 
 def final_kernel(
-    c_ref, z_ref, act_ref, p_ref, q_ref, down_ref, pg_ref, pu_ref, pd_ref, dx_ref,
+    c_ref, z_ref, act_ref, p_ref, q_ref, down_ref, pg_ref, pu_ref, pd_ref, dx_ref, c2_ref, z2_ref, act2_ref, dg2_ref, du2_ref,
     gg_hbm, gu_hbm, gd_hbm, dx_hbm, gg_ref, gu_ref, gd_ref, sem,
 ):
     copies = [pltpu.make_async_copy(dx_ref, dx_hbm, sem.at[0])]
     copies[0].start()
+    cut = split(act_ref.shape[0])
     ct = c_ref[...].T
-    c, z = c_ref[...], z_ref[...]
-    for k, hc in enumerate(chunks(gg_ref.shape[1])):
-        da = dot(ct, down_ref[:, hc])
-        gd_ref[:, hc] = (pd_ref[:, hc].astype(F32) + dot(c, act_ref[:, hc])).astype(BF16)
+    c = jnp.concatenate([c2_ref[:, cut:], c_ref[...]], axis=1)
+    z = jnp.concatenate([z2_ref[:, cut:], z_ref[...]], axis=1)
+    parts = chunks(gg_ref.shape[1])
+
+    def add(hc, m, left, rows, part_ref, ref, hbm):
+        ref[:, hc] = (part_ref[:, hc].astype(F32) + dot(left, jnp.concatenate(rows, axis=0))).astype(BF16)
+        copy = pltpu.make_async_copy(ref.at[:, hc], hbm.at[:, hc], sem.at[1 + 3 * (hc.start // parts[0].stop) + m])
+        copy.start()
+        copies.append(copy)
+
+    def ahead(hc):
+        return dot(ct, down_ref[:, hc])
+
+    def use(hc, da):
         dgate = (da * p_ref[:, hc].astype(F32)).astype(BF16)
-        gg_ref[:, hc] = (pg_ref[:, hc].astype(F32) + dot(z, dgate)).astype(BF16)
         dup = (da * q_ref[:, hc].astype(F32)).astype(BF16)
-        gu_ref[:, hc] = (pu_ref[:, hc].astype(F32) + dot(z, dup)).astype(BF16)
-        for m, (src, dst) in enumerate(((gg_ref, gg_hbm), (gu_ref, gu_hbm), (gd_ref, gd_hbm))):
-            copies.append(pltpu.make_async_copy(src.at[:, hc], dst.at[:, hc], sem.at[1 + 3 * k + m]))
-            copies[-1].start()
+        add(hc, 2, c, [act2_ref[cut:, hc], act_ref[:, hc]], pd_ref, gd_ref, gd_hbm)
+        add(hc, 0, z, [dg2_ref[cut:, hc], dgate], pg_ref, gg_ref, gg_hbm)
+        add(hc, 1, z, [du2_ref[cut:, hc], dup], pu_ref, gu_ref, gu_hbm)
+
+    staggered(parts, ahead, use)
     for copy in copies:
         copy.wait()
 
 
 PARAMS = pltpu.CompilerParams(vmem_limit_bytes=20 * 1024 * 1024)
+COST = pl.CostEstimate(flops=10**10, bytes_accessed=3 * 10**7, transcendentals=0)
 
 
 def in_vmem(x):
@@ -191,6 +224,7 @@
         out_specs=[spec] * len(out_shapes),
         out_shape=[pltpu.VMEM(s, BF16) for s in out_shapes],
         compiler_params=PARAMS,
+        cost_estimate=COST,
         name=name,
     )(*(in_vmem(a) for a in args))
 
@@ -212,6 +246,7 @@
         out_shape=[pltpu.VMEM(s, BF16) for s in shapes],
         scratch_shapes=[pltpu.SemaphoreType.DMA((1 + 3 * len(chunks(h)),))],
         compiler_params=PARAMS,
+        cost_estimate=COST,
         name=name,
     )(*(pltpu.with_memory_space_constraint(a, pltpu.HBM) for a in (x, *w)))
 
@@ -233,10 +268,10 @@
     return whole(partial_kernel, (*zs, *cs, *acts, *dgs, *dus), [(d, h)] * 3, "partial")
 
 
-def final(c, z, act, p, q, down, parts, dx):
+def final(c, z, act, p, q, down, parts, dx, held):
     d, t = c.shape
     h = down.shape[1]
-    args = (c, z, act, p, q, down, *parts, dx)
+    args = (c, z, act, p, q, down, *parts, dx, *held)
     return pl.pallas_call(
         final_kernel,
         in_specs=[pl.BlockSpec(memory_space=pltpu.VMEM)] * len(args),
@@ -244,6 +279,7 @@
         out_shape=[pltpu.HBM(s, BF16) for s in ((d, h), (d, h), (d, h), (d, t))],
         scratch_shapes=[pltpu.VMEM((d, h), BF16)] * 3 + [pltpu.SemaphoreType.DMA((1 + 3 * len(chunks(h)),))],
         compiler_params=PARAMS,
+        cost_estimate=COST,
         name="final",
     )(*(in_vmem(a) for a in args))
 
@@ -264,7 +300,7 @@
     d_o = shift(d_bo, 1)
     dx, dg2, du2 = first_back(x, after(d, d_bo), p2, q2, w, "first_back_own")
     parts = partial((z0, z1, z2), (g_b, g_bo, d), (act0, act1, act2), (dg0, dg1, dg2), (du0, du1, du2))
-    gg, gu, gd, dx = final(d_o, z3, act3, p3, q3, w[2], parts, dx)
+    gg, gu, gd, dx = final(d_o, z3, act3, p3, q3, w[2], parts, dx, (d, z2, act2, dg2, du2))
     return dx.T[None], gg[None], gu[None], gd.T[None]
 
 

time: 54.8 us -> 52.2 us (0.953)
  Pallas kernels: 35.7 us -> 32.8 us
  waiting for transfers between devices: 5.17 us -> 5.73 us
    pallas_call x5, Pallas kernels: 25.5 us -> 23 us  [whole(): pl.pallas_call(kernel, in_specs=[spec] * len(args), out_specs=[spec] * le...]
    ppermute x7, waiting for transfers between devices: 5.17 us -> 5.73 us  [shift(): return lax.ppermute(x, ('blk', 'dp'), pairs)]
  transfers between devices with their start and end apart: 7 -> 7, of which waited for: 3 -> 3; matrix products, arithmetic and copies ran while one was open for 0% -> 0% of each run, Pallas kernels for 56% -> 54%
where the time goes in v4:
time: 52.2 us; the launch traced here: 52.1 us
  Pallas kernels  32.8 us (63%)
  starting transfers between devices  12.7 us (24%)
  waiting for transfers between devices  5.73 us (11%)
  between operations  0.87 us (2%)
    pallas_call x5, Pallas kernels, whole(): pl.pallas_call(kernel, in_specs=[spec] * len(args), out_specs=[spec] * le...  23 us
    ppermute x7, starting transfers between devices, shift(): return lax.ppermute(x, ('blk', 'dp'), pairs)  12.7 us
    ppermute x7, waiting for transfers between devices, shift(): return lax.ppermute(x, ('blk', 'dp'), pairs)  5.73 us
    pallas_call x1, Pallas kernels, final(): pl.pallas_call(final_kernel, in_specs=[pl.BlockSpec(memory_space=pltpu.VM...  4.89 us
    pallas_call x1, Pallas kernels, loading_first(): pl.pallas_call(loading_forward_kernel, in_specs=[pl.BlockSpec(memory_spac...  4.86 us
  transfers between devices with their start and end apart: 7, of which 3 were waited for; matrix products, arithmetic and copies ran while one was open for 0% of the time, Pallas kernels for 54%

profile of v4, /device:TPU:0, one launch (start us, length us, event | category | flops | bytes accessed | tf_op | source)
XLA Modules:
  0.0 52.1 jit_solution(3945967946207628818)
XLA Ops:
  0.6 3.0 %collective-permute-start = (bf16[576,384]{1,0:T(8,128)(2,1)}, bf16[576,384]{1,0:T(8,128)(2,1)S(1)}, u32[]{:S(2)}, u32[]{:S(2)}) collective-permute-start(bf16[576,384]{1,0:T(8,128)(2,1)} %bitcast.22), channel_id=1, source_target_pairs={{0,1},{1,0},{2,3},{3,2},{4,5},{5,4},{6,7},{7,6},{8,9},{9,8},{10,11... | collective-permute-start | bytes 1327112 | tf_op jit(solution)/shard_map/ppermute | solution.py:22
  3.6 3.7 %collective-permute-start.1 = (bf16[576,384]{1,0:T(8,128)(2,1)}, bf16[576,384]{1,0:T(8,128)(2,1)S(1)}, u32[]{:S(2)}, u32[]{:S(2)}) collective-permute-start(bf16[576,384]{1,0:T(8,128)(2,1)} %bitcast.24), channel_id=1, source_target_pairs={{0,30},{1,31},{2,0},{3,1},{4,2},{5,3},{6,4},{7,5},{8,6},{9,7},{10,... | collective-permute-start | bytes 1327112 | tf_op jit(solution)/shard_map/ppermute | solution.py:22
  7.4 4.9 %first_own.1 = (bf16[576,384]{1,0:T(8,128)(2,1)S(1)}, bf16[576,384]{1,0:T(8,128)(2,1)S(1)}, bf16[384,1536]{1,0:T(8,128)(2,1)S(1)}, bf16[384,1536]{1,0:T(8,128)(2...) custom-call(bf16[576,384]{1,0:T(8,128)(2,1)} %bitcast.23, ...), custom_call_target="tpu_custom_call" | custom-call | flops 10000000000 | bytes 30000000 | tf_op jit(solution)/shard_map/first_own/pallas_call | solution.py:242
  12.2 1.0 %collective-permute-start.3 = (bf16[576,384]{1,0:T(8,128)(2,1)S(1)}, bf16[576,384]{1,0:T(8,128)(2,1)S(1)}, u32[]{:S(2)}, u32[]{:S(2)}) collective-permute-start(bf16[576,384]{1,0:T(8,128)(2,1)S(1)} %get-tuple-element.48), channel_id=1, source_target_pairs={{0,30},{1,31},{2,0},{3,1},{4,2},{5,3},{6,4},{7,5},{8,6},{9,7},{10,... | collective-permute-start | bytes 1327112 | tf_op jit(solution)/shard_map/ppermute | solution.py:22
  13.2 0.8 %collective-permute-done.refs_0_ = bf16[576,384]{1,0:T(8,128)(2,1)S(1)} collective-permute-done((bf16[576,384]{1,0:T(8,128)(2,1)}, bf16[576,384]{1,0:T(8,128)(2,1)S(1)}, u32[]{:S(2)}, u32[]{:S(2)}) %collective-permute-start) | collective-permute-done | bytes 442400 | tf_op jit(solution)/shard_map/ppermute | solution.py:22
  14.0 0.0 collective-permute-done.1.c_ref.refs_3_
  14.0 1.7 %collective-permute-start.4 = (bf16[576,384]{1,0:T(8,128)(2,1)S(1)}, bf16[576,384]{1,0:T(8,128)(2,1)S(1)}, u32[]{:S(2)}, u32[]{:S(2)}) collective-permute-start(bf16[576,384]{1,0:T(8,128)(2,1)S(1)} %collective-permute-done.1.c_ref.refs_3_), channel_id=1, source_target_pairs={{0,1},{1,0},{2,3},{3,2},{4,5},{5,4},{6,7},{7,6},{8,9},{9,8},{10,11... | collective-permute-start | bytes 1327112 | tf_op jit(solution)/shard_map/ppermute | solution.py:22
  15.8 3.2 %first_other.1 = (bf16[576,384]{1,0:T(8,128)(2,1)S(1)}, bf16[576,384]{1,0:T(8,128)(2,1)S(1)}, bf16[384,1536]{1,0:T(8,128)(2,1)S(1)}, bf16[384,1536]{1,0:T(8,128)(2,1)S(1)}, bf16[384,1536]{1,0:T(8,128)(2,1)S(1)}) custom-call(bf16[576,384]{1,0:T(8,128)(2,1)S(1)} %collective-permute-done.refs_0_, bf16[576,1536]{1,0:T(8,128)(2,1)S(1)} %get-tuple-element.44.refs_1_.gate_ref, ...), custom_call_target="tpu_custom_call" | custom-call | flops 10000000000 | bytes 30000000 | tf_op jit(solution)/shard_map/first_other/pallas_call | solution.py:221
  18.9 2.9 %collective-permute-start.2 = (bf16[576,384]{1,0:T(8,128)(2,1)S(1)}, bf16[576,384]{1,0:T(8,128)(2,1)S(1)}, u32[]{:S(2)}, u32[]{:S(2)}) collective-permute-start(bf16[576,384]{1,0:T(8,128)(2,1)S(1)} %get-tuple-element.47), channel_id=1, source_target_pairs={{0,30},{1,31},{2,0},{3,1},{4,2},{5,3},{6,4},{7,5},{8,6},{9,7},{10,... | collective-permute-start | bytes 1327112 | tf_op jit(solution)/shard_map/ppermute | solution.py:22
  21.8 0.0 collective-permute-done.3.h_ref
  21.8 5.4 %second_own.1 = (bf16[576,384]{1,0:T(8,128)(2,1)S(1)}, bf16[576,384]{1,0:T(8,128)(2,1)S(1)}, bf16[384,1536]{1,0:T(8,128)(2,1)S(1)}, bf16[384,1536]{1,0:T(8,128)(2,1)S(1)}, bf16[384,1536]{1,0:T(8,128)(2,1)S(1)}) custom-call(bf16[576,384]{1,0:T(8,128)(2,1)S(1)} %collective-permute-done.3.h_ref, bf16[576,384]{1,0:T(8,128)(2,1)S(1)} %collective-permute-done.1.c_ref.refs_3_, ...), custom_call_target="tpu_custom_call" | custom-call | flops 10000000000 | bytes 30000000 | tf_op jit(solution)/shard_map/second_own/pallas_call | solution.py:221
  27.2 0.2 collective-permute-start.6
  27.5 0.2 collective-permute-done.2.h_ref
  27.7 0.0 collective-permute-done.4.c_ref.refs_4_
  27.7 5.4 %second_other.1 = (bf16[576,384]{1,0:T(8,128)(2,1)S(1)}, bf16[576,384]{1,0:T(8,128)(2,1)S(1)}, bf16[384,1536]{1,0:T(8,128)(2,1)S(1)}, bf16[384,1536]{1,0:T(8,128)(2,1)S(1)}, bf16[384,1536]{1,0:T(8,128)(2,1)S(1)}) custom-call(bf16[576,384]{1,0:T(8,128)(2,1)S(1)} %collective-permute-done.2.h_ref, bf16[576,384]{1,0:T(8,128)(2,1)S(1)} %collective-permute-done.4.c_ref.refs_4_, ...), custom_call_target="tpu_custom_call" | custom-call | flops 10000000000 | bytes 30000000 | tf_op jit(solution)/shard_map/second_other/pallas_call | solution.py:221
  33.1 0.1 collective-permute-start.5
  33.1 4.8 %collective-permute-done.6.c_ref.refs_5_.c2_ref = bf16[576,384]{1,0:T(8,128)(2,1)S(1)} collective-permute-done((bf16[576,384]{1,0:T(8,128)(2,1)S(1)}, bf16[576,384]{1,0:T(8,128)(2,1)S(1)}, u32[]{:S(2)}, u32[]{:S(2)}) %collective-permute-start.6) | collective-permute-done | bytes 442400 | tf_op jit(solution)/shard_map/ppermute | solution.py:22
  37.9 3.4 %first_back_own.1 = (bf16[576,384]{1,0:T(8,128)(2,1)S(1)}, bf16[384,1536]{1,0:T(8,128)(2,1)S(1)}, bf16[384,1536]{1,0:T(8,128)(2,1)S(1)}) custom-call(bf16[576,384]{1,0:T(8,128)(2,1)S(1)} %get-tuple-element.66.x_ref, bf16[576,384]{1,0:T(8,128)(2,1)S(1)} %collective-permute-done.6.c_ref.refs_5_.c2_ref, bf16[384,1536]{1,0:T(8,128)(2,1)S(1)} %get-tuple-element.68.p_ref, ...), custom_call_target="tpu_custom_call" | custom-call | flops 10000000000 | bytes 30000000 | tf_op jit(solution)/shard_map/first_back_own/pallas_call | solution.py:221
  41.3 5.7 %partial.1 = (bf16[576,1536]{1,0:T(8,128)(2,1)S(1)}, bf16[576,1536]{1,0:T(8,128)(2,1)S(1)}, bf16[576,1536]{1,0:T(8,128)(2,1)S(1)}) custom-call(bf16[576,384]{1,0:T(8,128)(2,1)S(1)} %get-tuple-element.58.refs_0_, bf16[576,384]{1,0:T(8,128)(2,1)S(1)} %get-tuple-element.59.refs_1_, bf16[576,384]{1,0:T(8,128)(2,1)S(1)} %get-tuple-element.60.refs_2_.z2_ref, ...), custom_call_target="tpu_custom_call" | custom-call | flops 10000000000 | bytes 30000000 | tf_op jit(solution)/shard_map/partial/pallas_call | solution.py:221
  47.0 0.0 collective-permute-done.5.c_ref
  47.0 4.9 %final.1 = (bf16[576,1536]{1,0:T(8,128)(2,1)}, bf16[576,1536]{1,0:T(8,128)(2,1)}, bf16[576,1536]{1,0:T(8,128)(2,1)}, bf16[576,384]{1,0:T(8,128)(2,1)}) custom-call(bf16[576,384]{1,0:T(8,128)(2,1)S(1)} %collective-permute-done.5.c_ref, bf16[576,384]{1,0:T(8,128)(2,1)S(1)} %get-tuple-element.54.z_ref, bf16[384,1536]{1,0:T(8,128)(2,1)S(1)} %get-tuple-element.55.act_ref, ...), custom_call_target="tpu_custom_call" | custom-call | flops 10000000000 | bytes 30000000 | tf_op jit(solution)/shard_map/final/pallas_call | solution.py:275
Async XLA Ops:
  0.6 13.4 %collective-permute-start = (bf16[576,384]{1,0:T(8,128)(2,1)}, bf16[576,384]{1,0:T(8,128)(2,1)S(1)}, u32[]{:S(2)}, u32[]{:S(2)}) collective-permute-start(bf16[576,384]{1,0:T(8,128)(2,1)} %bitcast.22), channel_id=1, source_target_pairs={{0,1},{1,0},{2,3},{3,2},{4,5},{5,4},{6,7},{7,6},{8,9},{9,8},{10,11... | collective-permute-start | bytes 1327112 | tf_op jit(solution)/shard_map/ppermute | solution.py:22
  3.6 10.4 %collective-permute-start.1 = (bf16[576,384]{1,0:T(8,128)(2,1)}, bf16[576,384]{1,0:T(8,128)(2,1)S(1)}, u32[]{:S(2)}, u32[]{:S(2)}) collective-permute-start(bf16[576,384]{1,0:T(8,128)(2,1)} %bitcast.24), channel_id=1, source_target_pairs={{0,30},{1,31},{2,0},{3,1},{4,2},{5,3},{6,4},{7,5},{8,6},{9,7},{10,... | collective-permute-start | bytes 1327112 | tf_op jit(solution)/shard_map/ppermute | solution.py:22
  12.2 9.6 %collective-permute-start.3 = (bf16[576,384]{1,0:T(8,128)(2,1)S(1)}, bf16[576,384]{1,0:T(8,128)(2,1)S(1)}, u32[]{:S(2)}, u32[]{:S(2)}) collective-permute-start(bf16[576,384]{1,0:T(8,128)(2,1)S(1)} %get-tuple-element.48), channel_id=1, source_target_pairs={{0,30},{1,31},{2,0},{3,1},{4,2},{5,3},{6,4},{7,5},{8,6},{9,7},{10,... | collective-permute-start | bytes 1327112 | tf_op jit(solution)/shard_map/ppermute | solution.py:22
  14.0 13.7 %collective-permute-start.4 = (bf16[576,384]{1,0:T(8,128)(2,1)S(1)}, bf16[576,384]{1,0:T(8,128)(2,1)S(1)}, u32[]{:S(2)}, u32[]{:S(2)}) collective-permute-start(bf16[576,384]{1,0:T(8,128)(2,1)S(1)} %collective-permute-done.1.c_ref.refs_3_), channel_id=1, source_target_pairs={{0,1},{1,0},{2,3},{3,2},{4,5},{5,4},{6,7},{7,6},{8,9},{9,8},{10,11... | collective-permute-start | bytes 1327112 | tf_op jit(solution)/shard_map/ppermute | solution.py:22
  18.9 8.7 %collective-permute-start.2 = (bf16[576,384]{1,0:T(8,128)(2,1)S(1)}, bf16[576,384]{1,0:T(8,128)(2,1)S(1)}, u32[]{:S(2)}, u32[]{:S(2)}) collective-permute-start(bf16[576,384]{1,0:T(8,128)(2,1)S(1)} %get-tuple-element.47), channel_id=1, source_target_pairs={{0,30},{1,31},{2,0},{3,1},{4,2},{5,3},{6,4},{7,5},{8,6},{9,7},{10,... | collective-permute-start | bytes 1327112 | tf_op jit(solution)/shard_map/ppermute | solution.py:22
  27.2 10.7 %collective-permute-start.6 = (bf16[576,384]{1,0:T(8,128)(2,1)S(1)}, bf16[576,384]{1,0:T(8,128)(2,1)S(1)}, u32[]{:S(2)}, u32[]{:S(2)}) collective-permute-start(bf16[576,384]{1,0:T(8,128)(2,1)S(1)} %get-tuple-element.50), channel_id=1, source_target_pairs={{0,2},{1,3},{2,4},{3,5},{4,6},{5,7},{6,8},{7,9},{8,10},{9,11},{10,... | collective-permute-start | bytes 1327112 | tf_op jit(solution)/shard_map/ppermute | solution.py:22
  33.1 13.9 %collective-permute-start.5 = (bf16[576,384]{1,0:T(8,128)(2,1)S(1)}, bf16[576,384]{1,0:T(8,128)(2,1)S(1)}, u32[]{:S(2)}, u32[]{:S(2)}) collective-permute-start(bf16[576,384]{1,0:T(8,128)(2,1)S(1)} %get-tuple-element.53), channel_id=1, source_target_pairs={{0,2},{1,3},{2,4},{3,5},{4,6},{5,7},{6,8},{7,9},{8,10},{9,11},{10,... | collective-permute-start | bytes 1327112 | tf_op jit(solution)/shard_map/ppermute | solution.py:22

commit v5 on v4

--- a/solution.py
+++ b/solution.py
@@ -69,7 +69,6 @@
     zed = normed.astype(BF16)
     z_ref[...] = zed
     zt = zed.T
-    total = [x]
 
     def ahead(hc):
         arrived(hc)
@@ -77,14 +76,12 @@
 
     def use(hc, ready):
         active, p, q = gate_values(*ready)
-        active = active.astype(BF16)
-        act_ref[:, hc] = active
+        act_ref[:, hc] = active.astype(BF16)
         p_ref[:, hc] = p.astype(BF16)
         q_ref[:, hc] = q.astype(BF16)
-        total[0] += dot(down_ref[:, hc], active, NT)
 
     staggered(chunks(gate_ref.shape[1]), ahead, use)
-    h_ref[...] = total[0].astype(BF16)
+    h_ref[...] = (x + dot(down_ref[...], act_ref[...], NT)).astype(BF16)
 
 
 def forward_kernel(*refs):
@@ -118,41 +115,35 @@
     z_ref[...] = zed
     zt = zed.T
     ct = c_ref[...].T
-    dz = [jnp.zeros(c_ref.shape, F32)]
 
     def ahead(hc):
         return dot(zt, gate_ref[:, hc]), dot(zt, up_ref[:, hc]), dot(ct, down_ref[:, hc])
 
     def use(hc, ready):
         active, p, q = gate_values(*ready[:2])
-        dgate = (ready[2] * p).astype(BF16)
-        dup = (ready[2] * q).astype(BF16)
         act_ref[:, hc] = active.astype(BF16)
-        dg_ref[:, hc] = dgate
-        du_ref[:, hc] = dup
-        dz[0] += dot(gate_ref[:, hc], dgate, NT) + dot(up_ref[:, hc], dup, NT)
+        dg_ref[:, hc] = (ready[2] * p).astype(BF16)
+        du_ref[:, hc] = (ready[2] * q).astype(BF16)
 
     staggered(chunks(gate_ref.shape[1]), ahead, use)
-    d_ref[...] = input_cotangent(c_ref[...].astype(F32), dz[0], inverse, normed)
+    dz = dot(gate_ref[...], dg_ref[...], NT) + dot(up_ref[...], du_ref[...], NT)
+    d_ref[...] = input_cotangent(c_ref[...].astype(F32), dz, inverse, normed)
 
 
 def first_back_kernel(x_ref, c_ref, p_ref, q_ref, gate_ref, up_ref, down_ref, d_ref, dg_ref, du_ref):
     inverse, normed = normalize(x_ref[...].astype(F32))
     ct = c_ref[...].T
-    dz = [jnp.zeros(c_ref.shape, F32)]
 
     def ahead(hc):
         return dot(ct, down_ref[:, hc])
 
     def use(hc, da):
-        dgate = (da * p_ref[:, hc].astype(F32)).astype(BF16)
-        dup = (da * q_ref[:, hc].astype(F32)).astype(BF16)
-        dg_ref[:, hc] = dgate
-        du_ref[:, hc] = dup
-        dz[0] += dot(gate_ref[:, hc], dgate, NT) + dot(up_ref[:, hc], dup, NT)
+        dg_ref[:, hc] = (da * p_ref[:, hc].astype(F32)).astype(BF16)
+        du_ref[:, hc] = (da * q_ref[:, hc].astype(F32)).astype(BF16)
 
     staggered(chunks(gate_ref.shape[1]), ahead, use)
-    d_ref[...] = input_cotangent(c_ref[...].astype(F32), dz[0], inverse, normed)
+    dz = dot(gate_ref[...], dg_ref[...], NT) + dot(up_ref[...], du_ref[...], NT)
+    d_ref[...] = input_cotangent(c_ref[...].astype(F32), dz, inverse, normed)
 
 
 def split(tokens):

time: 52.2 us -> 52 us (level)
  waiting for transfers between devices: 5.73 us -> 5.05 us
  Pallas kernels: 32.8 us -> 33.4 us
    pallas_call x1, Pallas kernels: 4.86 us -> 5.76 us  [loading_first(): pl.pallas_call(loading_forward_kernel, in_specs=[pl.BlockSpec(memory_spac...]
    ppermute x7, waiting for transfers between devices: 5.73 us -> 5.05 us  [shift(): return lax.ppermute(x, ('blk', 'dp'), pairs)]
  transfers between devices with their start and end apart: 7 -> 7, of which waited for: 3 -> 2; matrix products, arithmetic and copies ran while one was open for 0% -> 0% of each run, Pallas kernels for 54% -> 55%
where the time goes in v5:
time: 52 us; the launch traced here: 51.9 us
  Pallas kernels  33.4 us (64%)
  starting transfers between devices  12.5 us (24%)
  waiting for transfers between devices  5.05 us (10%)
  between operations  0.87 us (2%)
    pallas_call x5, Pallas kernels, whole(): pl.pallas_call(kernel, in_specs=[spec] * len(args), out_specs=[spec] * le...  22.8 us
    ppermute x7, starting transfers between devices, shift(): return lax.ppermute(x, ('blk', 'dp'), pairs)  12.5 us
    pallas_call x1, Pallas kernels, loading_first(): pl.pallas_call(loading_forward_kernel, in_specs=[pl.BlockSpec(memory_spac...  5.76 us
    ppermute x7, waiting for transfers between devices, shift(): return lax.ppermute(x, ('blk', 'dp'), pairs)  5.05 us
    pallas_call x1, Pallas kernels, final(): pl.pallas_call(final_kernel, in_specs=[pl.BlockSpec(memory_space=pltpu.VM...  4.9 us
  transfers between devices with their start and end apart: 7, of which 2 were waited for; matrix products, arithmetic and copies ran while one was open for 0% of the time, Pallas kernels for 55%

profile of v5, /device:TPU:0, one launch (start us, length us, event | category | flops | bytes accessed | tf_op | source)
XLA Modules:
  0.0 51.9 jit_solution(4038285510281709635)
XLA Ops:
  0.6 3.0 %collective-permute-start = (bf16[576,384]{1,0:T(8,128)(2,1)}, bf16[576,384]{1,0:T(8,128)(2,1)S(1)}, u32[]{:S(2)}, u32[]{:S(2)}) collective-permute-start(bf16[576,384]{1,0:T(8,128)(2,1)} %bitcast.22), channel_id=1, source_target_pairs={{0,1},{1,0},{2,3},{3,2},{4,5},{5,4},{6,7},{7,6},{8,9},{9,8},{10,11... | collective-permute-start | bytes 1327112 | tf_op jit(solution)/shard_map/ppermute | solution.py:22
  3.6 3.7 %collective-permute-start.1 = (bf16[576,384]{1,0:T(8,128)(2,1)}, bf16[576,384]{1,0:T(8,128)(2,1)S(1)}, u32[]{:S(2)}, u32[]{:S(2)}) collective-permute-start(bf16[576,384]{1,0:T(8,128)(2,1)} %bitcast.24), channel_id=1, source_target_pairs={{0,30},{1,31},{2,0},{3,1},{4,2},{5,3},{6,4},{7,5},{8,6},{9,7},{10,... | collective-permute-start | bytes 1327112 | tf_op jit(solution)/shard_map/ppermute | solution.py:22
  7.4 5.8 %first_own.1 = (bf16[576,384]{1,0:T(8,128)(2,1)S(1)}, bf16[576,384]{1,0:T(8,128)(2,1)S(1)}, bf16[384,1536]{1,0:T(8,128)(2,1)S(1)}, bf16[384,1536]{1,0:T(8,128)(2...) custom-call(bf16[576,384]{1,0:T(8,128)(2,1)} %bitcast.23, ...), custom_call_target="tpu_custom_call" | custom-call | flops 10000000000 | bytes 30000000 | tf_op jit(solution)/shard_map/first_own/pallas_call | solution.py:233
  13.1 1.0 %collective-permute-start.3 = (bf16[576,384]{1,0:T(8,128)(2,1)S(1)}, bf16[576,384]{1,0:T(8,128)(2,1)S(1)}, u32[]{:S(2)}, u32[]{:S(2)}) collective-permute-start(bf16[576,384]{1,0:T(8,128)(2,1)S(1)} %get-tuple-element.48), channel_id=1, source_target_pairs={{0,30},{1,31},{2,0},{3,1},{4,2},{5,3},{6,4},{7,5},{8,6},{9,7},{10,... | collective-permute-start | bytes 1327112 | tf_op jit(solution)/shard_map/ppermute | solution.py:22
  14.1 0.0 collective-permute-done.refs_0_
  14.1 0.0 collective-permute-done.1.c_ref.refs_3_
  14.2 1.6 %collective-permute-start.4 = (bf16[576,384]{1,0:T(8,128)(2,1)S(1)}, bf16[576,384]{1,0:T(8,128)(2,1)S(1)}, u32[]{:S(2)}, u32[]{:S(2)}) collective-permute-start(bf16[576,384]{1,0:T(8,128)(2,1)S(1)} %collective-permute-done.1.c_ref.refs_3_), channel_id=1, source_target_pairs={{0,1},{1,0},{2,3},{3,2},{4,5},{5,4},{6,7},{7,6},{8,9},{9,8},{10,11... | collective-permute-start | bytes 1327112 | tf_op jit(solution)/shard_map/ppermute | solution.py:22
  15.8 3.1 %first_other.1 = (bf16[576,384]{1,0:T(8,128)(2,1)S(1)}, bf16[576,384]{1,0:T(8,128)(2,1)S(1)}, bf16[384,1536]{1,0:T(8,128)(2,1)S(1)}, bf16[384,1536]{1,0:T(8,128)(2,1)S(1)}, bf16[384,1536]{1,0:T(8,128)(2,1)S(1)}) custom-call(bf16[576,384]{1,0:T(8,128)(2,1)S(1)} %collective-permute-done.refs_0_, bf16[576,1536]{1,0:T(8,128)(2,1)S(1)} %get-tuple-element.44.refs_1_.gate_ref, ...), custom_call_target="tpu_custom_call" | custom-call | flops 10000000000 | bytes 30000000 | tf_op jit(solution)/shard_map/first_other/pallas_call | solution.py:212
  18.9 2.9 %collective-permute-start.2 = (bf16[576,384]{1,0:T(8,128)(2,1)S(1)}, bf16[576,384]{1,0:T(8,128)(2,1)S(1)}, u32[]{:S(2)}, u32[]{:S(2)}) collective-permute-start(bf16[576,384]{1,0:T(8,128)(2,1)S(1)} %get-tuple-element.47), channel_id=1, source_target_pairs={{0,30},{1,31},{2,0},{3,1},{4,2},{5,3},{6,4},{7,5},{8,6},{9,7},{10,... | collective-permute-start | bytes 1327112 | tf_op jit(solution)/shard_map/ppermute | solution.py:22
  21.8 0.0 collective-permute-done.3.h_ref
  21.8 5.3 %second_own.1 = (bf16[576,384]{1,0:T(8,128)(2,1)S(1)}, bf16[576,384]{1,0:T(8,128)(2,1)S(1)}, bf16[384,1536]{1,0:T(8,128)(2,1)S(1)}, bf16[384,1536]{1,0:T(8,128)(2,1)S(1)}, bf16[384,1536]{1,0:T(8,128)(2,1)S(1)}) custom-call(bf16[576,384]{1,0:T(8,128)(2,1)S(1)} %collective-permute-done.3.h_ref, bf16[576,384]{1,0:T(8,128)(2,1)S(1)} %collective-permute-done.1.c_ref.refs_3_, ...), custom_call_target="tpu_custom_call" | custom-call | flops 10000000000 | bytes 30000000 | tf_op jit(solution)/shard_map/second_own/pallas_call | solution.py:212
  27.1 0.2 collective-permute-start.6
  27.3 0.3 collective-permute-done.2.h_ref
  27.6 0.0 collective-permute-done.4.c_ref.refs_4_
  27.6 5.3 %second_other.1 = (bf16[576,384]{1,0:T(8,128)(2,1)S(1)}, bf16[576,384]{1,0:T(8,128)(2,1)S(1)}, bf16[384,1536]{1,0:T(8,128)(2,1)S(1)}, bf16[384,1536]{1,0:T(8,128)(2,1)S(1)}, bf16[384,1536]{1,0:T(8,128)(2,1)S(1)}) custom-call(bf16[576,384]{1,0:T(8,128)(2,1)S(1)} %collective-permute-done.2.h_ref, bf16[576,384]{1,0:T(8,128)(2,1)S(1)} %collective-permute-done.4.c_ref.refs_4_, ...), custom_call_target="tpu_custom_call" | custom-call | flops 10000000000 | bytes 30000000 | tf_op jit(solution)/shard_map/second_other/pallas_call | solution.py:212
  32.9 0.1 collective-permute-start.5
  33.0 4.8 %collective-permute-done.6.c_ref.refs_5_.c2_ref = bf16[576,384]{1,0:T(8,128)(2,1)S(1)} collective-permute-done((bf16[576,384]{1,0:T(8,128)(2,1)S(1)}, bf16[576,384]{1,0:T(8,128)(2,1)S(1)}, u32[]{:S(2)}, u32[]{:S(2)}) %collective-permute-start.6) | collective-permute-done | bytes 442400 | tf_op jit(solution)/shard_map/ppermute | solution.py:22
  37.7 3.4 %first_back_own.1 = (bf16[576,384]{1,0:T(8,128)(2,1)S(1)}, bf16[384,1536]{1,0:T(8,128)(2,1)S(1)}, bf16[384,1536]{1,0:T(8,128)(2,1)S(1)}) custom-call(bf16[576,384]{1,0:T(8,128)(2,1)S(1)} %get-tuple-element.66.x_ref, bf16[576,384]{1,0:T(8,128)(2,1)S(1)} %collective-permute-done.6.c_ref.refs_5_.c2_ref, bf16[384,1536]{1,0:T(8,128)(2,1)S(1)} %get-tuple-element.68.p_ref, ...), custom_call_target="tpu_custom_call" | custom-call | flops 10000000000 | bytes 30000000 | tf_op jit(solution)/shard_map/first_back_own/pallas_call | solution.py:212
  41.2 5.7 %partial.1 = (bf16[576,1536]{1,0:T(8,128)(2,1)S(1)}, bf16[576,1536]{1,0:T(8,128)(2,1)S(1)}, bf16[576,1536]{1,0:T(8,128)(2,1)S(1)}) custom-call(bf16[576,384]{1,0:T(8,128)(2,1)S(1)} %get-tuple-element.58.refs_0_, bf16[576,384]{1,0:T(8,128)(2,1)S(1)} %get-tuple-element.59.refs_1_, bf16[576,384]{1,0:T(8,128)(2,1)S(1)} %get-tuple-element.60.refs_2_.z2_ref, ...), custom_call_target="tpu_custom_call" | custom-call | flops 10000000000 | bytes 30000000 | tf_op jit(solution)/shard_map/partial/pallas_call | solution.py:212
  46.8 0.0 collective-permute-done.5.c_ref
  46.8 4.9 %final.1 = (bf16[576,1536]{1,0:T(8,128)(2,1)}, bf16[576,1536]{1,0:T(8,128)(2,1)}, bf16[576,1536]{1,0:T(8,128)(2,1)}, bf16[576,384]{1,0:T(8,128)(2,1)}) custom-call(bf16[576,384]{1,0:T(8,128)(2,1)S(1)} %collective-permute-done.5.c_ref, bf16[576,384]{1,0:T(8,128)(2,1)S(1)} %get-tuple-element.54.z_ref, bf16[384,1536]{1,0:T(8,128)(2,1)S(1)} %get-tuple-element.55.act_ref, ...), custom_call_target="tpu_custom_call" | custom-call | flops 10000000000 | bytes 30000000 | tf_op jit(solution)/shard_map/final/pallas_call | solution.py:266
Async XLA Ops:
  0.6 13.5 %collective-permute-start = (bf16[576,384]{1,0:T(8,128)(2,1)}, bf16[576,384]{1,0:T(8,128)(2,1)S(1)}, u32[]{:S(2)}, u32[]{:S(2)}) collective-permute-start(bf16[576,384]{1,0:T(8,128)(2,1)} %bitcast.22), channel_id=1, source_target_pairs={{0,1},{1,0},{2,3},{3,2},{4,5},{5,4},{6,7},{7,6},{8,9},{9,8},{10,11... | collective-permute-start | bytes 1327112 | tf_op jit(solution)/shard_map/ppermute | solution.py:22
  3.6 10.5 %collective-permute-start.1 = (bf16[576,384]{1,0:T(8,128)(2,1)}, bf16[576,384]{1,0:T(8,128)(2,1)S(1)}, u32[]{:S(2)}, u32[]{:S(2)}) collective-permute-start(bf16[576,384]{1,0:T(8,128)(2,1)} %bitcast.24), channel_id=1, source_target_pairs={{0,30},{1,31},{2,0},{3,1},{4,2},{5,3},{6,4},{7,5},{8,6},{9,7},{10,... | collective-permute-start | bytes 1327112 | tf_op jit(solution)/shard_map/ppermute | solution.py:22
  13.1 8.7 %collective-permute-start.3 = (bf16[576,384]{1,0:T(8,128)(2,1)S(1)}, bf16[576,384]{1,0:T(8,128)(2,1)S(1)}, u32[]{:S(2)}, u32[]{:S(2)}) collective-permute-start(bf16[576,384]{1,0:T(8,128)(2,1)S(1)} %get-tuple-element.48), channel_id=1, source_target_pairs={{0,30},{1,31},{2,0},{3,1},{4,2},{5,3},{6,4},{7,5},{8,6},{9,7},{10,... | collective-permute-start | bytes 1327112 | tf_op jit(solution)/shard_map/ppermute | solution.py:22
  14.2 13.4 %collective-permute-start.4 = (bf16[576,384]{1,0:T(8,128)(2,1)S(1)}, bf16[576,384]{1,0:T(8,128)(2,1)S(1)}, u32[]{:S(2)}, u32[]{:S(2)}) collective-permute-start(bf16[576,384]{1,0:T(8,128)(2,1)S(1)} %collective-permute-done.1.c_ref.refs_3_), channel_id=1, source_target_pairs={{0,1},{1,0},{2,3},{3,2},{4,5},{5,4},{6,7},{7,6},{8,9},{9,8},{10,11... | collective-permute-start | bytes 1327112 | tf_op jit(solution)/shard_map/ppermute | solution.py:22
  18.9 8.7 %collective-permute-start.2 = (bf16[576,384]{1,0:T(8,128)(2,1)S(1)}, bf16[576,384]{1,0:T(8,128)(2,1)S(1)}, u32[]{:S(2)}, u32[]{:S(2)}) collective-permute-start(bf16[576,384]{1,0:T(8,128)(2,1)S(1)} %get-tuple-element.47), channel_id=1, source_target_pairs={{0,30},{1,31},{2,0},{3,1},{4,2},{5,3},{6,4},{7,5},{8,6},{9,7},{10,... | collective-permute-start | bytes 1327112 | tf_op jit(solution)/shard_map/ppermute | solution.py:22
  27.1 10.7 %collective-permute-start.6 = (bf16[576,384]{1,0:T(8,128)(2,1)S(1)}, bf16[576,384]{1,0:T(8,128)(2,1)S(1)}, u32[]{:S(2)}, u32[]{:S(2)}) collective-permute-start(bf16[576,384]{1,0:T(8,128)(2,1)S(1)} %get-tuple-element.50), channel_id=1, source_target_pairs={{0,2},{1,3},{2,4},{3,5},{4,6},{5,7},{6,8},{7,9},{8,10},{9,11},{10,... | collective-permute-start | bytes 1327112 | tf_op jit(solution)/shard_map/ppermute | solution.py:22
  32.9 13.9 %collective-permute-start.5 = (bf16[576,384]{1,0:T(8,128)(2,1)S(1)}, bf16[576,384]{1,0:T(8,128)(2,1)S(1)}, u32[]{:S(2)}, u32[]{:S(2)}) collective-permute-start(bf16[576,384]{1,0:T(8,128)(2,1)S(1)} %get-tuple-element.53), channel_id=1, source_target_pairs={{0,2},{1,3},{2,4},{3,5},{4,6},{5,7},{6,8},{7,9},{8,10},{9,11},{10,... | collective-permute-start | bytes 1327112 | tf_op jit(solution)/shard_map/ppermute | solution.py:22

commit v6 on v5

--- a/solution.py
+++ b/solution.py
@@ -130,6 +130,32 @@
     d_ref[...] = input_cotangent(c_ref[...].astype(F32), dz, inverse, normed)
 
 
+def second_grads_kernel(
+    h_ref, c_ref, gate_ref, up_ref, down_ref, z0_ref, c0_ref, act0_ref, dg0_ref, du0_ref, gg_ref, gu_ref, gd_ref
+):
+    _, normed = normalize(h_ref[...].astype(F32))
+    zed = normed.astype(BF16)
+    zt = zed.T
+    ct = c_ref[...].T
+    z = jnp.concatenate([z0_ref[...], zed], axis=1)
+    c = jnp.concatenate([c0_ref[...], c_ref[...]], axis=1)
+
+    def ahead(hc):
+        return dot(zt, gate_ref[:, hc]), dot(zt, up_ref[:, hc]), dot(ct, down_ref[:, hc])
+
+    def use(hc, ready):
+        active, p, q = gate_values(*ready[:2])
+        gd_ref[:, hc] = dot(c, stack(act0_ref[:, hc], active)).astype(BF16)
+        gg_ref[:, hc] = dot(z, stack(dg0_ref[:, hc], ready[2] * p)).astype(BF16)
+        gu_ref[:, hc] = dot(z, stack(du0_ref[:, hc], ready[2] * q)).astype(BF16)
+
+    staggered(chunks(gate_ref.shape[1]), ahead, use)
+
+
+def stack(above, below):
+    return jnp.concatenate([above, below.astype(BF16)], axis=0)
+
+
 def first_back_kernel(x_ref, c_ref, p_ref, q_ref, gate_ref, up_ref, down_ref, d_ref, dg_ref, du_ref):
     inverse, normed = normalize(x_ref[...].astype(F32))
     ct = c_ref[...].T
@@ -144,26 +170,6 @@
     staggered(chunks(gate_ref.shape[1]), ahead, use)
     dz = dot(gate_ref[...], dg_ref[...], NT) + dot(up_ref[...], du_ref[...], NT)
     d_ref[...] = input_cotangent(c_ref[...].astype(F32), dz, inverse, normed)
-
-
-def split(tokens):
-    return (3 * tokens // 256) * 256 - 2 * tokens
-
-
-def partial_kernel(*refs):
-    zs, cs, acts, dgs, dus = (refs[3 * k : 3 * k + 3] for k in range(5))
-    gg_ref, gu_ref, gd_ref = refs[15:]
-    cut = split(acts[0].shape[0])
-    z = jnp.concatenate([zs[0][...], zs[1][...], zs[2][:, :cut]], axis=1)
-    c = jnp.concatenate([cs[0][...], cs[1][...], cs[2][:, :cut]], axis=1)
-
-    def join(three, hc):
-        return jnp.concatenate([three[0][:, hc], three[1][:, hc], three[2][:cut, hc]], axis=0)
-
-    for hc in chunks(gg_ref.shape[1]):
-        gd_ref[:, hc] = dot(c, join(acts, hc)).astype(BF16)
-        gg_ref[:, hc] = dot(z, join(dgs, hc)).astype(BF16)
-        gu_ref[:, hc] = dot(z, join(dus, hc)).astype(BF16)
 
 
 def final_kernel(
@@ -172,14 +178,13 @@
 ):
     copies = [pltpu.make_async_copy(dx_ref, dx_hbm, sem.at[0])]
     copies[0].start()
-    cut = split(act_ref.shape[0])
     ct = c_ref[...].T
-    c = jnp.concatenate([c2_ref[:, cut:], c_ref[...]], axis=1)
-    z = jnp.concatenate([z2_ref[:, cut:], z_ref[...]], axis=1)
+    c = jnp.concatenate([c2_ref[...], c_ref[...]], axis=1)
+    z = jnp.concatenate([z2_ref[...], z_ref[...]], axis=1)
     parts = chunks(gg_ref.shape[1])
 
-    def add(hc, m, left, rows, part_ref, ref, hbm):
-        ref[:, hc] = (part_ref[:, hc].astype(F32) + dot(left, jnp.concatenate(rows, axis=0))).astype(BF16)
+    def add(hc, m, left, right, part_ref, ref, hbm):
+        ref[:, hc] = (part_ref[:, hc].astype(F32) + dot(left, right)).astype(BF16)
         copy = pltpu.make_async_copy(ref.at[:, hc], hbm.at[:, hc], sem.at[1 + 3 * (hc.start // parts[0].stop) + m])
         copy.start()
         copies.append(copy)
@@ -188,11 +193,9 @@
         return dot(ct, down_ref[:, hc])
 
     def use(hc, da):
-        dgate = (da * p_ref[:, hc].astype(F32)).astype(BF16)
-        dup = (da * q_ref[:, hc].astype(F32)).astype(BF16)
-        add(hc, 2, c, [act2_ref[cut:, hc], act_ref[:, hc]], pd_ref, gd_ref, gd_hbm)
-        add(hc, 0, z, [dg2_ref[cut:, hc], dgate], pg_ref, gg_ref, gg_hbm)
-        add(hc, 1, z, [du2_ref[cut:, hc], dup], pu_ref, gu_ref, gu_hbm)
+        add(hc, 2, c, stack(act2_ref[:, hc], act_ref[:, hc]), pd_ref, gd_ref, gd_hbm)
+        add(hc, 0, z, stack(dg2_ref[:, hc], da * p_ref[:, hc].astype(F32)), pg_ref, gg_ref, gg_hbm)
+        add(hc, 1, z, stack(du2_ref[:, hc], da * q_ref[:, hc].astype(F32)), pu_ref, gu_ref, gu_hbm)
 
     staggered(parts, ahead, use)
     for copy in copies:
@@ -200,7 +203,11 @@
 
 
 PARAMS = pltpu.CompilerParams(vmem_limit_bytes=20 * 1024 * 1024)
-COST = pl.CostEstimate(flops=10**10, bytes_accessed=3 * 10**7, transcendentals=0)
+COSTS = {}
+
+
+def cost(name):
+    return pl.CostEstimate(flops=COSTS.get(name, 10**10), bytes_accessed=3 * 10**7, transcendentals=0)
 
 
 def in_vmem(x):
@@ -215,7 +222,7 @@
         out_specs=[spec] * len(out_shapes),
         out_shape=[pltpu.VMEM(s, BF16) for s in out_shapes],
         compiler_params=PARAMS,
-        cost_estimate=COST,
+        cost_estimate=cost(name),
         name=name,
     )(*(in_vmem(a) for a in args))
 
@@ -237,26 +244,26 @@
         out_shape=[pltpu.VMEM(s, BF16) for s in shapes],
         scratch_shapes=[pltpu.SemaphoreType.DMA((1 + 3 * len(chunks(h)),))],
         compiler_params=PARAMS,
-        cost_estimate=COST,
+        cost_estimate=cost(name),
         name=name,
     )(*(pltpu.with_memory_space_constraint(a, pltpu.HBM) for a in (x, *w)))
 
 
-def second(v, c, w, name):
+def second(v, c, w):
     d, t = v.shape
     h = w[0].shape[1]
-    return whole(second_kernel, (v, c, *w), [(d, t), (d, t), (t, h), (t, h), (t, h)], name)
+    return whole(second_kernel, (v, c, *w), [(d, t), (d, t), (t, h), (t, h), (t, h)], "second_own")
+
+
+def second_grads(v, c, w, own):
+    d, h = w[0].shape
+    return whole(second_grads_kernel, (v, c, *w, *own), [(d, h)] * 3, "second_grads")
 
 
 def first_back(x, c, p, q, w, name):
     d, t = x.shape
     h = w[0].shape[1]
     return whole(first_back_kernel, (x, c, p, q, *w), [(d, t), (t, h), (t, h)], name)
-
-
-def partial(zs, cs, acts, dgs, dus):
-    d, h = zs[0].shape[0], acts[0].shape[1]
-    return whole(partial_kernel, (*zs, *cs, *acts, *dgs, *dus), [(d, h)] * 3, "partial")
 
 
 def final(c, z, act, p, q, down, parts, dx, held):
@@ -270,7 +277,7 @@
         out_shape=[pltpu.HBM(s, BF16) for s in ((d, h), (d, h), (d, h), (d, t))],
         scratch_shapes=[pltpu.VMEM((d, h), BF16)] * 3 + [pltpu.SemaphoreType.DMA((1 + 3 * len(chunks(h)),))],
         compiler_params=PARAMS,
-        cost_estimate=COST,
+        cost_estimate=cost("final"),
         name="final",
     )(*(in_vmem(a) for a in args))
 
@@ -285,12 +292,11 @@
     x_o = after(x_o, g_b)
     h_o, z3, act3, p3, q3 = first(x_o, w, "first_other")
     h_bo = shift(h_o, -1)
-    d_b, z0, act0, dg0, du0 = second(after(h_b, h_o), g_b, w, "second_own")
+    d_b, z0, act0, dg0, du0 = second(after(h_b, h_o), g_b, w)
     d = shift(d_b, 1)
-    d_bo, z1, act1, dg1, du1 = second(after(h_bo, d_b), g_bo, w, "second_other")
-    d_o = shift(d_bo, 1)
-    dx, dg2, du2 = first_back(x, after(d, d_bo), p2, q2, w, "first_back_own")
-    parts = partial((z0, z1, z2), (g_b, g_bo, d), (act0, act1, act2), (dg0, dg1, dg2), (du0, du1, du2))
+    d_o = shift(d_b, 1, True)
+    parts = second_grads(after(h_bo, d_b), g_bo, w, (z0, g_b, act0, dg0, du0))
+    dx, dg2, du2 = first_back(x, after(d, parts[0]), p2, q2, w, "first_back_own")
     gg, gu, gd, dx = final(d_o, z3, act3, p3, q3, w[2], parts, dx, (d, z2, act2, dg2, du2))
     return dx.T[None], gg[None], gu[None], gd.T[None]
 

time: 52 us -> 49.4 us (0.950)
  Pallas kernels: 33.4 us -> 31.2 us
    pallas_call x5 -> x4, Pallas kernels: 22.8 us -> 19.2 us  [whole(): pl.pallas_call(kernel, in_specs=[spec] * len(args), out_specs=[spec] * le...]
    pallas_call x1, Pallas kernels: 4.9 us -> 6.23 us  [final(): pl.pallas_call(final_kernel, in_specs=[pl.BlockSpec(memory_space=pltpu.VM...]
  transfers between devices with their start and end apart: 7 -> 7, of which waited for: 2 -> 3; matrix products, arithmetic and copies ran while one was open for 0% -> 0% of each run, Pallas kernels for 55% -> 51%
where the time goes in v6:
time: 49.4 us; the launch traced here: 49.3 us
  Pallas kernels  31.2 us (63%)
  starting transfers between devices  12.5 us (25%)
  waiting for transfers between devices  4.68 us (9%)
  between operations  0.85 us (2%)
    pallas_call x4, Pallas kernels, whole(): pl.pallas_call(kernel, in_specs=[spec] * len(args), out_specs=[spec] * le...  19.2 us
    ppermute x7, starting transfers between devices, shift(): return lax.ppermute(x, ('blk', 'dp'), pairs)  12.5 us
    pallas_call x1, Pallas kernels, final(): pl.pallas_call(final_kernel, in_specs=[pl.BlockSpec(memory_space=pltpu.VM...  6.23 us
    pallas_call x1, Pallas kernels, loading_first(): pl.pallas_call(loading_forward_kernel, in_specs=[pl.BlockSpec(memory_spac...  5.76 us
    ppermute x7, waiting for transfers between devices, shift(): return lax.ppermute(x, ('blk', 'dp'), pairs)  4.68 us
  transfers between devices with their start and end apart: 7, of which 3 were waited for; matrix products, arithmetic and copies ran while one was open for 0% of the time, Pallas kernels for 51%

profile of v6, /device:TPU:0, one launch (start us, length us, event | category | flops | bytes accessed | tf_op | source)
XLA Modules:
  0.0 49.3 jit_solution(3866650655031502608)
XLA Ops:
  0.6 3.0 %collective-permute-start.1 = (bf16[576,384]{1,0:T(8,128)(2,1)}, bf16[576,384]{1,0:T(8,128)(2,1)S(1)}, u32[]{:S(2)}, u32[]{:S(2)}) collective-permute-start(bf16[576,384]{1,0:T(8,128)(2,1)} %bitcast.22), channel_id=1, source_target_pairs={{0,1},{1,0},{2,3},{3,2},{4,5},{5,4},{6,7},{7,6},{8,9},{9,8},{10,11... | collective-permute-start | bytes 1327112 | tf_op jit(solution)/shard_map/ppermute | solution.py:22
  3.6 3.7 %collective-permute-start.2 = (bf16[576,384]{1,0:T(8,128)(2,1)}, bf16[576,384]{1,0:T(8,128)(2,1)S(1)}, u32[]{:S(2)}, u32[]{:S(2)}) collective-permute-start(bf16[576,384]{1,0:T(8,128)(2,1)} %bitcast.24), channel_id=1, source_target_pairs={{0,30},{1,31},{2,0},{3,1},{4,2},{5,3},{6,4},{7,5},{8,6},{9,7},{10,... | collective-permute-start | bytes 1327112 | tf_op jit(solution)/shard_map/ppermute | solution.py:22
  7.4 5.8 %first_own.1 = (bf16[576,384]{1,0:T(8,128)(2,1)S(1)}, bf16[576,384]{1,0:T(8,128)(2,1)S(1)}, bf16[384,1536]{1,0:T(8,128)(2,1)S(1)}, bf16[384,1536]{1,0:T(8,128)(2...) custom-call(bf16[576,384]{1,0:T(8,128)(2,1)} %bitcast.23, ...), custom_call_target="tpu_custom_call" | custom-call | flops 10000000000 | bytes 30000000 | tf_op jit(solution)/shard_map/first_own/pallas_call | solution.py:240
  13.1 1.0 %collective-permute-start = (bf16[576,384]{1,0:T(8,128)(2,1)S(1)}, bf16[576,384]{1,0:T(8,128)(2,1)S(1)}, u32[]{:S(2)}, u32[]{:S(2)}) collective-permute-start(bf16[576,384]{1,0:T(8,128)(2,1)S(1)} %get-tuple-element.38), channel_id=1, source_target_pairs={{0,30},{1,31},{2,0},{3,1},{4,2},{5,3},{6,4},{7,5},{8,6},{9,7},{10,... | collective-permute-start | bytes 1327112 | tf_op jit(solution)/shard_map/ppermute | solution.py:22
  14.1 0.0 collective-permute-done.1.refs_0_
  14.1 0.0 collective-permute-done.2.c_ref.c0_ref
  14.1 1.6 %collective-permute-start.5 = (bf16[576,384]{1,0:T(8,128)(2,1)S(1)}, bf16[576,384]{1,0:T(8,128)(2,1)S(1)}, u32[]{:S(2)}, u32[]{:S(2)}) collective-permute-start(bf16[576,384]{1,0:T(8,128)(2,1)S(1)} %collective-permute-done.2.c_ref.c0_ref), channel_id=1, source_target_pairs={{0,1},{1,0},{2,3},{3,2},{4,5},{5,4},{6,7},{7,6},{8,9},{9,8},{10,11... | collective-permute-start | bytes 1327112 | tf_op jit(solution)/shard_map/ppermute | solution.py:22
  15.8 3.1 %first_other.1 = (bf16[576,384]{1,0:T(8,128)(2,1)S(1)}, bf16[576,384]{1,0:T(8,128)(2,1)S(1)}, bf16[384,1536]{1,0:T(8,128)(2,1)S(1)}, bf16[384,1536]{1,0:T(8,128)(2,1)S(1)}, bf16[384,1536]{1,0:T(8,128)(2,1)S(1)}) custom-call(bf16[576,384]{1,0:T(8,128)(2,1)S(1)} %collective-permute-done.1.refs_0_, bf16[576,1536]{1,0:T(8,128)(2,1)S(1)} %get-tuple-element.40.refs_1_.gate_ref, ...), custom_call_target="tpu_custom_call" | custom-call | flops 10000000000 | bytes 30000000 | tf_op jit(solution)/shard_map/first_other/pallas_call | solution.py:219
  18.9 2.9 %collective-permute-start.4 = (bf16[576,384]{1,0:T(8,128)(2,1)S(1)}, bf16[576,384]{1,0:T(8,128)(2,1)S(1)}, u32[]{:S(2)}, u32[]{:S(2)}) collective-permute-start(bf16[576,384]{1,0:T(8,128)(2,1)S(1)} %get-tuple-element.43), channel_id=1, source_target_pairs={{0,30},{1,31},{2,0},{3,1},{4,2},{5,3},{6,4},{7,5},{8,6},{9,7},{10,... | collective-permute-start | bytes 1327112 | tf_op jit(solution)/shard_map/ppermute | solution.py:22
  21.8 0.0 collective-permute-done.h_ref
  21.8 5.3 %second_own.1 = (bf16[576,384]{1,0:T(8,128)(2,1)S(1)}, bf16[576,384]{1,0:T(8,128)(2,1)S(1)}, bf16[384,1536]{1,0:T(8,128)(2,1)S(1)}, bf16[384,1536]{1,0:T(8,128)(2,1)S(1)}, bf16[384,1536]{1,0:T(8,128)(2,1)S(1)}) custom-call(bf16[576,384]{1,0:T(8,128)(2,1)S(1)} %collective-permute-done.h_ref, bf16[576,384]{1,0:T(8,128)(2,1)S(1)} %collective-permute-done.2.c_ref.c0_ref, ...), custom_call_target="tpu_custom_call" | custom-call | flops 10000000000 | bytes 30000000 | tf_op jit(solution)/shard_map/second_own/pallas_call | solution.py:219
  27.1 0.1 collective-permute-start.6
  27.1 0.2 collective-permute-start.3
  27.4 0.2 collective-permute-done.4.h_ref
  27.6 0.0 collective-permute-done.5.c_ref
  27.6 7.4 %second_grads.1 = (bf16[576,1536]{1,0:T(8,128)(2,1)S(1)}, bf16[576,1536]{1,0:T(8,128)(2,1)S(1)}, bf16[576,1536]{1,0:T(8,128)(2,1)S(1)}) custom-call(bf16[576,384]{1,0:T(8,128)(2,1)S(1)} %collective-permute-done.4.h_ref, bf16[576,384]{1,0:T(8,128)(2,1)S(1)} %collective-permute-done.5.c_ref, bf16[576,1536]{1,0:T(8,128)(2,1)S(1)} %get-tuple-element.40.refs_1_.gate_ref, ...), custom_call_target="tpu_custom_call" | custom-call | flops 10000000000 | bytes 30000000 | tf_op jit(solution)/shard_map/second_grads/pallas_call | solution.py:219
  35.0 2.6 %collective-permute-done.6.c_ref.c2_ref = bf16[576,384]{1,0:T(8,128)(2,1)S(1)} collective-permute-done((bf16[576,384]{1,0:T(8,128)(2,1)S(1)}, bf16[576,384]{1,0:T(8,128)(2,1)S(1)}, u32[]{:S(2)}, u32[]{:S(2)}) %collective-permute-start.6) | collective-permute-done | bytes 442400 | tf_op jit(solution)/shard_map/ppermute | solution.py:22
  37.6 3.4 %first_back_own.1 = (bf16[576,384]{1,0:T(8,128)(2,1)S(1)}, bf16[384,1536]{1,0:T(8,128)(2,1)S(1)}, bf16[384,1536]{1,0:T(8,128)(2,1)S(1)}) custom-call(bf16[576,384]{1,0:T(8,128)(2,1)S(1)} %get-tuple-element.59.x_ref, bf16[576,384]{1,0:T(8,128)(2,1)S(1)} %collective-permute-done.6.c_ref.c2_ref, bf16[384,1536]{1,0:T(8,128)(2,1)S(1)} %get-tuple-element.61.p_ref, ...), custom_call_target="tpu_custom_call" | custom-call | flops 10000000000 | bytes 30000000 | tf_op jit(solution)/shard_map/first_back_own/pallas_call | solution.py:219
  41.0 1.9 %collective-permute-done.3.c_ref = bf16[576,384]{1,0:T(8,128)(2,1)S(1)} collective-permute-done((bf16[576,384]{1,0:T(8,128)(2,1)S(1)}, bf16[576,384]{1,0:T(8,128)(2,1)S(1)}, u32[]{:S(2)}, u32[]{:S(2)}) %collective-permute-start.3) | collective-permute-done | bytes 442400 | tf_op jit(solution)/shard_map/ppermute | solution.py:22
  42.9 6.2 %final.1 = (bf16[576,1536]{1,0:T(8,128)(2,1)}, bf16[576,1536]{1,0:T(8,128)(2,1)}, bf16[576,1536]{1,0:T(8,128)(2,1)}, bf16[576,384]{1,0:T(8,128)(2,1)}) custom-call(bf16[576,384]{1,0:T(8,128)(2,1)S(1)} %collective-permute-done.3.c_ref, bf16[576,384]{1,0:T(8,128)(2,1)S(1)} %get-tuple-element.46.z_ref, bf16[384,1536]{1,0:T(8,128)(2,1)S(1)} %get-tuple-element.47.act_ref, ...), custom_call_target="tpu_custom_call" | custom-call | flops 10000000000 | bytes 30000000 | tf_op jit(solution)/shard_map/final/pallas_call | solution.py:273
Async XLA Ops:
  0.6 13.5 %collective-permute-start.1 = (bf16[576,384]{1,0:T(8,128)(2,1)}, bf16[576,384]{1,0:T(8,128)(2,1)S(1)}, u32[]{:S(2)}, u32[]{:S(2)}) collective-permute-start(bf16[576,384]{1,0:T(8,128)(2,1)} %bitcast.22), channel_id=1, source_target_pairs={{0,1},{1,0},{2,3},{3,2},{4,5},{5,4},{6,7},{7,6},{8,9},{9,8},{10,11... | collective-permute-start | bytes 1327112 | tf_op jit(solution)/shard_map/ppermute | solution.py:22
  3.6 10.5 %collective-permute-start.2 = (bf16[576,384]{1,0:T(8,128)(2,1)}, bf16[576,384]{1,0:T(8,128)(2,1)S(1)}, u32[]{:S(2)}, u32[]{:S(2)}) collective-permute-start(bf16[576,384]{1,0:T(8,128)(2,1)} %bitcast.24), channel_id=1, source_target_pairs={{0,30},{1,31},{2,0},{3,1},{4,2},{5,3},{6,4},{7,5},{8,6},{9,7},{10,... | collective-permute-start | bytes 1327112 | tf_op jit(solution)/shard_map/ppermute | solution.py:22
  13.1 8.7 %collective-permute-start = (bf16[576,384]{1,0:T(8,128)(2,1)S(1)}, bf16[576,384]{1,0:T(8,128)(2,1)S(1)}, u32[]{:S(2)}, u32[]{:S(2)}) collective-permute-start(bf16[576,384]{1,0:T(8,128)(2,1)S(1)} %get-tuple-element.38), channel_id=1, source_target_pairs={{0,30},{1,31},{2,0},{3,1},{4,2},{5,3},{6,4},{7,5},{8,6},{9,7},{10,... | collective-permute-start | bytes 1327112 | tf_op jit(solution)/shard_map/ppermute | solution.py:22
  14.1 13.5 %collective-permute-start.5 = (bf16[576,384]{1,0:T(8,128)(2,1)S(1)}, bf16[576,384]{1,0:T(8,128)(2,1)S(1)}, u32[]{:S(2)}, u32[]{:S(2)}) collective-permute-start(bf16[576,384]{1,0:T(8,128)(2,1)S(1)} %collective-permute-done.2.c_ref.c0_ref), channel_id=1, source_target_pairs={{0,1},{1,0},{2,3},{3,2},{4,5},{5,4},{6,7},{7,6},{8,9},{9,8},{10,11... | collective-permute-start | bytes 1327112 | tf_op jit(solution)/shard_map/ppermute | solution.py:22
  18.9 8.7 %collective-permute-start.4 = (bf16[576,384]{1,0:T(8,128)(2,1)S(1)}, bf16[576,384]{1,0:T(8,128)(2,1)S(1)}, u32[]{:S(2)}, u32[]{:S(2)}) collective-permute-start(bf16[576,384]{1,0:T(8,128)(2,1)S(1)} %get-tuple-element.43), channel_id=1, source_target_pairs={{0,30},{1,31},{2,0},{3,1},{4,2},{5,3},{6,4},{7,5},{8,6},{9,7},{10,... | collective-permute-start | bytes 1327112 | tf_op jit(solution)/shard_map/ppermute | solution.py:22
  27.1 10.5 %collective-permute-start.6 = (bf16[576,384]{1,0:T(8,128)(2,1)S(1)}, bf16[576,384]{1,0:T(8,128)(2,1)S(1)}, u32[]{:S(2)}, u32[]{:S(2)}) collective-permute-start(bf16[576,384]{1,0:T(8,128)(2,1)S(1)} %get-tuple-element.45), channel_id=1, source_target_pairs={{0,2},{1,3},{2,4},{3,5},{4,6},{5,7},{6,8},{7,9},{8,10},{9,11},{10,... | collective-permute-start | bytes 1327112 | tf_op jit(solution)/shard_map/ppermute | solution.py:22
  27.1 15.7 %collective-permute-start.3 = (bf16[576,384]{1,0:T(8,128)(2,1)S(1)}, bf16[576,384]{1,0:T(8,128)(2,1)S(1)}, u32[]{:S(2)}, u32[]{:S(2)}) collective-permute-start(bf16[576,384]{1,0:T(8,128)(2,1)S(1)} %get-tuple-element.45), channel_id=1, source_target_pairs={{0,3},{1,2},{2,5},{3,4},{4,7},{5,6},{6,9},{7,8},{8,11},{9,10},{10,... | collective-permute-start | bytes 1327112 | tf_op jit(solution)/shard_map/ppermute | solution.py:22

commit v7 on v6

--- a/solution.py
+++ b/solution.py
@@ -74,14 +74,18 @@
         arrived(hc)
         return dot(zt, gate_ref[:, hc]), dot(zt, up_ref[:, hc])
 
+    total = [x]
+
     def use(hc, ready):
         active, p, q = gate_values(*ready)
-        act_ref[:, hc] = active.astype(BF16)
+        active = active.astype(BF16)
+        act_ref[:, hc] = active
         p_ref[:, hc] = p.astype(BF16)
         q_ref[:, hc] = q.astype(BF16)
+        total[0] += dot(down_ref[:, hc], active, NT)
 
     staggered(chunks(gate_ref.shape[1]), ahead, use)
-    h_ref[...] = (x + dot(down_ref[...], act_ref[...], NT)).astype(BF16)
+    h_ref[...] = total[0].astype(BF16)
 
 
 def forward_kernel(*refs):
@@ -109,21 +113,26 @@
     forward_body(x_ref, gate_ref, up_ref, down_ref, h_ref, z_ref, act_ref, p_ref, q_ref, arrived)
 
 
-def second_kernel(h_ref, c_ref, gate_ref, up_ref, down_ref, d_ref, z_ref, act_ref, dg_ref, du_ref):
+def hidden_cotangent_kernel(c_ref, down_ref, da_ref):
+    ct = c_ref[...].T
+    for hc in chunks(down_ref.shape[1]):
+        da_ref[:, hc] = dot(ct, down_ref[:, hc])
+
+
+def second_kernel(h_ref, c_ref, gate_ref, up_ref, da_ref, d_ref, z_ref, act_ref, dg_ref, du_ref):
     inverse, normed = normalize(h_ref[...].astype(F32))
     zed = normed.astype(BF16)
     z_ref[...] = zed
     zt = zed.T
-    ct = c_ref[...].T
-
-    def ahead(hc):
-        return dot(zt, gate_ref[:, hc]), dot(zt, up_ref[:, hc]), dot(ct, down_ref[:, hc])
+
+    def ahead(hc):
+        return dot(zt, gate_ref[:, hc]), dot(zt, up_ref[:, hc])
 
     def use(hc, ready):
-        active, p, q = gate_values(*ready[:2])
+        active, p, q = gate_values(*ready)
         act_ref[:, hc] = active.astype(BF16)
-        dg_ref[:, hc] = (ready[2] * p).astype(BF16)
-        du_ref[:, hc] = (ready[2] * q).astype(BF16)
+        dg_ref[:, hc] = (da_ref[:, hc] * p).astype(BF16)
+        du_ref[:, hc] = (da_ref[:, hc] * q).astype(BF16)
 
     staggered(chunks(gate_ref.shape[1]), ahead, use)
     dz = dot(gate_ref[...], dg_ref[...], NT) + dot(up_ref[...], du_ref[...], NT)
@@ -214,13 +223,13 @@
     return pltpu.with_memory_space_constraint(x, pltpu.VMEM)
 
 
-def whole(kernel, args, out_shapes, name):
+def whole(kernel, args, out_shapes, name, kind=BF16):
     spec = pl.BlockSpec(memory_space=pltpu.VMEM)
     return pl.pallas_call(
         kernel,
         in_specs=[spec] * len(args),
         out_specs=[spec] * len(out_shapes),
-        out_shape=[pltpu.VMEM(s, BF16) for s in out_shapes],
+        out_shape=[pltpu.VMEM(s, kind) for s in out_shapes],
         compiler_params=PARAMS,
         cost_estimate=cost(name),
         name=name,
@@ -249,10 +258,14 @@
     )(*(pltpu.with_memory_space_constraint(a, pltpu.HBM) for a in (x, *w)))
 
 
-def second(v, c, w):
+def hidden_cotangent(c, down):
+    return whole(hidden_cotangent_kernel, (c, down), [(c.shape[1], down.shape[1])], "hidden_cotangent", F32)[0]
+
+
+def second(v, c, gate, up, da):
     d, t = v.shape
-    h = w[0].shape[1]
-    return whole(second_kernel, (v, c, *w), [(d, t), (d, t), (t, h), (t, h), (t, h)], "second_own")
+    h = gate.shape[1]
+    return whole(second_kernel, (v, c, gate, up, da), [(d, t), (d, t), (t, h), (t, h), (t, h)], "second_own")
 
 
 def second_grads(v, c, w, own):
@@ -289,10 +302,11 @@
     h, z2, act2, p2, q2, x, *w = loading_first(x, (w_gate[0], w_up[0], w_down[0].T), "first_own")
     h_b = shift(h, -1)
     g_bo = shift(after(g_b, h), 0, True)
-    x_o = after(x_o, g_b)
+    da_b = hidden_cotangent(after(g_b, h), w[2])
+    x_o = after(x_o, da_b)
     h_o, z3, act3, p3, q3 = first(x_o, w, "first_other")
     h_bo = shift(h_o, -1)
-    d_b, z0, act0, dg0, du0 = second(after(h_b, h_o), g_b, w)
+    d_b, z0, act0, dg0, du0 = second(after(h_b, h_o), g_b, w[0], w[1], da_b)
     d = shift(d_b, 1)
     d_o = shift(d_b, 1, True)
     parts = second_grads(after(h_bo, d_b), g_bo, w, (z0, g_b, act0, dg0, du0))

time: 49.4 us -> 49.7 us (level)
  waiting for transfers between devices: 4.68 us -> 5.3 us
  Pallas kernels: 31.2 us -> 30.6 us
    pallas_call x1, Pallas kernels: 5.76 us -> 4.86 us  [loading_first(): pl.pallas_call(loading_forward_kernel, in_specs=[pl.BlockSpec(memory_spac...]
    ppermute x7, waiting for transfers between devices: 4.68 us -> 5.3 us  [shift(): return lax.ppermute(x, ('blk', 'dp'), pairs)]
    pallas_call x4 -> x5, Pallas kernels: 19.2 us -> 19.5 us  [whole(): pl.pallas_call(kernel, in_specs=[spec] * len(args), out_specs=[spec] * le...]
  transfers between devices with their start and end apart: 7 -> 7, of which waited for: 3 -> 4; matrix products, arithmetic and copies ran while one was open for 0% -> 0% of each run, Pallas kernels for 51% -> 49%
where the time goes in v7:
time: 49.7 us; the launch traced here: 49.6 us
  Pallas kernels  30.6 us (62%)
  starting transfers between devices  12.8 us (26%)
  waiting for transfers between devices  5.3 us (11%)
  between operations  0.86 us (2%)
    pallas_call x5, Pallas kernels, whole(): pl.pallas_call(kernel, in_specs=[spec] * len(args), out_specs=[spec] * le...  19.5 us
    ppermute x7, starting transfers between devices, shift(): return lax.ppermute(x, ('blk', 'dp'), pairs)  12.8 us
    pallas_call x1, Pallas kernels, final(): pl.pallas_call(final_kernel, in_specs=[pl.BlockSpec(memory_space=pltpu.VM...  6.23 us
    ppermute x7, waiting for transfers between devices, shift(): return lax.ppermute(x, ('blk', 'dp'), pairs)  5.3 us
    pallas_call x1, Pallas kernels, loading_first(): pl.pallas_call(loading_forward_kernel, in_specs=[pl.BlockSpec(memory_spac...  4.86 us
  transfers between devices with their start and end apart: 7, of which 4 were waited for; matrix products, arithmetic and copies ran while one was open for 0% of the time, Pallas kernels for 49%

profile of v7, /device:TPU:0, one launch (start us, length us, event | category | flops | bytes accessed | tf_op | source)
XLA Modules:
  0.0 49.6 jit_solution(11694958359266658682)
XLA Ops:
  0.6 3.0 %collective-permute-start.1 = (bf16[576,384]{1,0:T(8,128)(2,1)}, bf16[576,384]{1,0:T(8,128)(2,1)S(1)}, u32[]{:S(2)}, u32[]{:S(2)}) collective-permute-start(bf16[576,384]{1,0:T(8,128)(2,1)} %bitcast.23), channel_id=1, source_target_pairs={{0,1},{1,0},{2,3},{3,2},{4,5},{5,4},{6,7},{7,6},{8,9},{9,8},{10,11... | collective-permute-start | bytes 1327112 | tf_op jit(solution)/shard_map/ppermute | solution.py:22
  3.6 3.7 %collective-permute-start.2 = (bf16[576,384]{1,0:T(8,128)(2,1)}, bf16[576,384]{1,0:T(8,128)(2,1)S(1)}, u32[]{:S(2)}, u32[]{:S(2)}) collective-permute-start(bf16[576,384]{1,0:T(8,128)(2,1)} %bitcast.22), channel_id=1, source_target_pairs={{0,30},{1,31},{2,0},{3,1},{4,2},{5,3},{6,4},{7,5},{8,6},{9,7},{10,... | collective-permute-start | bytes 1327112 | tf_op jit(solution)/shard_map/ppermute | solution.py:22
  7.4 4.9 %first_own.1 = (bf16[576,384]{1,0:T(8,128)(2,1)S(1)}, bf16[576,384]{1,0:T(8,128)(2,1)S(1)}, bf16[384,1536]{1,0:T(8,128)(2,1)S(1)}, bf16[384,1536]{1,0:T(8,128)(2...) custom-call(bf16[576,384]{1,0:T(8,128)(2,1)} %bitcast.24, ...), custom_call_target="tpu_custom_call" | custom-call | flops 10000000000 | bytes 30000000 | tf_op jit(solution)/shard_map/first_own/pallas_call | solution.py:249
  12.2 1.0 %collective-permute-start = (bf16[576,384]{1,0:T(8,128)(2,1)S(1)}, bf16[576,384]{1,0:T(8,128)(2,1)S(1)}, u32[]{:S(2)}, u32[]{:S(2)}) collective-permute-start(bf16[576,384]{1,0:T(8,128)(2,1)S(1)} %get-tuple-element.38), channel_id=1, source_target_pairs={{0,30},{1,31},{2,0},{3,1},{4,2},{5,3},{6,4},{7,5},{8,6},{9,7},{10,... | collective-permute-start | bytes 1327112 | tf_op jit(solution)/shard_map/ppermute | solution.py:22
  13.2 0.3 collective-permute-done.2.c_ref.c0_ref
  13.5 0.5 %collective-permute-start.5 = (bf16[576,384]{1,0:T(8,128)(2,1)S(1)}, bf16[576,384]{1,0:T(8,128)(2,1)S(1)}, u32[]{:S(2)}, u32[]{:S(2)}) collective-permute-start(bf16[576,384]{1,0:T(8,128)(2,1)S(1)} %collective-permute-done.2.c_ref.c0_ref), channel_id=1, source_target_pairs={{0,1},{1,0},{2,3},{3,2},{4,5},{5,4},{6,7},{7,6},{8,9},{9,8},{10,11... | collective-permute-start | bytes 1327112 | tf_op jit(solution)/shard_map/ppermute | solution.py:22
  14.0 1.1 %hidden_cotangent.1.da_ref = f32[384,1536]{1,0:T(8,128)S(1)} custom-call(bf16[576,384]{1,0:T(8,128)(2,1)S(1)} %collective-permute-done.2.c_ref.c0_ref, bf16[576,1536]{1,0:T(8,128)(2,1)S(1)} %get-tuple-element.40.down_ref.refs_3_), custom_call_target="tpu_custom_call" | custom-call | flops 10000000000 | bytes 30000000 | tf_op jit(solution)/shard_map/hidden_cotangent/pallas_call | solution.py:228
  15.1 0.0 collective-permute-done.1.refs_0_
  15.1 3.2 %first_other.1 = (bf16[576,384]{1,0:T(8,128)(2,1)S(1)}, bf16[576,384]{1,0:T(8,128)(2,1)S(1)}, bf16[384,1536]{1,0:T(8,128)(2,1)S(1)}, bf16[384,1536]{1,0:T(8,128)(2,1)S(1)}, bf16[384,1536]{1,0:T(8,128)(2,1)S(1)}) custom-call(bf16[576,384]{1,0:T(8,128)(2,1)S(1)} %collective-permute-done.1.refs_0_, bf16[576,1536]{1,0:T(8,128)(2,1)S(1)} %get-tuple-element.42.refs_1_.gate_ref, ...), custom_call_target="tpu_custom_call" | custom-call | flops 10000000000 | bytes 30000000 | tf_op jit(solution)/shard_map/first_other/pallas_call | solution.py:228
  18.3 4.3 %collective-permute-start.4 = (bf16[576,384]{1,0:T(8,128)(2,1)S(1)}, bf16[576,384]{1,0:T(8,128)(2,1)S(1)}, u32[]{:S(2)}, u32[]{:S(2)}) collective-permute-start(bf16[576,384]{1,0:T(8,128)(2,1)S(1)} %get-tuple-element.44), channel_id=1, source_target_pairs={{0,30},{1,31},{2,0},{3,1},{4,2},{5,3},{6,4},{7,5},{8,6},{9,7},{10,... | collective-permute-start | bytes 1327112 | tf_op jit(solution)/shard_map/ppermute | solution.py:22
  22.6 0.0 collective-permute-done.h_ref
  22.6 4.4 %second_own.1 = (bf16[576,384]{1,0:T(8,128)(2,1)S(1)}, bf16[576,384]{1,0:T(8,128)(2,1)S(1)}, bf16[384,1536]{1,0:T(8,128)(2,1)S(1)}, bf16[384,1536]{1,0:T(8,128)(2,1)S(1)}, bf16[384,1536]{1,0:T(8,128)(2,1)S(1)}) custom-call(bf16[576,384]{1,0:T(8,128)(2,1)S(1)} %collective-permute-done.h_ref, bf16[576,384]{1,0:T(8,128)(2,1)S(1)} %collective-permute-done.2.c_ref.c0_ref, ...), custom_call_target="tpu_custom_call" | custom-call | flops 10000000000 | bytes 30000000 | tf_op jit(solution)/shard_map/second_own/pallas_call | solution.py:228
  27.0 0.1 collective-permute-start.6
  27.1 0.2 collective-permute-start.3
  27.3 1.1 %collective-permute-done.4.h_ref = bf16[576,384]{1,0:T(8,128)(2,1)S(1)} collective-permute-done((bf16[576,384]{1,0:T(8,128)(2,1)S(1)}, bf16[576,384]{1,0:T(8,128)(2,1)S(1)}, u32[]{:S(2)}, u32[]{:S(2)}) %collective-permute-start.4) | collective-permute-done | bytes 442400 | tf_op jit(solution)/shard_map/ppermute | solution.py:22
  28.4 0.0 collective-permute-done.5.c_ref
  28.4 7.4 %second_grads.1 = (bf16[576,1536]{1,0:T(8,128)(2,1)S(1)}, bf16[576,1536]{1,0:T(8,128)(2,1)S(1)}, bf16[576,1536]{1,0:T(8,128)(2,1)S(1)}) custom-call(bf16[576,384]{1,0:T(8,128)(2,1)S(1)} %collective-permute-done.4.h_ref, bf16[576,384]{1,0:T(8,128)(2,1)S(1)} %collective-permute-done.5.c_ref, bf16[576,1536]{1,0:T(8,128)(2,1)S(1)} %get-tuple-element.42.refs_1_.gate_ref, ...), custom_call_target="tpu_custom_call" | custom-call | flops 10000000000 | bytes 30000000 | tf_op jit(solution)/shard_map/second_grads/pallas_call | solution.py:228
  35.8 1.7 %collective-permute-done.6.c_ref.c2_ref = bf16[576,384]{1,0:T(8,128)(2,1)S(1)} collective-permute-done((bf16[576,384]{1,0:T(8,128)(2,1)S(1)}, bf16[576,384]{1,0:T(8,128)(2,1)S(1)}, u32[]{:S(2)}, u32[]{:S(2)}) %collective-permute-start.6) | collective-permute-done | bytes 442400 | tf_op jit(solution)/shard_map/ppermute | solution.py:22
  37.5 3.4 %first_back_own.1 = (bf16[576,384]{1,0:T(8,128)(2,1)S(1)}, bf16[384,1536]{1,0:T(8,128)(2,1)S(1)}, bf16[384,1536]{1,0:T(8,128)(2,1)S(1)}) custom-call(bf16[576,384]{1,0:T(8,128)(2,1)S(1)} %get-tuple-element.59.x_ref, bf16[576,384]{1,0:T(8,128)(2,1)S(1)} %collective-permute-done.6.c_ref.c2_ref, bf16[384,1536]{1,0:T(8,128)(2,1)S(1)} %get-tuple-element.61.p_ref, ...), custom_call_target="tpu_custom_call" | custom-call | flops 10000000000 | bytes 30000000 | tf_op jit(solution)/shard_map/first_back_own/pallas_call | solution.py:228
  40.9 2.2 %collective-permute-done.3.c_ref = bf16[576,384]{1,0:T(8,128)(2,1)S(1)} collective-permute-done((bf16[576,384]{1,0:T(8,128)(2,1)S(1)}, bf16[576,384]{1,0:T(8,128)(2,1)S(1)}, u32[]{:S(2)}, u32[]{:S(2)}) %collective-permute-start.3) | collective-permute-done | bytes 442400 | tf_op jit(solution)/shard_map/ppermute | solution.py:22
  43.2 6.2 %final.1 = (bf16[576,1536]{1,0:T(8,128)(2,1)}, bf16[576,1536]{1,0:T(8,128)(2,1)}, bf16[576,1536]{1,0:T(8,128)(2,1)}, bf16[576,384]{1,0:T(8,128)(2,1)}) custom-call(bf16[576,384]{1,0:T(8,128)(2,1)S(1)} %collective-permute-done.3.c_ref, bf16[576,384]{1,0:T(8,128)(2,1)S(1)} %get-tuple-element.47.z_ref, bf16[384,1536]{1,0:T(8,128)(2,1)S(1)} %get-tuple-element.48.act_ref, ...), custom_call_target="tpu_custom_call" | custom-call | flops 10000000000 | bytes 30000000 | tf_op jit(solution)/shard_map/final/pallas_call | solution.py:286
Async XLA Ops:
  0.6 14.5 %collective-permute-start.1 = (bf16[576,384]{1,0:T(8,128)(2,1)}, bf16[576,384]{1,0:T(8,128)(2,1)S(1)}, u32[]{:S(2)}, u32[]{:S(2)}) collective-permute-start(bf16[576,384]{1,0:T(8,128)(2,1)} %bitcast.23), channel_id=1, source_target_pairs={{0,1},{1,0},{2,3},{3,2},{4,5},{5,4},{6,7},{7,6},{8,9},{9,8},{10,11... | collective-permute-start | bytes 1327112 | tf_op jit(solution)/shard_map/ppermute | solution.py:22
  3.6 9.9 %collective-permute-start.2 = (bf16[576,384]{1,0:T(8,128)(2,1)}, bf16[576,384]{1,0:T(8,128)(2,1)S(1)}, u32[]{:S(2)}, u32[]{:S(2)}) collective-permute-start(bf16[576,384]{1,0:T(8,128)(2,1)} %bitcast.22), channel_id=1, source_target_pairs={{0,30},{1,31},{2,0},{3,1},{4,2},{5,3},{6,4},{7,5},{8,6},{9,7},{10,... | collective-permute-start | bytes 1327112 | tf_op jit(solution)/shard_map/ppermute | solution.py:22
  12.2 10.4 %collective-permute-start = (bf16[576,384]{1,0:T(8,128)(2,1)S(1)}, bf16[576,384]{1,0:T(8,128)(2,1)S(1)}, u32[]{:S(2)}, u32[]{:S(2)}) collective-permute-start(bf16[576,384]{1,0:T(8,128)(2,1)S(1)} %get-tuple-element.38), channel_id=1, source_target_pairs={{0,30},{1,31},{2,0},{3,1},{4,2},{5,3},{6,4},{7,5},{8,6},{9,7},{10,... | collective-permute-start | bytes 1327112 | tf_op jit(solution)/shard_map/ppermute | solution.py:22
  13.5 14.9 %collective-permute-start.5 = (bf16[576,384]{1,0:T(8,128)(2,1)S(1)}, bf16[576,384]{1,0:T(8,128)(2,1)S(1)}, u32[]{:S(2)}, u32[]{:S(2)}) collective-permute-start(bf16[576,384]{1,0:T(8,128)(2,1)S(1)} %collective-permute-done.2.c_ref.c0_ref), channel_id=1, source_target_pairs={{0,1},{1,0},{2,3},{3,2},{4,5},{5,4},{6,7},{7,6},{8,9},{9,8},{10,11... | collective-permute-start | bytes 1327112 | tf_op jit(solution)/shard_map/ppermute | solution.py:22
  18.3 10.1 %collective-permute-start.4 = (bf16[576,384]{1,0:T(8,128)(2,1)S(1)}, bf16[576,384]{1,0:T(8,128)(2,1)S(1)}, u32[]{:S(2)}, u32[]{:S(2)}) collective-permute-start(bf16[576,384]{1,0:T(8,128)(2,1)S(1)} %get-tuple-element.44), channel_id=1, source_target_pairs={{0,30},{1,31},{2,0},{3,1},{4,2},{5,3},{6,4},{7,5},{8,6},{9,7},{10,... | collective-permute-start | bytes 1327112 | tf_op jit(solution)/shard_map/ppermute | solution.py:22
  27.0 10.5 %collective-permute-start.6 = (bf16[576,384]{1,0:T(8,128)(2,1)S(1)}, bf16[576,384]{1,0:T(8,128)(2,1)S(1)}, u32[]{:S(2)}, u32[]{:S(2)}) collective-permute-start(bf16[576,384]{1,0:T(8,128)(2,1)S(1)} %get-tuple-element.46), channel_id=1, source_target_pairs={{0,2},{1,3},{2,4},{3,5},{4,6},{5,7},{6,8},{7,9},{8,10},{9,11},{10,... | collective-permute-start | bytes 1327112 | tf_op jit(solution)/shard_map/ppermute | solution.py:22
  27.1 16.1 %collective-permute-start.3 = (bf16[576,384]{1,0:T(8,128)(2,1)S(1)}, bf16[576,384]{1,0:T(8,128)(2,1)S(1)}, u32[]{:S(2)}, u32[]{:S(2)}) collective-permute-start(bf16[576,384]{1,0:T(8,128)(2,1)S(1)} %get-tuple-element.46), channel_id=1, source_target_pairs={{0,3},{1,2},{2,5},{3,4},{4,7},{5,6},{6,9},{7,8},{8,11},{9,10},{10,... | collective-permute-start | bytes 1327112 | tf_op jit(solution)/shard_map/ppermute | solution.py:22

commit v8 on v7

--- a/solution.py
+++ b/solution.py
@@ -165,16 +165,31 @@
     return jnp.concatenate([above, below.astype(BF16)], axis=0)
 
 
-def first_back_kernel(x_ref, c_ref, p_ref, q_ref, gate_ref, up_ref, down_ref, d_ref, dg_ref, du_ref):
+def whole_tiles(tokens):
+    return tokens // 256 * 256 if tokens > 256 else tokens
+
+
+def first_back_kernel(
+    x_ref, c_ref, p_ref, q_ref, gate_ref, up_ref, down_ref, z_ref, act_ref, pg_ref, pu_ref, pd_ref,
+    d_ref, dg_ref, du_ref, gg_ref, gu_ref, gd_ref,
+):
     inverse, normed = normalize(x_ref[...].astype(F32))
     ct = c_ref[...].T
+    cut = whole_tiles(act_ref.shape[0])
+    c = c_ref[:, :cut]
+    z = z_ref[:, :cut]
 
     def ahead(hc):
         return dot(ct, down_ref[:, hc])
 
     def use(hc, da):
-        dg_ref[:, hc] = (da * p_ref[:, hc].astype(F32)).astype(BF16)
-        du_ref[:, hc] = (da * q_ref[:, hc].astype(F32)).astype(BF16)
+        dgate = (da * p_ref[:, hc].astype(F32)).astype(BF16)
+        dup = (da * q_ref[:, hc].astype(F32)).astype(BF16)
+        dg_ref[:, hc] = dgate
+        du_ref[:, hc] = dup
+        gd_ref[:, hc] = (pd_ref[:, hc].astype(F32) + dot(c, act_ref[:cut, hc])).astype(BF16)
+        gg_ref[:, hc] = (pg_ref[:, hc].astype(F32) + dot(z, dgate[:cut])).astype(BF16)
+        gu_ref[:, hc] = (pu_ref[:, hc].astype(F32) + dot(z, dup[:cut])).astype(BF16)
 
     staggered(chunks(gate_ref.shape[1]), ahead, use)
     dz = dot(gate_ref[...], dg_ref[...], NT) + dot(up_ref[...], du_ref[...], NT)
@@ -188,8 +203,9 @@
     copies = [pltpu.make_async_copy(dx_ref, dx_hbm, sem.at[0])]
     copies[0].start()
     ct = c_ref[...].T
-    c = jnp.concatenate([c2_ref[...], c_ref[...]], axis=1)
-    z = jnp.concatenate([z2_ref[...], z_ref[...]], axis=1)
+    cut = whole_tiles(act_ref.shape[0])
+    c = jnp.concatenate([c2_ref[:, cut:], c_ref[...]], axis=1)
+    z = jnp.concatenate([z2_ref[:, cut:], z_ref[...]], axis=1)
     parts = chunks(gg_ref.shape[1])
 
     def add(hc, m, left, right, part_ref, ref, hbm):
@@ -202,9 +218,9 @@
         return dot(ct, down_ref[:, hc])
 
     def use(hc, da):
-        add(hc, 2, c, stack(act2_ref[:, hc], act_ref[:, hc]), pd_ref, gd_ref, gd_hbm)
-        add(hc, 0, z, stack(dg2_ref[:, hc], da * p_ref[:, hc].astype(F32)), pg_ref, gg_ref, gg_hbm)
-        add(hc, 1, z, stack(du2_ref[:, hc], da * q_ref[:, hc].astype(F32)), pu_ref, gu_ref, gu_hbm)
+        add(hc, 2, c, stack(act2_ref[cut:, hc], act_ref[:, hc]), pd_ref, gd_ref, gd_hbm)
+        add(hc, 0, z, stack(dg2_ref[cut:, hc], da * p_ref[:, hc].astype(F32)), pg_ref, gg_ref, gg_hbm)
+        add(hc, 1, z, stack(du2_ref[cut:, hc], da * q_ref[:, hc].astype(F32)), pu_ref, gu_ref, gu_hbm)
 
     staggered(parts, ahead, use)
     for copy in copies:
@@ -273,10 +289,11 @@
     return whole(second_grads_kernel, (v, c, *w, *own), [(d, h)] * 3, "second_grads")
 
 
-def first_back(x, c, p, q, w, name):
+def first_back(x, c, p, q, w, z, act, parts):
     d, t = x.shape
     h = w[0].shape[1]
-    return whole(first_back_kernel, (x, c, p, q, *w), [(d, t), (t, h), (t, h)], name)
+    shapes = [(d, t), (t, h), (t, h)] + [(d, h)] * 3
+    return whole(first_back_kernel, (x, c, p, q, *w, z, act, *parts), shapes, "first_back_own")
 
 
 def final(c, z, act, p, q, down, parts, dx, held):
@@ -310,7 +327,7 @@
     d = shift(d_b, 1)
     d_o = shift(d_b, 1, True)
     parts = second_grads(after(h_bo, d_b), g_bo, w, (z0, g_b, act0, dg0, du0))
-    dx, dg2, du2 = first_back(x, after(d, parts[0]), p2, q2, w, "first_back_own")
+    dx, dg2, du2, *parts = first_back(x, d, p2, q2, w, z2, act2, parts)
     gg, gu, gd, dx = final(d_o, z3, act3, p3, q3, w[2], parts, dx, (d, z2, act2, dg2, du2))
     return dx.T[None], gg[None], gu[None], gd.T[None]
 

time: 49.7 us -> 48.4 us (0.974)
  waiting for transfers between devices: 5.3 us -> 3.97 us
    pallas_call x1, Pallas kernels: 6.23 us -> 4.89 us  [final(): pl.pallas_call(final_kernel, in_specs=[pl.BlockSpec(memory_space=pltpu.VM...]
    ppermute x7, waiting for transfers between devices: 5.3 us -> 3.97 us  [shift(): return lax.ppermute(x, ('blk', 'dp'), pairs)]
    pallas_call x5, Pallas kernels: 19.5 us -> 20.8 us  [whole(): pl.pallas_call(kernel, in_specs=[spec] * len(args), out_specs=[spec] * le...]
  transfers between devices with their start and end apart: 7 -> 7, of which waited for: 4 -> 4; matrix products, arithmetic and copies ran while one was open for 0% -> 0% of each run, Pallas kernels for 49% -> 53%
where the time goes in v8:
time: 48.4 us; the launch traced here: 48.2 us
  Pallas kernels  30.5 us (63%)
  starting transfers between devices  12.8 us (26%)
  waiting for transfers between devices  3.97 us (8%)
  between operations  0.87 us (2%)
    pallas_call x5, Pallas kernels, whole(): pl.pallas_call(kernel, in_specs=[spec] * len(args), out_specs=[spec] * le...  20.8 us
    ppermute x7, starting transfers between devices, shift(): return lax.ppermute(x, ('blk', 'dp'), pairs)  12.8 us
    pallas_call x1, Pallas kernels, final(): pl.pallas_call(final_kernel, in_specs=[pl.BlockSpec(memory_space=pltpu.VM...  4.89 us
    pallas_call x1, Pallas kernels, loading_first(): pl.pallas_call(loading_forward_kernel, in_specs=[pl.BlockSpec(memory_spac...  4.86 us
    ppermute x7, waiting for transfers between devices, shift(): return lax.ppermute(x, ('blk', 'dp'), pairs)  3.97 us
  transfers between devices with their start and end apart: 7, of which 4 were waited for; matrix products, arithmetic and copies ran while one was open for 0% of the time, Pallas kernels for 53%

profile of v8, /device:TPU:0, one launch (start us, length us, event | category | flops | bytes accessed | tf_op | source)
XLA Modules:
  0.0 48.2 jit_solution(15979093563476013214)
XLA Ops:
  0.6 3.0 %collective-permute-start.1 = (bf16[576,384]{1,0:T(8,128)(2,1)}, bf16[576,384]{1,0:T(8,128)(2,1)S(1)}, u32[]{:S(2)}, u32[]{:S(2)}) collective-permute-start(bf16[576,384]{1,0:T(8,128)(2,1)} %bitcast.23), channel_id=1, source_target_pairs={{0,1},{1,0},{2,3},{3,2},{4,5},{5,4},{6,7},{7,6},{8,9},{9,8},{10,11... | collective-permute-start | bytes 1327112 | tf_op jit(solution)/shard_map/ppermute | solution.py:22
  3.6 3.7 %collective-permute-start.2 = (bf16[576,384]{1,0:T(8,128)(2,1)}, bf16[576,384]{1,0:T(8,128)(2,1)S(1)}, u32[]{:S(2)}, u32[]{:S(2)}) collective-permute-start(bf16[576,384]{1,0:T(8,128)(2,1)} %bitcast.22), channel_id=1, source_target_pairs={{0,30},{1,31},{2,0},{3,1},{4,2},{5,3},{6,4},{7,5},{8,6},{9,7},{10,... | collective-permute-start | bytes 1327112 | tf_op jit(solution)/shard_map/ppermute | solution.py:22
  7.4 4.9 %first_own.1 = (bf16[576,384]{1,0:T(8,128)(2,1)S(1)}, bf16[576,384]{1,0:T(8,128)(2,1)S(1)}, bf16[384,1536]{1,0:T(8,128)(2,1)S(1)}, bf16[384,1536]{1,0:T(8,128)(2...) custom-call(bf16[576,384]{1,0:T(8,128)(2,1)} %bitcast.24, ...), custom_call_target="tpu_custom_call" | custom-call | flops 10000000000 | bytes 30000000 | tf_op jit(solution)/shard_map/first_own/pallas_call | solution.py:265
  12.2 1.0 %collective-permute-start = (bf16[576,384]{1,0:T(8,128)(2,1)S(1)}, bf16[576,384]{1,0:T(8,128)(2,1)S(1)}, u32[]{:S(2)}, u32[]{:S(2)}) collective-permute-start(bf16[576,384]{1,0:T(8,128)(2,1)S(1)} %get-tuple-element.40), channel_id=1, source_target_pairs={{0,30},{1,31},{2,0},{3,1},{4,2},{5,3},{6,4},{7,5},{8,6},{9,7},{10,... | collective-permute-start | bytes 1327112 | tf_op jit(solution)/shard_map/ppermute | solution.py:22
  13.2 0.3 collective-permute-done.2.c_ref.c0_ref
  13.5 0.5 %collective-permute-start.6 = (bf16[576,384]{1,0:T(8,128)(2,1)S(1)}, bf16[576,384]{1,0:T(8,128)(2,1)S(1)}, u32[]{:S(2)}, u32[]{:S(2)}) collective-permute-start(bf16[576,384]{1,0:T(8,128)(2,1)S(1)} %collective-permute-done.2.c_ref.c0_ref), channel_id=1, source_target_pairs={{0,1},{1,0},{2,3},{3,2},{4,5},{5,4},{6,7},{7,6},{8,9},{9,8},{10,11... | collective-permute-start | bytes 1327112 | tf_op jit(solution)/shard_map/ppermute | solution.py:22
  14.0 1.1 %hidden_cotangent.1.da_ref = f32[384,1536]{1,0:T(8,128)S(1)} custom-call(bf16[576,384]{1,0:T(8,128)(2,1)S(1)} %collective-permute-done.2.c_ref.c0_ref, bf16[576,1536]{1,0:T(8,128)(2,1)S(1)} %get-tuple-element.42.down_ref.refs_3_), custom_call_target="tpu_custom_call" | custom-call | flops 10000000000 | bytes 30000000 | tf_op jit(solution)/shard_map/hidden_cotangent/pallas_call | solution.py:244
  15.1 0.0 collective-permute-done.1.refs_0_
  15.1 3.2 %first_other.1 = (bf16[576,384]{1,0:T(8,128)(2,1)S(1)}, bf16[576,384]{1,0:T(8,128)(2,1)S(1)}, bf16[384,1536]{1,0:T(8,128)(2,1)S(1)}, bf16[384,1536]{1,0:T(8,128)(2,1)S(1)}, bf16[384,1536]{1,0:T(8,128)(2,1)S(1)}) custom-call(bf16[576,384]{1,0:T(8,128)(2,1)S(1)} %collective-permute-done.1.refs_0_, bf16[576,1536]{1,0:T(8,128)(2,1)S(1)} %get-tuple-element.44.refs_1_.gate_ref, ...), custom_call_target="tpu_custom_call" | custom-call | flops 10000000000 | bytes 30000000 | tf_op jit(solution)/shard_map/first_other/pallas_call | solution.py:244
  18.3 4.3 %collective-permute-start.5 = (bf16[576,384]{1,0:T(8,128)(2,1)S(1)}, bf16[576,384]{1,0:T(8,128)(2,1)S(1)}, u32[]{:S(2)}, u32[]{:S(2)}) collective-permute-start(bf16[576,384]{1,0:T(8,128)(2,1)S(1)} %get-tuple-element.46), channel_id=1, source_target_pairs={{0,30},{1,31},{2,0},{3,1},{4,2},{5,3},{6,4},{7,5},{8,6},{9,7},{10,... | collective-permute-start | bytes 1327112 | tf_op jit(solution)/shard_map/ppermute | solution.py:22
  22.6 0.0 collective-permute-done.h_ref
  22.6 4.4 %second_own.1 = (bf16[576,384]{1,0:T(8,128)(2,1)S(1)}, bf16[576,384]{1,0:T(8,128)(2,1)S(1)}, bf16[384,1536]{1,0:T(8,128)(2,1)S(1)}, bf16[384,1536]{1,0:T(8,128)(2,1)S(1)}, bf16[384,1536]{1,0:T(8,128)(2,1)S(1)}) custom-call(bf16[576,384]{1,0:T(8,128)(2,1)S(1)} %collective-permute-done.h_ref, bf16[576,384]{1,0:T(8,128)(2,1)S(1)} %collective-permute-done.2.c_ref.c0_ref, ...), custom_call_target="tpu_custom_call" | custom-call | flops 10000000000 | bytes 30000000 | tf_op jit(solution)/shard_map/second_own/pallas_call | solution.py:244
  27.0 0.1 collective-permute-start.4
  27.1 0.2 collective-permute-start.3
  27.3 1.1 %collective-permute-done.5.h_ref = bf16[576,384]{1,0:T(8,128)(2,1)S(1)} collective-permute-done((bf16[576,384]{1,0:T(8,128)(2,1)S(1)}, bf16[576,384]{1,0:T(8,128)(2,1)S(1)}, u32[]{:S(2)}, u32[]{:S(2)}) %collective-permute-start.5) | collective-permute-done | bytes 442400 | tf_op jit(solution)/shard_map/ppermute | solution.py:22
  28.4 0.0 collective-permute-done.6.c_ref
  28.4 7.4 %second_grads.1 = (bf16[576,1536]{1,0:T(8,128)(2,1)S(1)}, bf16[576,1536]{1,0:T(8,128)(2,1)S(1)}, bf16[576,1536]{1,0:T(8,128)(2,1)S(1)}) custom-call(bf16[576,384]{1,0:T(8,128)(2,1)S(1)} %collective-permute-done.5.h_ref, bf16[576,384]{1,0:T(8,128)(2,1)S(1)} %collective-permute-done.6.c_ref, bf16[576,1536]{1,0:T(8,128)(2,1)S(1)} %get-tuple-element.44.refs_1_.gate_ref, ...), custom_call_target="tpu_custom_call" | custom-call | flops 10000000000 | bytes 30000000 | tf_op jit(solution)/shard_map/second_grads/pallas_call | solution.py:244
  35.8 1.7 %collective-permute-done.4.c_ref.c2_ref = bf16[576,384]{1,0:T(8,128)(2,1)S(1)} collective-permute-done((bf16[576,384]{1,0:T(8,128)(2,1)S(1)}, bf16[576,384]{1,0:T(8,128)(2,1)S(1)}, u32[]{:S(2)}, u32[]{:S(2)}) %collective-permute-start.4) | collective-permute-done | bytes 442400 | tf_op jit(solution)/shard_map/ppermute | solution.py:22
  37.5 4.7 %first_back_own.1 = (bf16[576,384]{1,0:T(8,128)(2,1)S(1)}, bf16[384,1536]{1,0:T(8,128)(2,1)S(1)}, bf16[384,1536]{1,0:T(8,128)(2,1)S(1)}, bf16[576,1536]{1,0:T(8,...) custom-call(bf16[576,384]{1,0:T(8,128)(2,1)S(1)} %get-tuple-element.53.x_ref, ...), custom_call_target="tpu_custom_call" | custom-call | flops 10000000000 | bytes 30000000 | tf_op jit(solution)/shard_map/first_back_own/pallas_call | solution.py:244
  42.2 0.9 %collective-permute-done.3.c_ref = bf16[576,384]{1,0:T(8,128)(2,1)S(1)} collective-permute-done((bf16[576,384]{1,0:T(8,128)(2,1)S(1)}, bf16[576,384]{1,0:T(8,128)(2,1)S(1)}, u32[]{:S(2)}, u32[]{:S(2)}) %collective-permute-start.3) | collective-permute-done | bytes 442400 | tf_op jit(solution)/shard_map/ppermute | solution.py:22
  43.2 4.9 %final.1 = (bf16[576,1536]{1,0:T(8,128)(2,1)}, bf16[576,1536]{1,0:T(8,128)(2,1)}, bf16[576,1536]{1,0:T(8,128)(2,1)}, bf16[576,384]{1,0:T(8,128)(2,1)}) custom-call(bf16[576,384]{1,0:T(8,128)(2,1)S(1)} %collective-permute-done.3.c_ref, bf16[576,384]{1,0:T(8,128)(2,1)S(1)} %get-tuple-element.49.z_ref, bf16[384,1536]{1,0:T(8,128)(2,1)S(1)} %get-tuple-element.50.act_ref, ...), custom_call_target="tpu_custom_call" | custom-call | flops 10000000000 | bytes 30000000 | tf_op jit(solution)/shard_map/final/pallas_call | solution.py:303
Async XLA Ops:
  0.6 14.5 %collective-permute-start.1 = (bf16[576,384]{1,0:T(8,128)(2,1)}, bf16[576,384]{1,0:T(8,128)(2,1)S(1)}, u32[]{:S(2)}, u32[]{:S(2)}) collective-permute-start(bf16[576,384]{1,0:T(8,128)(2,1)} %bitcast.23), channel_id=1, source_target_pairs={{0,1},{1,0},{2,3},{3,2},{4,5},{5,4},{6,7},{7,6},{8,9},{9,8},{10,11... | collective-permute-start | bytes 1327112 | tf_op jit(solution)/shard_map/ppermute | solution.py:22
  3.6 9.9 %collective-permute-start.2 = (bf16[576,384]{1,0:T(8,128)(2,1)}, bf16[576,384]{1,0:T(8,128)(2,1)S(1)}, u32[]{:S(2)}, u32[]{:S(2)}) collective-permute-start(bf16[576,384]{1,0:T(8,128)(2,1)} %bitcast.22), channel_id=1, source_target_pairs={{0,30},{1,31},{2,0},{3,1},{4,2},{5,3},{6,4},{7,5},{8,6},{9,7},{10,... | collective-permute-start | bytes 1327112 | tf_op jit(solution)/shard_map/ppermute | solution.py:22
  12.2 10.4 %collective-permute-start = (bf16[576,384]{1,0:T(8,128)(2,1)S(1)}, bf16[576,384]{1,0:T(8,128)(2,1)S(1)}, u32[]{:S(2)}, u32[]{:S(2)}) collective-permute-start(bf16[576,384]{1,0:T(8,128)(2,1)S(1)} %get-tuple-element.40), channel_id=1, source_target_pairs={{0,30},{1,31},{2,0},{3,1},{4,2},{5,3},{6,4},{7,5},{8,6},{9,7},{10,... | collective-permute-start | bytes 1327112 | tf_op jit(solution)/shard_map/ppermute | solution.py:22
  13.5 14.9 %collective-permute-start.6 = (bf16[576,384]{1,0:T(8,128)(2,1)S(1)}, bf16[576,384]{1,0:T(8,128)(2,1)S(1)}, u32[]{:S(2)}, u32[]{:S(2)}) collective-permute-start(bf16[576,384]{1,0:T(8,128)(2,1)S(1)} %collective-permute-done.2.c_ref.c0_ref), channel_id=1, source_target_pairs={{0,1},{1,0},{2,3},{3,2},{4,5},{5,4},{6,7},{7,6},{8,9},{9,8},{10,11... | collective-permute-start | bytes 1327112 | tf_op jit(solution)/shard_map/ppermute | solution.py:22
  18.3 10.1 %collective-permute-start.5 = (bf16[576,384]{1,0:T(8,128)(2,1)S(1)}, bf16[576,384]{1,0:T(8,128)(2,1)S(1)}, u32[]{:S(2)}, u32[]{:S(2)}) collective-permute-start(bf16[576,384]{1,0:T(8,128)(2,1)S(1)} %get-tuple-element.46), channel_id=1, source_target_pairs={{0,30},{1,31},{2,0},{3,1},{4,2},{5,3},{6,4},{7,5},{8,6},{9,7},{10,... | collective-permute-start | bytes 1327112 | tf_op jit(solution)/shard_map/ppermute | solution.py:22
  27.0 10.5 %collective-permute-start.4 = (bf16[576,384]{1,0:T(8,128)(2,1)S(1)}, bf16[576,384]{1,0:T(8,128)(2,1)S(1)}, u32[]{:S(2)}, u32[]{:S(2)}) collective-permute-start(bf16[576,384]{1,0:T(8,128)(2,1)S(1)} %get-tuple-element.48), channel_id=1, source_target_pairs={{0,2},{1,3},{2,4},{3,5},{4,6},{5,7},{6,8},{7,9},{8,10},{9,11},{10,... | collective-permute-start | bytes 1327112 | tf_op jit(solution)/shard_map/ppermute | solution.py:22
  27.1 16.1 %collective-permute-start.3 = (bf16[576,384]{1,0:T(8,128)(2,1)S(1)}, bf16[576,384]{1,0:T(8,128)(2,1)S(1)}, u32[]{:S(2)}, u32[]{:S(2)}) collective-permute-start(bf16[576,384]{1,0:T(8,128)(2,1)S(1)} %get-tuple-element.48), channel_id=1, source_target_pairs={{0,3},{1,2},{2,5},{3,4},{4,7},{5,6},{6,9},{7,8},{8,11},{9,10},{10,... | collective-permute-start | bytes 1327112 | tf_op jit(solution)/shard_map/ppermute | solution.py:22

commit v9 on v8

--- a/solution.py
+++ b/solution.py
@@ -318,7 +318,7 @@
     g_b = shift(g, -1)
     h, z2, act2, p2, q2, x, *w = loading_first(x, (w_gate[0], w_up[0], w_down[0].T), "first_own")
     h_b = shift(h, -1)
-    g_bo = shift(after(g_b, h), 0, True)
+    g_bo = shift(after(g, h), -1, True)
     da_b = hidden_cotangent(after(g_b, h), w[2])
     x_o = after(x_o, da_b)
     h_o, z3, act3, p3, q3 = first(x_o, w, "first_other")

time: 48.4 us -> 53.9 us (1.11)
  the two profiles are of different devices: /device:TPU:0 before, /device:TPU:25 now
where the time goes in v9:
time: 53.9 us; the launch traced here: 53.8 us
  Pallas kernels  30.6 us (57%)
  waiting for transfers between devices  13 us (24%)
  starting transfers between devices  9.31 us (17%)
  between operations  0.86 us (2%)
    pallas_call x5, Pallas kernels, whole(): pl.pallas_call(kernel, in_specs=[spec] * len(args), out_specs=[spec] * le...  20.8 us
    ppermute x7, waiting for transfers between devices, shift(): return lax.ppermute(x, ('blk', 'dp'), pairs)  13 us
    ppermute x7, starting transfers between devices, shift(): return lax.ppermute(x, ('blk', 'dp'), pairs)  9.31 us
    pallas_call x1, Pallas kernels, loading_first(): pl.pallas_call(loading_forward_kernel, in_specs=[pl.BlockSpec(memory_spac...  4.92 us
    pallas_call x1, Pallas kernels, final(): pl.pallas_call(final_kernel, in_specs=[pl.BlockSpec(memory_space=pltpu.VM...  4.89 us
  transfers between devices with their start and end apart: 7, of which 3 were waited for; matrix products, arithmetic and copies ran while one was open for 0% of the time, Pallas kernels for 48%

profile of v9, /device:TPU:25, one launch (start us, length us, event | category | flops | bytes accessed | tf_op | source)
XLA Modules:
  0.0 53.8 jit_solution(15327481756535344098)
XLA Ops:
  0.6 1.3 %collective-permute-start.1 = (bf16[576,384]{1,0:T(8,128)(2,1)}, bf16[576,384]{1,0:T(8,128)(2,1)S(1)}, u32[]{:S(2)}, u32[]{:S(2)}) collective-permute-start(bf16[576,384]{1,0:T(8,128)(2,1)} %bitcast.22), channel_id=1, source_target_pairs={{0,1},{1,0},{2,3},{3,2},{4,5},{5,4},{6,7},{7,6},{8,9},{9,8},{10,11... | collective-permute-start | bytes 1327112 | tf_op jit(solution)/shard_map/ppermute | solution.py:22
  1.9 1.0 %collective-permute-start.2 = (bf16[576,384]{1,0:T(8,128)(2,1)}, bf16[576,384]{1,0:T(8,128)(2,1)S(1)}, u32[]{:S(2)}, u32[]{:S(2)}) collective-permute-start(bf16[576,384]{1,0:T(8,128)(2,1)} %bitcast.24), channel_id=1, source_target_pairs={{0,30},{1,31},{2,0},{3,1},{4,2},{5,3},{6,4},{7,5},{8,6},{9,7},{10,... | collective-permute-start | bytes 1327112 | tf_op jit(solution)/shard_map/ppermute | solution.py:22
  2.9 0.0 copy-start
  2.9 4.9 %first_own.1 = (bf16[576,384]{1,0:T(8,128)(2,1)S(1)}, bf16[576,384]{1,0:T(8,128)(2,1)S(1)}, bf16[384,1536]{1,0:T(8,128)(2,1)S(1)}, bf16[384,1536]{1,0:T(8,128)(2...) custom-call(bf16[576,384]{1,0:T(8,128)(2,1)} %bitcast.23, ...), custom_call_target="tpu_custom_call" | custom-call | flops 10000000000 | bytes 30000000 | tf_op jit(solution)/shard_map/first_own/pallas_call | solution.py:265
  7.8 0.6 %collective-permute-start = (bf16[576,384]{1,0:T(8,128)(2,1)S(1)}, bf16[576,384]{1,0:T(8,128)(2,1)S(1)}, u32[]{:S(2)}, u32[]{:S(2)}) collective-permute-start(bf16[576,384]{1,0:T(8,128)(2,1)S(1)} %get-tuple-element.41), channel_id=1, source_target_pairs={{0,30},{1,31},{2,0},{3,1},{4,2},{5,3},{6,4},{7,5},{8,6},{9,7},{10,... | collective-permute-start | bytes 1327112 | tf_op jit(solution)/shard_map/ppermute | solution.py:22
  8.4 0.0 copy-done
  8.4 1.1 %collective-permute-start.6 = (bf16[576,384]{1,0:T(8,128)(2,1)S(1)}, bf16[576,384]{1,0:T(8,128)(2,1)S(1)}, u32[]{:S(2)}, u32[]{:S(2)}) collective-permute-start(bf16[576,384]{1,0:T(8,128)(2,1)S(1)} %bitcast.25), channel_id=1, source_target_pairs={{0,31},{1,30},{2,1},{3,0},{4,3},{5,2},{6,5},{7,4},{8,7},{9,6},{10,... | collective-permute-start | bytes 1327112 | tf_op jit(solution)/shard_map/ppermute | solution.py:22
  9.5 1.0 %collective-permute-done.2.c_ref.c0_ref = bf16[576,384]{1,0:T(8,128)(2,1)S(1)} collective-permute-done((bf16[576,384]{1,0:T(8,128)(2,1)}, bf16[576,384]{1,0:T(8,128)(2,1)S(1)}, u32[]{:S(2)}, u32[]{:S(2)}) %collective-permute-start.2) | collective-permute-done | bytes 442400 | tf_op jit(solution)/shard_map/ppermute | solution.py:22
  10.5 1.1 %hidden_cotangent.1.da_ref = f32[384,1536]{1,0:T(8,128)S(1)} custom-call(bf16[576,384]{1,0:T(8,128)(2,1)S(1)} %collective-permute-done.2.c_ref.c0_ref, bf16[576,1536]{1,0:T(8,128)(2,1)S(1)} %get-tuple-element.43.down_ref.refs_3_), custom_call_target="tpu_custom_call" | custom-call | flops 10000000000 | bytes 30000000 | tf_op jit(solution)/shard_map/hidden_cotangent/pallas_call | solution.py:244
  11.6 0.4 collective-permute-done.1.refs_0_
  11.9 3.2 %first_other.1 = (bf16[576,384]{1,0:T(8,128)(2,1)S(1)}, bf16[576,384]{1,0:T(8,128)(2,1)S(1)}, bf16[384,1536]{1,0:T(8,128)(2,1)S(1)}, bf16[384,1536]{1,0:T(8,128)(2,1)S(1)}, bf16[384,1536]{1,0:T(8,128)(2,1)S(1)}) custom-call(bf16[576,384]{1,0:T(8,128)(2,1)S(1)} %collective-permute-done.1.refs_0_, bf16[576,1536]{1,0:T(8,128)(2,1)S(1)} %get-tuple-element.45.refs_1_.gate_ref, ...), custom_call_target="tpu_custom_call" | custom-call | flops 10000000000 | bytes 30000000 | tf_op jit(solution)/shard_map/first_other/pallas_call | solution.py:244
  15.1 2.7 %collective-permute-start.5 = (bf16[576,384]{1,0:T(8,128)(2,1)S(1)}, bf16[576,384]{1,0:T(8,128)(2,1)S(1)}, u32[]{:S(2)}, u32[]{:S(2)}) collective-permute-start(bf16[576,384]{1,0:T(8,128)(2,1)S(1)} %get-tuple-element.47), channel_id=1, source_target_pairs={{0,30},{1,31},{2,0},{3,1},{4,2},{5,3},{6,4},{7,5},{8,6},{9,7},{10,... | collective-permute-start | bytes 1327112 | tf_op jit(solution)/shard_map/ppermute | solution.py:22
  17.8 0.0 collective-permute-done.h_ref
  17.8 4.4 %second_own.1 = (bf16[576,384]{1,0:T(8,128)(2,1)S(1)}, bf16[576,384]{1,0:T(8,128)(2,1)S(1)}, bf16[384,1536]{1,0:T(8,128)(2,1)S(1)}, bf16[384,1536]{1,0:T(8,128)(2,1)S(1)}, bf16[384,1536]{1,0:T(8,128)(2,1)S(1)}) custom-call(bf16[576,384]{1,0:T(8,128)(2,1)S(1)} %collective-permute-done.h_ref, bf16[576,384]{1,0:T(8,128)(2,1)S(1)} %collective-permute-done.2.c_ref.c0_ref, ...), custom_call_target="tpu_custom_call" | custom-call | flops 10000000000 | bytes 30000000 | tf_op jit(solution)/shard_map/second_own/pallas_call | solution.py:244
  22.2 1.3 %collective-permute-start.4 = (bf16[576,384]{1,0:T(8,128)(2,1)S(1)}, bf16[576,384]{1,0:T(8,128)(2,1)S(1)}, u32[]{:S(2)}, u32[]{:S(2)}) collective-permute-start(bf16[576,384]{1,0:T(8,128)(2,1)S(1)} %get-tuple-element.49), channel_id=1, source_target_pairs={{0,2},{1,3},{2,4},{3,5},{4,6},{5,7},{6,8},{7,9},{8,10},{9,11},{10,... | collective-permute-start | bytes 1327112 | tf_op jit(solution)/shard_map/ppermute | solution.py:22
  23.5 1.4 %collective-permute-start.3 = (bf16[576,384]{1,0:T(8,128)(2,1)S(1)}, bf16[576,384]{1,0:T(8,128)(2,1)S(1)}, u32[]{:S(2)}, u32[]{:S(2)}) collective-permute-start(bf16[576,384]{1,0:T(8,128)(2,1)S(1)} %get-tuple-element.49), channel_id=1, source_target_pairs={{0,3},{1,2},{2,5},{3,4},{4,7},{5,6},{6,9},{7,8},{8,11},{9,10},{10,... | collective-permute-start | bytes 1327112 | tf_op jit(solution)/shard_map/ppermute | solution.py:22
  24.9 11.6 %collective-permute-done.5.h_ref = bf16[576,384]{1,0:T(8,128)(2,1)S(1)} collective-permute-done((bf16[576,384]{1,0:T(8,128)(2,1)S(1)}, bf16[576,384]{1,0:T(8,128)(2,1)S(1)}, u32[]{:S(2)}, u32[]{:S(2)}) %collective-permute-start.5) | collective-permute-done | bytes 442400 | tf_op jit(solution)/shard_map/ppermute | solution.py:22
  36.5 0.0 collective-permute-done.6.c_ref
  36.5 7.4 %second_grads.1 = (bf16[576,1536]{1,0:T(8,128)(2,1)S(1)}, bf16[576,1536]{1,0:T(8,128)(2,1)S(1)}, bf16[576,1536]{1,0:T(8,128)(2,1)S(1)}) custom-call(bf16[576,384]{1,0:T(8,128)(2,1)S(1)} %collective-permute-done.5.h_ref, bf16[576,384]{1,0:T(8,128)(2,1)S(1)} %collective-permute-done.6.c_ref, bf16[576,1536]{1,0:T(8,128)(2,1)S(1)} %get-tuple-element.45.refs_1_.gate_ref, ...), custom_call_target="tpu_custom_call" | custom-call | flops 10000000000 | bytes 30000000 | tf_op jit(solution)/shard_map/second_grads/pallas_call | solution.py:244
  43.9 0.0 collective-permute-done.4.c_ref.c2_ref
  43.9 4.8 %first_back_own.1 = (bf16[576,384]{1,0:T(8,128)(2,1)S(1)}, bf16[384,1536]{1,0:T(8,128)(2,1)S(1)}, bf16[384,1536]{1,0:T(8,128)(2,1)S(1)}, bf16[576,1536]{1,0:T(8,...) custom-call(bf16[576,384]{1,0:T(8,128)(2,1)S(1)} %get-tuple-element.54.x_ref, ...), custom_call_target="tpu_custom_call" | custom-call | flops 10000000000 | bytes 30000000 | tf_op jit(solution)/shard_map/first_back_own/pallas_call | solution.py:244
  48.7 0.0 collective-permute-done.3.c_ref
  48.7 4.9 %final.1 = (bf16[576,1536]{1,0:T(8,128)(2,1)}, bf16[576,1536]{1,0:T(8,128)(2,1)}, bf16[576,1536]{1,0:T(8,128)(2,1)}, bf16[576,384]{1,0:T(8,128)(2,1)}) custom-call(bf16[576,384]{1,0:T(8,128)(2,1)S(1)} %collective-permute-done.3.c_ref, bf16[576,384]{1,0:T(8,128)(2,1)S(1)} %get-tuple-element.50.z_ref, bf16[384,1536]{1,0:T(8,128)(2,1)S(1)} %get-tuple-element.51.act_ref, ...), custom_call_target="tpu_custom_call" | custom-call | flops 10000000000 | bytes 30000000 | tf_op jit(solution)/shard_map/final/pallas_call | solution.py:303
Async XLA Ops:
  0.6 11.3 %collective-permute-start.1 = (bf16[576,384]{1,0:T(8,128)(2,1)}, bf16[576,384]{1,0:T(8,128)(2,1)S(1)}, u32[]{:S(2)}, u32[]{:S(2)}) collective-permute-start(bf16[576,384]{1,0:T(8,128)(2,1)} %bitcast.22), channel_id=1, source_target_pairs={{0,1},{1,0},{2,3},{3,2},{4,5},{5,4},{6,7},{7,6},{8,9},{9,8},{10,11... | collective-permute-start | bytes 1327112 | tf_op jit(solution)/shard_map/ppermute | solution.py:22
  1.9 8.6 %collective-permute-start.2 = (bf16[576,384]{1,0:T(8,128)(2,1)}, bf16[576,384]{1,0:T(8,128)(2,1)S(1)}, u32[]{:S(2)}, u32[]{:S(2)}) collective-permute-start(bf16[576,384]{1,0:T(8,128)(2,1)} %bitcast.24), channel_id=1, source_target_pairs={{0,30},{1,31},{2,0},{3,1},{4,2},{5,3},{6,4},{7,5},{8,6},{9,7},{10,... | collective-permute-start | bytes 1327112 | tf_op jit(solution)/shard_map/ppermute | solution.py:22
  2.9 5.5 %copy-start = (bf16[1,384,576]{1,2,0:T(8,128)(2,1)S(1)}, bf16[1,384,576]{1,2,0:T(8,128)(2,1)}, u32[]{:S(2)}) copy-start(bf16[1,384,576]{1,2,0:T(8,128)(2,1)} %param.6) | copy-start | bytes 1327108
  7.8 10.0 %collective-permute-start = (bf16[576,384]{1,0:T(8,128)(2,1)S(1)}, bf16[576,384]{1,0:T(8,128)(2,1)S(1)}, u32[]{:S(2)}, u32[]{:S(2)}) collective-permute-start(bf16[576,384]{1,0:T(8,128)(2,1)S(1)} %get-tuple-element.41), channel_id=1, source_target_pairs={{0,30},{1,31},{2,0},{3,1},{4,2},{5,3},{6,4},{7,5},{8,6},{9,7},{10,... | collective-permute-start | bytes 1327112 | tf_op jit(solution)/shard_map/ppermute | solution.py:22
  8.4 28.1 %collective-permute-start.6 = (bf16[576,384]{1,0:T(8,128)(2,1)S(1)}, bf16[576,384]{1,0:T(8,128)(2,1)S(1)}, u32[]{:S(2)}, u32[]{:S(2)}) collective-permute-start(bf16[576,384]{1,0:T(8,128)(2,1)S(1)} %bitcast.25), channel_id=1, source_target_pairs={{0,31},{1,30},{2,1},{3,0},{4,3},{5,2},{6,5},{7,4},{8,7},{9,6},{10,... | collective-permute-start | bytes 1327112 | tf_op jit(solution)/shard_map/ppermute | solution.py:22
  15.1 21.4 %collective-permute-start.5 = (bf16[576,384]{1,0:T(8,128)(2,1)S(1)}, bf16[576,384]{1,0:T(8,128)(2,1)S(1)}, u32[]{:S(2)}, u32[]{:S(2)}) collective-permute-start(bf16[576,384]{1,0:T(8,128)(2,1)S(1)} %get-tuple-element.47), channel_id=1, source_target_pairs={{0,30},{1,31},{2,0},{3,1},{4,2},{5,3},{6,4},{7,5},{8,6},{9,7},{10,... | collective-permute-start | bytes 1327112 | tf_op jit(solution)/shard_map/ppermute | solution.py:22
  22.2 21.7 %collective-permute-start.4 = (bf16[576,384]{1,0:T(8,128)(2,1)S(1)}, bf16[576,384]{1,0:T(8,128)(2,1)S(1)}, u32[]{:S(2)}, u32[]{:S(2)}) collective-permute-start(bf16[576,384]{1,0:T(8,128)(2,1)S(1)} %get-tuple-element.49), channel_id=1, source_target_pairs={{0,2},{1,3},{2,4},{3,5},{4,6},{5,7},{6,8},{7,9},{8,10},{9,11},{10,... | collective-permute-start | bytes 1327112 | tf_op jit(solution)/shard_map/ppermute | solution.py:22
  23.5 25.2 %collective-permute-start.3 = (bf16[576,384]{1,0:T(8,128)(2,1)S(1)}, bf16[576,384]{1,0:T(8,128)(2,1)S(1)}, u32[]{:S(2)}, u32[]{:S(2)}) collective-permute-start(bf16[576,384]{1,0:T(8,128)(2,1)S(1)} %get-tuple-element.49), channel_id=1, source_target_pairs={{0,3},{1,2},{2,5},{3,4},{4,7},{5,6},{6,9},{7,8},{8,11},{9,10},{10,... | collective-permute-start | bytes 1327112 | tf_op jit(solution)/shard_map/ppermute | solution.py:22

commit v10 on v8

--- a/solution.py
+++ b/solution.py
@@ -119,7 +119,7 @@
         da_ref[:, hc] = dot(ct, down_ref[:, hc])
 
 
-def second_kernel(h_ref, c_ref, gate_ref, up_ref, da_ref, d_ref, z_ref, act_ref, dg_ref, du_ref):
+def second_kernel(h_ref, c_ref, gate_ref, up_ref, da_ref, d_lo_ref, d_hi_ref, z_ref, act_ref, dg_ref, du_ref):
     inverse, normed = normalize(h_ref[...].astype(F32))
     zed = normed.astype(BF16)
     z_ref[...] = zed
@@ -136,7 +136,10 @@
 
     staggered(chunks(gate_ref.shape[1]), ahead, use)
     dz = dot(gate_ref[...], dg_ref[...], NT) + dot(up_ref[...], du_ref[...], NT)
-    d_ref[...] = input_cotangent(c_ref[...].astype(F32), dz, inverse, normed)
+    d = input_cotangent(c_ref[...].astype(F32), dz, inverse, normed)
+    half = d_lo_ref.shape[0]
+    d_lo_ref[...] = d[:half]
+    d_hi_ref[...] = d[half:]
 
 
 def second_grads_kernel(
@@ -170,13 +173,14 @@
 
 
 def first_back_kernel(
-    x_ref, c_ref, p_ref, q_ref, gate_ref, up_ref, down_ref, z_ref, act_ref, pg_ref, pu_ref, pd_ref,
+    x_ref, c_lo_ref, c_hi_ref, p_ref, q_ref, gate_ref, up_ref, down_ref, z_ref, act_ref, pg_ref, pu_ref, pd_ref,
     d_ref, dg_ref, du_ref, gg_ref, gu_ref, gd_ref,
 ):
     inverse, normed = normalize(x_ref[...].astype(F32))
-    ct = c_ref[...].T
+    whole_c = jnp.concatenate([c_lo_ref[...], c_hi_ref[...]], axis=0)
+    ct = whole_c.T
     cut = whole_tiles(act_ref.shape[0])
-    c = c_ref[:, :cut]
+    c = whole_c[:, :cut]
     z = z_ref[:, :cut]
 
     def ahead(hc):
@@ -193,18 +197,20 @@
 
     staggered(chunks(gate_ref.shape[1]), ahead, use)
     dz = dot(gate_ref[...], dg_ref[...], NT) + dot(up_ref[...], du_ref[...], NT)
-    d_ref[...] = input_cotangent(c_ref[...].astype(F32), dz, inverse, normed)
+    d_ref[...] = input_cotangent(whole_c.astype(F32), dz, inverse, normed)
 
 
 def final_kernel(
-    c_ref, z_ref, act_ref, p_ref, q_ref, down_ref, pg_ref, pu_ref, pd_ref, dx_ref, c2_ref, z2_ref, act2_ref, dg2_ref, du2_ref,
+    c_lo_ref, c_hi_ref, z_ref, act_ref, p_ref, q_ref, down_ref, pg_ref, pu_ref, pd_ref, dx_ref, c2_lo_ref, c2_hi_ref, z2_ref, act2_ref, dg2_ref, du2_ref,
     gg_hbm, gu_hbm, gd_hbm, dx_hbm, gg_ref, gu_ref, gd_ref, sem,
 ):
     copies = [pltpu.make_async_copy(dx_ref, dx_hbm, sem.at[0])]
     copies[0].start()
-    ct = c_ref[...].T
+    whole_c = jnp.concatenate([c_lo_ref[...], c_hi_ref[...]], axis=0)
+    ct = whole_c.T
     cut = whole_tiles(act_ref.shape[0])
-    c = jnp.concatenate([c2_ref[:, cut:], c_ref[...]], axis=1)
+    c2 = jnp.concatenate([c2_lo_ref[:, cut:], c2_hi_ref[:, cut:]], axis=0)
+    c = jnp.concatenate([c2, whole_c], axis=1)
     z = jnp.concatenate([z2_ref[:, cut:], z_ref[...]], axis=1)
     parts = chunks(gg_ref.shape[1])
 
@@ -281,7 +287,8 @@
 def second(v, c, gate, up, da):
     d, t = v.shape
     h = gate.shape[1]
-    return whole(second_kernel, (v, c, gate, up, da), [(d, t), (d, t), (t, h), (t, h), (t, h)], "second_own")
+    shapes = [(d // 2, t), (d - d // 2, t), (d, t), (t, h), (t, h), (t, h)]
+    return whole(second_kernel, (v, c, gate, up, da), shapes, "second_own")
 
 
 def second_grads(v, c, w, own):
@@ -293,13 +300,12 @@
     d, t = x.shape
     h = w[0].shape[1]
     shapes = [(d, t), (t, h), (t, h)] + [(d, h)] * 3
-    return whole(first_back_kernel, (x, c, p, q, *w, z, act, *parts), shapes, "first_back_own")
+    return whole(first_back_kernel, (x, *c, p, q, *w, z, act, *parts), shapes, "first_back_own")
 
 
 def final(c, z, act, p, q, down, parts, dx, held):
-    d, t = c.shape
-    h = down.shape[1]
-    args = (c, z, act, p, q, down, *parts, dx, *held)
+    (d, h), t = down.shape, act.shape[0]
+    args = (*c, z, act, p, q, down, *parts, dx, *held)
     return pl.pallas_call(
         final_kernel,
         in_specs=[pl.BlockSpec(memory_space=pltpu.VMEM)] * len(args),
@@ -323,12 +329,12 @@
     x_o = after(x_o, da_b)
     h_o, z3, act3, p3, q3 = first(x_o, w, "first_other")
     h_bo = shift(h_o, -1)
-    d_b, z0, act0, dg0, du0 = second(after(h_b, h_o), g_b, w[0], w[1], da_b)
-    d = shift(d_b, 1)
-    d_o = shift(d_b, 1, True)
-    parts = second_grads(after(h_bo, d_b), g_bo, w, (z0, g_b, act0, dg0, du0))
+    *d_b, z0, act0, dg0, du0 = second(after(h_b, h_o), g_b, w[0], w[1], da_b)
+    d = [shift(part, 1) for part in d_b]
+    d_o = [shift(part, 1, True) for part in d_b]
+    parts = second_grads(after(h_bo, d_b[0]), g_bo, w, (z0, g_b, act0, dg0, du0))
     dx, dg2, du2, *parts = first_back(x, d, p2, q2, w, z2, act2, parts)
-    gg, gu, gd, dx = final(d_o, z3, act3, p3, q3, w[2], parts, dx, (d, z2, act2, dg2, du2))
+    gg, gu, gd, dx = final(d_o, z3, act3, p3, q3, w[2], parts, dx, (*d, z2, act2, dg2, du2))
     return dx.T[None], gg[None], gu[None], gd.T[None]
 
 

time: 48.4 us -> 50.8 us (1.050)
  waiting for transfers between devices: 3.97 us -> 6.47 us
    ppermute x7 -> x9, waiting for transfers between devices: 3.97 us -> 6.47 us  [shift(): return lax.ppermute(x, ('blk', 'dp'), pairs)]
    ppermute x7 -> x9, starting transfers between devices: 12.8 us -> 12.7 us  [shift(): return lax.ppermute(x, ('blk', 'dp'), pairs)]
  transfers between devices with their start and end apart: 7 -> 9, of which waited for: 4 -> 3; matrix products, arithmetic and copies ran while one was open for 0% -> 0% of each run, Pallas kernels for 53% -> 51%
where the time goes in v10:
time: 50.8 us; the launch traced here: 50.6 us
  Pallas kernels  30.5 us (60%)
  starting transfers between devices  12.7 us (25%)
  waiting for transfers between devices  6.47 us (13%)
  between operations  0.9 us (2%)
    pallas_call x5, Pallas kernels, whole(): pl.pallas_call(kernel, in_specs=[spec] * len(args), out_specs=[spec] * le...  20.8 us
    ppermute x9, starting transfers between devices, shift(): return lax.ppermute(x, ('blk', 'dp'), pairs)  12.7 us
    ppermute x9, waiting for transfers between devices, shift(): return lax.ppermute(x, ('blk', 'dp'), pairs)  6.47 us
    pallas_call x1, Pallas kernels, final(): pl.pallas_call(final_kernel, in_specs=[pl.BlockSpec(memory_space=pltpu.VM...  4.92 us
    pallas_call x1, Pallas kernels, loading_first(): pl.pallas_call(loading_forward_kernel, in_specs=[pl.BlockSpec(memory_spac...  4.86 us
  transfers between devices with their start and end apart: 9, of which 3 were waited for; matrix products, arithmetic and copies ran while one was open for 0% of the time, Pallas kernels for 51%

profile of v10, /device:TPU:0, one launch (start us, length us, event | category | flops | bytes accessed | tf_op | source)
XLA Modules:
  0.0 50.6 jit_solution(14161550692815323440)
XLA Ops:
  0.6 3.0 %collective-permute-start.1 = (bf16[576,384]{1,0:T(8,128)(2,1)}, bf16[576,384]{1,0:T(8,128)(2,1)S(1)}, u32[]{:S(2)}, u32[]{:S(2)}) collective-permute-start(bf16[576,384]{1,0:T(8,128)(2,1)} %bitcast.23), channel_id=1, source_target_pairs={{0,1},{1,0},{2,3},{3,2},{4,5},{5,4},{6,7},{7,6},{8,9},{9,8},{10,11... | collective-permute-start | bytes 1327112 | tf_op jit(solution)/shard_map/ppermute | solution.py:22
  3.6 3.7 %collective-permute-start.2 = (bf16[576,384]{1,0:T(8,128)(2,1)}, bf16[576,384]{1,0:T(8,128)(2,1)S(1)}, u32[]{:S(2)}, u32[]{:S(2)}) collective-permute-start(bf16[576,384]{1,0:T(8,128)(2,1)} %bitcast.22), channel_id=1, source_target_pairs={{0,30},{1,31},{2,0},{3,1},{4,2},{5,3},{6,4},{7,5},{8,6},{9,7},{10,... | collective-permute-start | bytes 1327112 | tf_op jit(solution)/shard_map/ppermute | solution.py:22
  7.4 4.9 %first_own.1 = (bf16[576,384]{1,0:T(8,128)(2,1)S(1)}, bf16[576,384]{1,0:T(8,128)(2,1)S(1)}, bf16[384,1536]{1,0:T(8,128)(2,1)S(1)}, bf16[384,1536]{1,0:T(8,128)(2...) custom-call(bf16[576,384]{1,0:T(8,128)(2,1)} %bitcast.24, ...), custom_call_target="tpu_custom_call" | custom-call | flops 10000000000 | bytes 30000000 | tf_op jit(solution)/shard_map/first_own/pallas_call | solution.py:271
  12.2 1.0 %collective-permute-start = (bf16[576,384]{1,0:T(8,128)(2,1)S(1)}, bf16[576,384]{1,0:T(8,128)(2,1)S(1)}, u32[]{:S(2)}, u32[]{:S(2)}) collective-permute-start(bf16[576,384]{1,0:T(8,128)(2,1)S(1)} %get-tuple-element.41), channel_id=1, source_target_pairs={{0,30},{1,31},{2,0},{3,1},{4,2},{5,3},{6,4},{7,5},{8,6},{9,7},{10,... | collective-permute-start | bytes 1327112 | tf_op jit(solution)/shard_map/ppermute | solution.py:22
  13.2 0.3 collective-permute-done.2.c_ref.c0_ref
  13.5 0.5 %collective-permute-start.8 = (bf16[576,384]{1,0:T(8,128)(2,1)S(1)}, bf16[576,384]{1,0:T(8,128)(2,1)S(1)}, u32[]{:S(2)}, u32[]{:S(2)}) collective-permute-start(bf16[576,384]{1,0:T(8,128)(2,1)S(1)} %collective-permute-done.2.c_ref.c0_ref), channel_id=1, source_target_pairs={{0,1},{1,0},{2,3},{3,2},{4,5},{5,4},{6,7},{7,6},{8,9},{9,8},{10,11... | collective-permute-start | bytes 1327112 | tf_op jit(solution)/shard_map/ppermute | solution.py:22
  14.0 1.1 %hidden_cotangent.1.da_ref = f32[384,1536]{1,0:T(8,128)S(1)} custom-call(bf16[576,384]{1,0:T(8,128)(2,1)S(1)} %collective-permute-done.2.c_ref.c0_ref, bf16[576,1536]{1,0:T(8,128)(2,1)S(1)} %get-tuple-element.43.down_ref.refs_3_), custom_call_target="tpu_custom_call" | custom-call | flops 10000000000 | bytes 30000000 | tf_op jit(solution)/shard_map/hidden_cotangent/pallas_call | solution.py:250
  15.1 0.0 collective-permute-done.1.refs_0_
  15.1 3.2 %first_other.1 = (bf16[576,384]{1,0:T(8,128)(2,1)S(1)}, bf16[576,384]{1,0:T(8,128)(2,1)S(1)}, bf16[384,1536]{1,0:T(8,128)(2,1)S(1)}, bf16[384,1536]{1,0:T(8,128)(2,1)S(1)}, bf16[384,1536]{1,0:T(8,128)(2,1)S(1)}) custom-call(bf16[576,384]{1,0:T(8,128)(2,1)S(1)} %collective-permute-done.1.refs_0_, bf16[576,1536]{1,0:T(8,128)(2,1)S(1)} %get-tuple-element.45.refs_1_.gate_ref, ...), custom_call_target="tpu_custom_call" | custom-call | flops 10000000000 | bytes 30000000 | tf_op jit(solution)/shard_map/first_other/pallas_call | solution.py:250
  18.3 4.3 %collective-permute-start.7 = (bf16[576,384]{1,0:T(8,128)(2,1)S(1)}, bf16[576,384]{1,0:T(8,128)(2,1)S(1)}, u32[]{:S(2)}, u32[]{:S(2)}) collective-permute-start(bf16[576,384]{1,0:T(8,128)(2,1)S(1)} %get-tuple-element.47), channel_id=1, source_target_pairs={{0,30},{1,31},{2,0},{3,1},{4,2},{5,3},{6,4},{7,5},{8,6},{9,7},{10,... | collective-permute-start | bytes 1327112 | tf_op jit(solution)/shard_map/ppermute | solution.py:22
  22.6 0.0 collective-permute-done.h_ref
  22.6 4.4 %second_own.1 = (bf16[288,384]{1,0:T(8,128)(2,1)S(1)}, bf16[288,384]{1,0:T(8,128)(2,1)S(1)}, bf16[576,384]{1,0:T(8,128)(2,1)S(1)}, bf16[384,1536]{1,0:T(8,128)(2...) custom-call(bf16[576,384]{1,0:T(8,128)(2,1)S(1)} %collective-permute-done.h_ref, ...), custom_call_target="tpu_custom_call" | custom-call | flops 10000000000 | bytes 30000000 | tf_op jit(solution)/shard_map/second_own/pallas_call | solution.py:250
  27.0 0.1 collective-permute-start.6
  27.1 0.1 collective-permute-start.4
  27.1 0.1 collective-permute-start.5
  27.2 1.2 %collective-permute-done.7.h_ref = bf16[576,384]{1,0:T(8,128)(2,1)S(1)} collective-permute-done((bf16[576,384]{1,0:T(8,128)(2,1)S(1)}, bf16[576,384]{1,0:T(8,128)(2,1)S(1)}, u32[]{:S(2)}, u32[]{:S(2)}) %collective-permute-start.7) | collective-permute-done | bytes 442400 | tf_op jit(solution)/shard_map/ppermute | solution.py:22
  28.4 0.0 collective-permute-start.3
  28.4 0.0 collective-permute-done.8.c_ref
  28.4 7.4 %second_grads.1 = (bf16[576,1536]{1,0:T(8,128)(2,1)S(1)}, bf16[576,1536]{1,0:T(8,128)(2,1)S(1)}, bf16[576,1536]{1,0:T(8,128)(2,1)S(1)}) custom-call(bf16[576,384]{1,0:T(8,128)(2,1)S(1)} %collective-permute-done.7.h_ref, bf16[576,384]{1,0:T(8,128)(2,1)S(1)} %collective-permute-done.8.c_ref, bf16[576,1536]{1,0:T(8,128)(2,1)S(1)} %get-tuple-element.45.refs_1_.gate_ref, ...), custom_call_target="tpu_custom_call" | custom-call | flops 10000000000 | bytes 30000000 | tf_op jit(solution)/shard_map/second_grads/pallas_call | solution.py:250
  35.8 0.0 collective-permute-done.6.c_hi_ref.c2_hi_ref
  35.8 5.0 %collective-permute-done.5.c_lo_ref.c2_lo_ref = bf16[288,384]{1,0:T(8,128)(2,1)S(1)} collective-permute-done((bf16[288,384]{1,0:T(8,128)(2,1)S(1)}, bf16[288,384]{1,0:T(8,128)(2,1)S(1)}, u32[]{:S(2)}, u32[]{:S(2)}) %collective-permute-start.5) | collective-permute-done | bytes 221216 | tf_op jit(solution)/shard_map/ppermute | solution.py:22
  40.8 4.7 %first_back_own.1 = (bf16[576,384]{1,0:T(8,128)(2,1)S(1)}, bf16[384,1536]{1,0:T(8,128)(2,1)S(1)}, bf16[384,1536]{1,0:T(8,128)(2,1)S(1)}, bf16[576,1536]{1,0:T(8,...) custom-call(bf16[576,384]{1,0:T(8,128)(2,1)S(1)} %get-tuple-element.55.x_ref, ...), custom_call_target="tpu_custom_call" | custom-call | flops 10000000000 | bytes 30000000 | tf_op jit(solution)/shard_map/first_back_own/pallas_call | solution.py:250
  45.5 0.0 collective-permute-done.4.c_hi_ref
  45.5 0.0 collective-permute-done.3.c_lo_ref
  45.5 4.9 %final.1 = (bf16[576,1536]{1,0:T(8,128)(2,1)}, bf16[576,1536]{1,0:T(8,128)(2,1)}, bf16[576,1536]{1,0:T(8,128)(2,1)}, bf16[576,384]{1,0:T(8,128)(2,1)}) custom-call(bf16[288,384]{1,0:T(8,128)(2,1)S(1)} %collective-permute-done.3.c_lo_ref, bf16[288,384]{1,0:T(8,128)(2,1)S(1)} %collective-permute-done.4.c_hi_ref, bf16[576,384]{1,0:T(8,128)(2,1)S(1)} %get-tuple-element.51.z_ref, ...), custom_call_target="tpu_custom_call" | custom-call | flops 10000000000 | bytes 30000000 | tf_op jit(solution)/shard_map/final/pallas_call | solution.py:309
Async XLA Ops:
  0.6 14.5 %collective-permute-start.1 = (bf16[576,384]{1,0:T(8,128)(2,1)}, bf16[576,384]{1,0:T(8,128)(2,1)S(1)}, u32[]{:S(2)}, u32[]{:S(2)}) collective-permute-start(bf16[576,384]{1,0:T(8,128)(2,1)} %bitcast.23), channel_id=1, source_target_pairs={{0,1},{1,0},{2,3},{3,2},{4,5},{5,4},{6,7},{7,6},{8,9},{9,8},{10,11... | collective-permute-start | bytes 1327112 | tf_op jit(solution)/shard_map/ppermute | solution.py:22
  3.6 9.9 %collective-permute-start.2 = (bf16[576,384]{1,0:T(8,128)(2,1)}, bf16[576,384]{1,0:T(8,128)(2,1)S(1)}, u32[]{:S(2)}, u32[]{:S(2)}) collective-permute-start(bf16[576,384]{1,0:T(8,128)(2,1)} %bitcast.22), channel_id=1, source_target_pairs={{0,30},{1,31},{2,0},{3,1},{4,2},{5,3},{6,4},{7,5},{8,6},{9,7},{10,... | collective-permute-start | bytes 1327112 | tf_op jit(solution)/shard_map/ppermute | solution.py:22
  12.2 10.4 %collective-permute-start = (bf16[576,384]{1,0:T(8,128)(2,1)S(1)}, bf16[576,384]{1,0:T(8,128)(2,1)S(1)}, u32[]{:S(2)}, u32[]{:S(2)}) collective-permute-start(bf16[576,384]{1,0:T(8,128)(2,1)S(1)} %get-tuple-element.41), channel_id=1, source_target_pairs={{0,30},{1,31},{2,0},{3,1},{4,2},{5,3},{6,4},{7,5},{8,6},{9,7},{10,... | collective-permute-start | bytes 1327112 | tf_op jit(solution)/shard_map/ppermute | solution.py:22
  13.5 14.9 %collective-permute-start.8 = (bf16[576,384]{1,0:T(8,128)(2,1)S(1)}, bf16[576,384]{1,0:T(8,128)(2,1)S(1)}, u32[]{:S(2)}, u32[]{:S(2)}) collective-permute-start(bf16[576,384]{1,0:T(8,128)(2,1)S(1)} %collective-permute-done.2.c_ref.c0_ref), channel_id=1, source_target_pairs={{0,1},{1,0},{2,3},{3,2},{4,5},{5,4},{6,7},{7,6},{8,9},{9,8},{10,11... | collective-permute-start | bytes 1327112 | tf_op jit(solution)/shard_map/ppermute | solution.py:22
  18.3 10.1 %collective-permute-start.7 = (bf16[576,384]{1,0:T(8,128)(2,1)S(1)}, bf16[576,384]{1,0:T(8,128)(2,1)S(1)}, u32[]{:S(2)}, u32[]{:S(2)}) collective-permute-start(bf16[576,384]{1,0:T(8,128)(2,1)S(1)} %get-tuple-element.47), channel_id=1, source_target_pairs={{0,30},{1,31},{2,0},{3,1},{4,2},{5,3},{6,4},{7,5},{8,6},{9,7},{10,... | collective-permute-start | bytes 1327112 | tf_op jit(solution)/shard_map/ppermute | solution.py:22
  27.0 8.8 %collective-permute-start.6 = (bf16[288,384]{1,0:T(8,128)(2,1)S(1)}, bf16[288,384]{1,0:T(8,128)(2,1)S(1)}, u32[]{:S(2)}, u32[]{:S(2)}) collective-permute-start(bf16[288,384]{1,0:T(8,128)(2,1)S(1)} %get-tuple-element.50), channel_id=1, source_target_pairs={{0,2},{1,3},{2,4},{3,5},{4,6},{5,7},{6,8},{7,9},{8,10},{9,11},{10,... | collective-permute-start | bytes 663560 | tf_op jit(solution)/shard_map/ppermute | solution.py:22
  27.1 18.4 %collective-permute-start.4 = (bf16[288,384]{1,0:T(8,128)(2,1)S(1)}, bf16[288,384]{1,0:T(8,128)(2,1)S(1)}, u32[]{:S(2)}, u32[]{:S(2)}) collective-permute-start(bf16[288,384]{1,0:T(8,128)(2,1)S(1)} %get-tuple-element.50), channel_id=1, source_target_pairs={{0,3},{1,2},{2,5},{3,4},{4,7},{5,6},{6,9},{7,8},{8,11},{9,10},{10,... | collective-permute-start | bytes 663560 | tf_op jit(solution)/shard_map/ppermute | solution.py:22
  27.1 13.6 %collective-permute-start.5 = (bf16[288,384]{1,0:T(8,128)(2,1)S(1)}, bf16[288,384]{1,0:T(8,128)(2,1)S(1)}, u32[]{:S(2)}, u32[]{:S(2)}) collective-permute-start(bf16[288,384]{1,0:T(8,128)(2,1)S(1)} %get-tuple-element.49), channel_id=1, source_target_pairs={{0,2},{1,3},{2,4},{3,5},{4,6},{5,7},{6,8},{7,9},{8,10},{9,11},{10,... | collective-permute-start | bytes 663560 | tf_op jit(solution)/shard_map/ppermute | solution.py:22
  28.4 17.1 %collective-permute-start.3 = (bf16[288,384]{1,0:T(8,128)(2,1)S(1)}, bf16[288,384]{1,0:T(8,128)(2,1)S(1)}, u32[]{:S(2)}, u32[]{:S(2)}) collective-permute-start(bf16[288,384]{1,0:T(8,128)(2,1)S(1)} %get-tuple-element.49), channel_id=1, source_target_pairs={{0,3},{1,2},{2,5},{3,4},{4,7},{5,6},{6,9},{7,8},{8,11},{9,10},{10,... | collective-permute-start | bytes 663560 | tf_op jit(solution)/shard_map/ppermute | solution.py:22

commit v11 on v10

--- a/solution.py
+++ b/solution.py
@@ -119,7 +119,7 @@
         da_ref[:, hc] = dot(ct, down_ref[:, hc])
 
 
-def second_kernel(h_ref, c_ref, gate_ref, up_ref, da_ref, d_lo_ref, d_hi_ref, z_ref, act_ref, dg_ref, du_ref):
+def second_kernel(h_ref, c_ref, gate_ref, up_ref, da_ref, d_ref, d_lo_ref, d_hi_ref, z_ref, act_ref, dg_ref, du_ref):
     inverse, normed = normalize(h_ref[...].astype(F32))
     zed = normed.astype(BF16)
     z_ref[...] = zed
@@ -137,6 +137,7 @@
     staggered(chunks(gate_ref.shape[1]), ahead, use)
     dz = dot(gate_ref[...], dg_ref[...], NT) + dot(up_ref[...], du_ref[...], NT)
     d = input_cotangent(c_ref[...].astype(F32), dz, inverse, normed)
+    d_ref[...] = d
     half = d_lo_ref.shape[0]
     d_lo_ref[...] = d[:half]
     d_hi_ref[...] = d[half:]
@@ -201,16 +202,15 @@
 
 
 def final_kernel(
-    c_lo_ref, c_hi_ref, z_ref, act_ref, p_ref, q_ref, down_ref, pg_ref, pu_ref, pd_ref, dx_ref, c2_lo_ref, c2_hi_ref, z2_ref, act2_ref, dg2_ref, du2_ref,
+    c_ref, z_ref, act_ref, p_ref, q_ref, down_ref, pg_ref, pu_ref, pd_ref, dx_ref, c2_lo_ref, c2_hi_ref, z2_ref, act2_ref, dg2_ref, du2_ref,
     gg_hbm, gu_hbm, gd_hbm, dx_hbm, gg_ref, gu_ref, gd_ref, sem,
 ):
     copies = [pltpu.make_async_copy(dx_ref, dx_hbm, sem.at[0])]
     copies[0].start()
-    whole_c = jnp.concatenate([c_lo_ref[...], c_hi_ref[...]], axis=0)
-    ct = whole_c.T
+    ct = c_ref[...].T
     cut = whole_tiles(act_ref.shape[0])
     c2 = jnp.concatenate([c2_lo_ref[:, cut:], c2_hi_ref[:, cut:]], axis=0)
-    c = jnp.concatenate([c2, whole_c], axis=1)
+    c = jnp.concatenate([c2, c_ref[...]], axis=1)
     z = jnp.concatenate([z2_ref[:, cut:], z_ref[...]], axis=1)
     parts = chunks(gg_ref.shape[1])
 
@@ -287,7 +287,7 @@
 def second(v, c, gate, up, da):
     d, t = v.shape
     h = gate.shape[1]
-    shapes = [(d // 2, t), (d - d // 2, t), (d, t), (t, h), (t, h), (t, h)]
+    shapes = [(d, t), (d // 2, t), (d - d // 2, t), (d, t), (t, h), (t, h), (t, h)]
     return whole(second_kernel, (v, c, gate, up, da), shapes, "second_own")
 
 
@@ -305,7 +305,7 @@
 
 def final(c, z, act, p, q, down, parts, dx, held):
     (d, h), t = down.shape, act.shape[0]
-    args = (*c, z, act, p, q, down, *parts, dx, *held)
+    args = (c, z, act, p, q, down, *parts, dx, *held)
     return pl.pallas_call(
         final_kernel,
         in_specs=[pl.BlockSpec(memory_space=pltpu.VMEM)] * len(args),
@@ -329,10 +329,10 @@
     x_o = after(x_o, da_b)
     h_o, z3, act3, p3, q3 = first(x_o, w, "first_other")
     h_bo = shift(h_o, -1)
-    *d_b, z0, act0, dg0, du0 = second(after(h_b, h_o), g_b, w[0], w[1], da_b)
-    d = [shift(part, 1) for part in d_b]
-    d_o = [shift(part, 1, True) for part in d_b]
-    parts = second_grads(after(h_bo, d_b[0]), g_bo, w, (z0, g_b, act0, dg0, du0))
+    d_b, *d_halves, z0, act0, dg0, du0 = second(after(h_b, h_o), g_b, w[0], w[1], da_b)
+    d = [shift(part, 1) for part in d_halves]
+    d_o = shift(d_b, 1, True)
+    parts = second_grads(after(h_bo, d_b), g_bo, w, (z0, g_b, act0, dg0, du0))
     dx, dg2, du2, *parts = first_back(x, d, p2, q2, w, z2, act2, parts)
     gg, gu, gd, dx = final(d_o, z3, act3, p3, q3, w[2], parts, dx, (*d, z2, act2, dg2, du2))
     return dx.T[None], gg[None], gu[None], gd.T[None]

time: 50.8 us -> 48.4 us (0.953)
  waiting for transfers between devices: 6.47 us -> 3.91 us
    ppermute x9 -> x8, waiting for transfers between devices: 6.47 us -> 3.91 us  [shift(): return lax.ppermute(x, ('blk', 'dp'), pairs)]
    ppermute x9 -> x8, starting transfers between devices: 12.7 us -> 12.9 us  [shift(): return lax.ppermute(x, ('blk', 'dp'), pairs)]
  transfers between devices with their start and end apart: 9 -> 8, of which waited for: 3 -> 4; matrix products, arithmetic and copies ran while one was open for 0% -> 0% of each run, Pallas kernels for 51% -> 53%
where the time goes in v11:
time: 48.4 us; the launch traced here: 48.2 us
  Pallas kernels  30.6 us (63%)
  starting transfers between devices  12.9 us (27%)
  waiting for transfers between devices  3.91 us (8%)
  between operations  0.88 us (2%)
    pallas_call x5, Pallas kernels, whole(): pl.pallas_call(kernel, in_specs=[spec] * len(args), out_specs=[spec] * le...  20.8 us
    ppermute x8, starting transfers between devices, shift(): return lax.ppermute(x, ('blk', 'dp'), pairs)  12.9 us
    pallas_call x1, Pallas kernels, final(): pl.pallas_call(final_kernel, in_specs=[pl.BlockSpec(memory_space=pltpu.VM...  4.89 us
    pallas_call x1, Pallas kernels, loading_first(): pl.pallas_call(loading_forward_kernel, in_specs=[pl.BlockSpec(memory_spac...  4.86 us
    ppermute x8, waiting for transfers between devices, shift(): return lax.ppermute(x, ('blk', 'dp'), pairs)  3.91 us
  transfers between devices with their start and end apart: 8, of which 4 were waited for; matrix products, arithmetic and copies ran while one was open for 0% of the time, Pallas kernels for 53%

profile of v11, /device:TPU:0, one launch (start us, length us, event | category | flops | bytes accessed | tf_op | source)
XLA Modules:
  0.0 48.2 jit_solution(506841880593568821)
XLA Ops:
  0.6 3.0 %collective-permute-start.1 = (bf16[576,384]{1,0:T(8,128)(2,1)}, bf16[576,384]{1,0:T(8,128)(2,1)S(1)}, u32[]{:S(2)}, u32[]{:S(2)}) collective-permute-start(bf16[576,384]{1,0:T(8,128)(2,1)} %bitcast.23), channel_id=1, source_target_pairs={{0,1},{1,0},{2,3},{3,2},{4,5},{5,4},{6,7},{7,6},{8,9},{9,8},{10,11... | collective-permute-start | bytes 1327112 | tf_op jit(solution)/shard_map/ppermute | solution.py:22
  3.6 3.7 %collective-permute-start.2 = (bf16[576,384]{1,0:T(8,128)(2,1)}, bf16[576,384]{1,0:T(8,128)(2,1)S(1)}, u32[]{:S(2)}, u32[]{:S(2)}) collective-permute-start(bf16[576,384]{1,0:T(8,128)(2,1)} %bitcast.22), channel_id=1, source_target_pairs={{0,30},{1,31},{2,0},{3,1},{4,2},{5,3},{6,4},{7,5},{8,6},{9,7},{10,... | collective-permute-start | bytes 1327112 | tf_op jit(solution)/shard_map/ppermute | solution.py:22
  7.4 4.9 %first_own.1 = (bf16[576,384]{1,0:T(8,128)(2,1)S(1)}, bf16[576,384]{1,0:T(8,128)(2,1)S(1)}, bf16[384,1536]{1,0:T(8,128)(2,1)S(1)}, bf16[384,1536]{1,0:T(8,128)(2...) custom-call(bf16[576,384]{1,0:T(8,128)(2,1)} %bitcast.24, ...), custom_call_target="tpu_custom_call" | custom-call | flops 10000000000 | bytes 30000000 | tf_op jit(solution)/shard_map/first_own/pallas_call | solution.py:271
  12.2 1.0 %collective-permute-start = (bf16[576,384]{1,0:T(8,128)(2,1)S(1)}, bf16[576,384]{1,0:T(8,128)(2,1)S(1)}, u32[]{:S(2)}, u32[]{:S(2)}) collective-permute-start(bf16[576,384]{1,0:T(8,128)(2,1)S(1)} %get-tuple-element.42), channel_id=1, source_target_pairs={{0,30},{1,31},{2,0},{3,1},{4,2},{5,3},{6,4},{7,5},{8,6},{9,7},{10,... | collective-permute-start | bytes 1327112 | tf_op jit(solution)/shard_map/ppermute | solution.py:22
  13.2 0.3 collective-permute-done.2.c_ref.c0_ref
  13.5 0.5 %collective-permute-start.7 = (bf16[576,384]{1,0:T(8,128)(2,1)S(1)}, bf16[576,384]{1,0:T(8,128)(2,1)S(1)}, u32[]{:S(2)}, u32[]{:S(2)}) collective-permute-start(bf16[576,384]{1,0:T(8,128)(2,1)S(1)} %collective-permute-done.2.c_ref.c0_ref), channel_id=1, source_target_pairs={{0,1},{1,0},{2,3},{3,2},{4,5},{5,4},{6,7},{7,6},{8,9},{9,8},{10,11... | collective-permute-start | bytes 1327112 | tf_op jit(solution)/shard_map/ppermute | solution.py:22
  14.0 1.1 %hidden_cotangent.1.da_ref = f32[384,1536]{1,0:T(8,128)S(1)} custom-call(bf16[576,384]{1,0:T(8,128)(2,1)S(1)} %collective-permute-done.2.c_ref.c0_ref, bf16[576,1536]{1,0:T(8,128)(2,1)S(1)} %get-tuple-element.44.down_ref.refs_3_), custom_call_target="tpu_custom_call" | custom-call | flops 10000000000 | bytes 30000000 | tf_op jit(solution)/shard_map/hidden_cotangent/pallas_call | solution.py:250
  15.1 0.0 collective-permute-done.1.refs_0_
  15.1 3.2 %first_other.1 = (bf16[576,384]{1,0:T(8,128)(2,1)S(1)}, bf16[576,384]{1,0:T(8,128)(2,1)S(1)}, bf16[384,1536]{1,0:T(8,128)(2,1)S(1)}, bf16[384,1536]{1,0:T(8,128)(2,1)S(1)}, bf16[384,1536]{1,0:T(8,128)(2,1)S(1)}) custom-call(bf16[576,384]{1,0:T(8,128)(2,1)S(1)} %collective-permute-done.1.refs_0_, bf16[576,1536]{1,0:T(8,128)(2,1)S(1)} %get-tuple-element.46.refs_1_.gate_ref, ...), custom_call_target="tpu_custom_call" | custom-call | flops 10000000000 | bytes 30000000 | tf_op jit(solution)/shard_map/first_other/pallas_call | solution.py:250
  18.3 4.3 %collective-permute-start.6 = (bf16[576,384]{1,0:T(8,128)(2,1)S(1)}, bf16[576,384]{1,0:T(8,128)(2,1)S(1)}, u32[]{:S(2)}, u32[]{:S(2)}) collective-permute-start(bf16[576,384]{1,0:T(8,128)(2,1)S(1)} %get-tuple-element.48), channel_id=1, source_target_pairs={{0,30},{1,31},{2,0},{3,1},{4,2},{5,3},{6,4},{7,5},{8,6},{9,7},{10,... | collective-permute-start | bytes 1327112 | tf_op jit(solution)/shard_map/ppermute | solution.py:22
  22.6 0.0 collective-permute-done.h_ref
  22.6 4.4 %second_own.1 = (bf16[576,384]{1,0:T(8,128)(2,1)S(1)}, bf16[288,384]{1,0:T(8,128)(2,1)S(1)}, bf16[288,384]{1,0:T(8,128)(2,1)S(1)}, bf16[576,384]{1,0:T(8,128)(2,...) custom-call(bf16[576,384]{1,0:T(8,128)(2,1)S(1)} %collective-permute-done.h_ref,, ...), custom_call_target="tpu_custom_call" | custom-call | flops 10000000000 | bytes 30000000 | tf_op jit(solution)/shard_map/second_own/pallas_call | solution.py:250
  27.0 0.1 collective-permute-start.4
  27.1 0.1 collective-permute-start.5
  27.2 0.2 collective-permute-start.3
  27.4 1.0 %collective-permute-done.6.h_ref = bf16[576,384]{1,0:T(8,128)(2,1)S(1)} collective-permute-done((bf16[576,384]{1,0:T(8,128)(2,1)S(1)}, bf16[576,384]{1,0:T(8,128)(2,1)S(1)}, u32[]{:S(2)}, u32[]{:S(2)}) %collective-permute-start.6) | collective-permute-done | bytes 442400 | tf_op jit(solution)/shard_map/ppermute | solution.py:22
  28.4 0.0 collective-permute-done.7.c_ref
  28.4 7.4 %second_grads.1 = (bf16[576,1536]{1,0:T(8,128)(2,1)S(1)}, bf16[576,1536]{1,0:T(8,128)(2,1)S(1)}, bf16[576,1536]{1,0:T(8,128)(2,1)S(1)}) custom-call(bf16[576,384]{1,0:T(8,128)(2,1)S(1)} %collective-permute-done.6.h_ref, bf16[576,384]{1,0:T(8,128)(2,1)S(1)} %collective-permute-done.7.c_ref, bf16[576,1536]{1,0:T(8,128)(2,1)S(1)} %get-tuple-element.46.refs_1_.gate_ref, ...), custom_call_target="tpu_custom_call" | custom-call | flops 10000000000 | bytes 30000000 | tf_op jit(solution)/shard_map/second_grads/pallas_call | solution.py:250
  35.8 0.0 collective-permute-done.4.c_lo_ref.c2_lo_ref
  35.8 1.7 %collective-permute-done.5.c_hi_ref.c2_hi_ref = bf16[288,384]{1,0:T(8,128)(2,1)S(1)} collective-permute-done((bf16[288,384]{1,0:T(8,128)(2,1)S(1)}, bf16[288,384]{1,0:T(8,128)(2,1)S(1)}, u32[]{:S(2)}, u32[]{:S(2)}) %collective-permute-start.5) | collective-permute-done | bytes 221216 | tf_op jit(solution)/shard_map/ppermute | solution.py:22
  37.5 4.7 %first_back_own.1 = (bf16[576,384]{1,0:T(8,128)(2,1)S(1)}, bf16[384,1536]{1,0:T(8,128)(2,1)S(1)}, bf16[384,1536]{1,0:T(8,128)(2,1)S(1)}, bf16[576,1536]{1,0:T(8,...) custom-call(bf16[576,384]{1,0:T(8,128)(2,1)S(1)} %get-tuple-element.55.x_ref, ...), custom_call_target="tpu_custom_call" | custom-call | flops 10000000000 | bytes 30000000 | tf_op jit(solution)/shard_map/first_back_own/pallas_call | solution.py:250
  42.3 0.9 %collective-permute-done.3.c_ref = bf16[576,384]{1,0:T(8,128)(2,1)S(1)} collective-permute-done((bf16[576,384]{1,0:T(8,128)(2,1)S(1)}, bf16[576,384]{1,0:T(8,128)(2,1)S(1)}, u32[]{:S(2)}, u32[]{:S(2)}) %collective-permute-start.3) | collective-permute-done | bytes 442400 | tf_op jit(solution)/shard_map/ppermute | solution.py:22
  43.2 4.9 %final.1 = (bf16[576,1536]{1,0:T(8,128)(2,1)}, bf16[576,1536]{1,0:T(8,128)(2,1)}, bf16[576,1536]{1,0:T(8,128)(2,1)}, bf16[576,384]{1,0:T(8,128)(2,1)}) custom-call(bf16[576,384]{1,0:T(8,128)(2,1)S(1)} %collective-permute-done.3.c_ref, bf16[576,384]{1,0:T(8,128)(2,1)S(1)} %get-tuple-element.51.z_ref, bf16[384,1536]{1,0:T(8,128)(2,1)S(1)} %get-tuple-element.52.act_ref, ...), custom_call_target="tpu_custom_call" | custom-call | flops 10000000000 | bytes 30000000 | tf_op jit(solution)/shard_map/final/pallas_call | solution.py:309
Async XLA Ops:
  0.6 14.5 %collective-permute-start.1 = (bf16[576,384]{1,0:T(8,128)(2,1)}, bf16[576,384]{1,0:T(8,128)(2,1)S(1)}, u32[]{:S(2)}, u32[]{:S(2)}) collective-permute-start(bf16[576,384]{1,0:T(8,128)(2,1)} %bitcast.23), channel_id=1, source_target_pairs={{0,1},{1,0},{2,3},{3,2},{4,5},{5,4},{6,7},{7,6},{8,9},{9,8},{10,11... | collective-permute-start | bytes 1327112 | tf_op jit(solution)/shard_map/ppermute | solution.py:22
  3.6 9.9 %collective-permute-start.2 = (bf16[576,384]{1,0:T(8,128)(2,1)}, bf16[576,384]{1,0:T(8,128)(2,1)S(1)}, u32[]{:S(2)}, u32[]{:S(2)}) collective-permute-start(bf16[576,384]{1,0:T(8,128)(2,1)} %bitcast.22), channel_id=1, source_target_pairs={{0,30},{1,31},{2,0},{3,1},{4,2},{5,3},{6,4},{7,5},{8,6},{9,7},{10,... | collective-permute-start | bytes 1327112 | tf_op jit(solution)/shard_map/ppermute | solution.py:22
  12.2 10.4 %collective-permute-start = (bf16[576,384]{1,0:T(8,128)(2,1)S(1)}, bf16[576,384]{1,0:T(8,128)(2,1)S(1)}, u32[]{:S(2)}, u32[]{:S(2)}) collective-permute-start(bf16[576,384]{1,0:T(8,128)(2,1)S(1)} %get-tuple-element.42), channel_id=1, source_target_pairs={{0,30},{1,31},{2,0},{3,1},{4,2},{5,3},{6,4},{7,5},{8,6},{9,7},{10,... | collective-permute-start | bytes 1327112 | tf_op jit(solution)/shard_map/ppermute | solution.py:22
  13.5 14.9 %collective-permute-start.7 = (bf16[576,384]{1,0:T(8,128)(2,1)S(1)}, bf16[576,384]{1,0:T(8,128)(2,1)S(1)}, u32[]{:S(2)}, u32[]{:S(2)}) collective-permute-start(bf16[576,384]{1,0:T(8,128)(2,1)S(1)} %collective-permute-done.2.c_ref.c0_ref), channel_id=1, source_target_pairs={{0,1},{1,0},{2,3},{3,2},{4,5},{5,4},{6,7},{7,6},{8,9},{9,8},{10,11... | collective-permute-start | bytes 1327112 | tf_op jit(solution)/shard_map/ppermute | solution.py:22
  18.3 10.1 %collective-permute-start.6 = (bf16[576,384]{1,0:T(8,128)(2,1)S(1)}, bf16[576,384]{1,0:T(8,128)(2,1)S(1)}, u32[]{:S(2)}, u32[]{:S(2)}) collective-permute-start(bf16[576,384]{1,0:T(8,128)(2,1)S(1)} %get-tuple-element.48), channel_id=1, source_target_pairs={{0,30},{1,31},{2,0},{3,1},{4,2},{5,3},{6,4},{7,5},{8,6},{9,7},{10,... | collective-permute-start | bytes 1327112 | tf_op jit(solution)/shard_map/ppermute | solution.py:22
  27.0 8.8 %collective-permute-start.4 = (bf16[288,384]{1,0:T(8,128)(2,1)S(1)}, bf16[288,384]{1,0:T(8,128)(2,1)S(1)}, u32[]{:S(2)}, u32[]{:S(2)}) collective-permute-start(bf16[288,384]{1,0:T(8,128)(2,1)S(1)} %get-tuple-element.56), channel_id=1, source_target_pairs={{0,2},{1,3},{2,4},{3,5},{4,6},{5,7},{6,8},{7,9},{8,10},{9,11},{10,... | collective-permute-start | bytes 663560 | tf_op jit(solution)/shard_map/ppermute | solution.py:22
  27.1 10.4 %collective-permute-start.5 = (bf16[288,384]{1,0:T(8,128)(2,1)S(1)}, bf16[288,384]{1,0:T(8,128)(2,1)S(1)}, u32[]{:S(2)}, u32[]{:S(2)}) collective-permute-start(bf16[288,384]{1,0:T(8,128)(2,1)S(1)} %get-tuple-element.57), channel_id=1, source_target_pairs={{0,2},{1,3},{2,4},{3,5},{4,6},{5,7},{6,8},{7,9},{8,10},{9,11},{10,... | collective-permute-start | bytes 663560 | tf_op jit(solution)/shard_map/ppermute | solution.py:22
  27.2 16.0 %collective-permute-start.3 = (bf16[576,384]{1,0:T(8,128)(2,1)S(1)}, bf16[576,384]{1,0:T(8,128)(2,1)S(1)}, u32[]{:S(2)}, u32[]{:S(2)}) collective-permute-start(bf16[576,384]{1,0:T(8,128)(2,1)S(1)} %get-tuple-element.50), channel_id=1, source_target_pairs={{0,3},{1,2},{2,5},{3,4},{4,7},{5,6},{6,9},{7,8},{8,11},{9,10},{10,... | collective-permute-start | bytes 1327112 | tf_op jit(solution)/shard_map/ppermute | solution.py:22

commit v12 on v11

--- a/solution.py
+++ b/solution.py
@@ -119,7 +119,7 @@
         da_ref[:, hc] = dot(ct, down_ref[:, hc])
 
 
-def second_kernel(h_ref, c_ref, gate_ref, up_ref, da_ref, d_ref, d_lo_ref, d_hi_ref, z_ref, act_ref, dg_ref, du_ref):
+def second_kernel(h_ref, c_ref, gate_ref, up_ref, da_ref, d_first_ref, d_last_ref, d_lo_ref, d_hi_ref, z_ref, act_ref, dg_ref, du_ref):
     inverse, normed = normalize(h_ref[...].astype(F32))
     zed = normed.astype(BF16)
     z_ref[...] = zed
@@ -137,7 +137,9 @@
     staggered(chunks(gate_ref.shape[1]), ahead, use)
     dz = dot(gate_ref[...], dg_ref[...], NT) + dot(up_ref[...], du_ref[...], NT)
     d = input_cotangent(c_ref[...].astype(F32), dz, inverse, normed)
-    d_ref[...] = d
+    cut = d_first_ref.shape[1]
+    d_first_ref[...] = d[:, :cut]
+    d_last_ref[...] = d[:, cut:]
     half = d_lo_ref.shape[0]
     d_lo_ref[...] = d[:half]
     d_hi_ref[...] = d[half:]
@@ -201,6 +203,25 @@
     d_ref[...] = input_cotangent(whole_c.astype(F32), dz, inverse, normed)
 
 
+def add_kernel(c_ref, z_ref, act_ref, p_ref, q_ref, down_ref, pg_ref, pu_ref, pd_ref, gg_ref, gu_ref, gd_ref):
+    c = c_ref[...]
+    cut = c.shape[1]
+    z = z_ref[:, :cut]
+    ct = c.T
+
+    def ahead(hc):
+        return dot(ct, down_ref[:, hc])
+
+    def use(hc, da):
+        dgate = (da * p_ref[:cut, hc].astype(F32)).astype(BF16)
+        dup = (da * q_ref[:cut, hc].astype(F32)).astype(BF16)
+        gd_ref[:, hc] = (pd_ref[:, hc].astype(F32) + dot(c, act_ref[:cut, hc])).astype(BF16)
+        gg_ref[:, hc] = (pg_ref[:, hc].astype(F32) + dot(z, dgate)).astype(BF16)
+        gu_ref[:, hc] = (pu_ref[:, hc].astype(F32) + dot(z, dup)).astype(BF16)
+
+    staggered(chunks(gg_ref.shape[1]), ahead, use)
+
+
 def final_kernel(
     c_ref, z_ref, act_ref, p_ref, q_ref, down_ref, pg_ref, pu_ref, pd_ref, dx_ref, c2_lo_ref, c2_hi_ref, z2_ref, act2_ref, dg2_ref, du2_ref,
     gg_hbm, gu_hbm, gd_hbm, dx_hbm, gg_ref, gu_ref, gd_ref, sem,
@@ -211,7 +232,7 @@
     cut = whole_tiles(act_ref.shape[0])
     c2 = jnp.concatenate([c2_lo_ref[:, cut:], c2_hi_ref[:, cut:]], axis=0)
     c = jnp.concatenate([c2, c_ref[...]], axis=1)
-    z = jnp.concatenate([z2_ref[:, cut:], z_ref[...]], axis=1)
+    z = jnp.concatenate([z2_ref[:, cut:], z_ref[:, cut:]], axis=1)
     parts = chunks(gg_ref.shape[1])
 
     def add(hc, m, left, right, part_ref, ref, hbm):
@@ -224,9 +245,9 @@
         return dot(ct, down_ref[:, hc])
 
     def use(hc, da):
-        add(hc, 2, c, stack(act2_ref[cut:, hc], act_ref[:, hc]), pd_ref, gd_ref, gd_hbm)
-        add(hc, 0, z, stack(dg2_ref[cut:, hc], da * p_ref[:, hc].astype(F32)), pg_ref, gg_ref, gg_hbm)
-        add(hc, 1, z, stack(du2_ref[cut:, hc], da * q_ref[:, hc].astype(F32)), pu_ref, gu_ref, gu_hbm)
+        add(hc, 2, c, stack(act2_ref[cut:, hc], act_ref[cut:, hc]), pd_ref, gd_ref, gd_hbm)
+        add(hc, 0, z, stack(dg2_ref[cut:, hc], da * p_ref[cut:, hc].astype(F32)), pg_ref, gg_ref, gg_hbm)
+        add(hc, 1, z, stack(du2_ref[cut:, hc], da * q_ref[cut:, hc].astype(F32)), pu_ref, gu_ref, gu_hbm)
 
     staggered(parts, ahead, use)
     for copy in copies:
@@ -287,7 +308,8 @@
 def second(v, c, gate, up, da):
     d, t = v.shape
     h = gate.shape[1]
-    shapes = [(d, t), (d // 2, t), (d - d // 2, t), (d, t), (t, h), (t, h), (t, h)]
+    cut = whole_tiles(t)
+    shapes = [(d, cut), (d, t - cut), (d // 2, t), (d - d // 2, t), (d, t), (t, h), (t, h), (t, h)]
     return whole(second_kernel, (v, c, gate, up, da), shapes, "second_own")
 
 
@@ -301,6 +323,10 @@
     h = w[0].shape[1]
     shapes = [(d, t), (t, h), (t, h)] + [(d, h)] * 3
     return whole(first_back_kernel, (x, *c, p, q, *w, z, act, *parts), shapes, "first_back_own")
+
+
+def add(c, z, act, p, q, down, parts):
+    return whole(add_kernel, (c, z, act, p, q, down, *parts), [down.shape] * 3, "add_other")
 
 
 def final(c, z, act, p, q, down, parts, dx, held):
@@ -329,12 +355,14 @@
     x_o = after(x_o, da_b)
     h_o, z3, act3, p3, q3 = first(x_o, w, "first_other")
     h_bo = shift(h_o, -1)
-    d_b, *d_halves, z0, act0, dg0, du0 = second(after(h_b, h_o), g_b, w[0], w[1], da_b)
+    d_first, d_last, *d_halves, z0, act0, dg0, du0 = second(after(h_b, h_o), g_b, w[0], w[1], da_b)
     d = [shift(part, 1) for part in d_halves]
-    d_o = shift(d_b, 1, True)
-    parts = second_grads(after(h_bo, d_b), g_bo, w, (z0, g_b, act0, dg0, du0))
+    o_first = shift(d_first, 1, True)
+    o_last = shift(after(d_last, h_bo), 1, True)
+    parts = second_grads(after(h_bo, d_first), g_bo, w, (z0, g_b, act0, dg0, du0))
     dx, dg2, du2, *parts = first_back(x, d, p2, q2, w, z2, act2, parts)
-    gg, gu, gd, dx = final(d_o, z3, act3, p3, q3, w[2], parts, dx, (*d, z2, act2, dg2, du2))
+    parts = add(o_first, z3, act3, p3, q3, w[2], parts)
+    gg, gu, gd, dx = final(o_last, z3, act3, p3, q3, w[2], parts, dx, (*d, z2, act2, dg2, du2))
     return dx.T[None], gg[None], gu[None], gd.T[None]
 
 

time: 48.4 us -> 48 us (level)
  waiting for transfers between devices: 3.91 us -> 3.16 us
  Pallas kernels: 30.6 us -> 31.1 us
    pallas_call x5 -> x6, Pallas kernels: 20.8 us -> 23.2 us  [whole(): pl.pallas_call(kernel, in_specs=[spec] * len(args), out_specs=[spec] * le...]
    pallas_call x1, Pallas kernels: 4.89 us -> 3.04 us  [final(): pl.pallas_call(final_kernel, in_specs=[pl.BlockSpec(memory_space=pltpu.VM...]
    ppermute x8 -> x9, waiting for transfers between devices: 3.91 us -> 3.16 us  [shift(): return lax.ppermute(x, ('blk', 'dp'), pairs)]
    ppermute x8 -> x9, starting transfers between devices: 12.9 us -> 12.7 us  [shift(): return lax.ppermute(x, ('blk', 'dp'), pairs)]
  transfers between devices with their start and end apart: 8 -> 9, of which waited for: 4 -> 3; matrix products, arithmetic and copies ran while one was open for 0% -> 0% of each run, Pallas kernels for 53% -> 59%
where the time goes in v12:
time: 48 us; the launch traced here: 47.8 us
  Pallas kernels  31.1 us (65%)
  starting transfers between devices  12.7 us (26%)
  waiting for transfers between devices  3.16 us (7%)
  between operations  0.9 us (2%)
    pallas_call x6, Pallas kernels, whole(): pl.pallas_call(kernel, in_specs=[spec] * len(args), out_specs=[spec] * le...  23.2 us
    ppermute x9, starting transfers between devices, shift(): return lax.ppermute(x, ('blk', 'dp'), pairs)  12.7 us
    pallas_call x1, Pallas kernels, loading_first(): pl.pallas_call(loading_forward_kernel, in_specs=[pl.BlockSpec(memory_spac...  4.86 us
    ppermute x9, waiting for transfers between devices, shift(): return lax.ppermute(x, ('blk', 'dp'), pairs)  3.16 us
    pallas_call x1, Pallas kernels, final(): pl.pallas_call(final_kernel, in_specs=[pl.BlockSpec(memory_space=pltpu.VM...  3.04 us
  transfers between devices with their start and end apart: 9, of which 3 were waited for; matrix products, arithmetic and copies ran while one was open for 0% of the time, Pallas kernels for 59%

profile of v12, /device:TPU:0, one launch (start us, length us, event | category | flops | bytes accessed | tf_op | source)
XLA Modules:
  0.0 47.8 jit_solution(13950359419101047795)
XLA Ops:
  0.6 3.0 %collective-permute-start.1 = (bf16[576,384]{1,0:T(8,128)(2,1)}, bf16[576,384]{1,0:T(8,128)(2,1)S(1)}, u32[]{:S(2)}, u32[]{:S(2)}) collective-permute-start(bf16[576,384]{1,0:T(8,128)(2,1)} %bitcast.23), channel_id=1, source_target_pairs={{0,1},{1,0},{2,3},{3,2},{4,5},{5,4},{6,7},{7,6},{8,9},{9,8},{10,11... | collective-permute-start | bytes 1327112 | tf_op jit(solution)/shard_map/ppermute | solution.py:22
  3.6 3.7 %collective-permute-start.2 = (bf16[576,384]{1,0:T(8,128)(2,1)}, bf16[576,384]{1,0:T(8,128)(2,1)S(1)}, u32[]{:S(2)}, u32[]{:S(2)}) collective-permute-start(bf16[576,384]{1,0:T(8,128)(2,1)} %bitcast.22), channel_id=1, source_target_pairs={{0,30},{1,31},{2,0},{3,1},{4,2},{5,3},{6,4},{7,5},{8,6},{9,7},{10,... | collective-permute-start | bytes 1327112 | tf_op jit(solution)/shard_map/ppermute | solution.py:22
  7.4 4.9 %first_own.1 = (bf16[576,384]{1,0:T(8,128)(2,1)S(1)}, bf16[576,384]{1,0:T(8,128)(2,1)S(1)}, bf16[384,1536]{1,0:T(8,128)(2,1)S(1)}, bf16[384,1536]{1,0:T(8,128)(2...) custom-call(bf16[576,384]{1,0:T(8,128)(2,1)} %bitcast.24, ...), custom_call_target="tpu_custom_call" | custom-call | flops 10000000000 | bytes 30000000 | tf_op jit(solution)/shard_map/first_own/pallas_call | solution.py:292
  12.2 1.0 %collective-permute-start = (bf16[576,384]{1,0:T(8,128)(2,1)S(1)}, bf16[576,384]{1,0:T(8,128)(2,1)S(1)}, u32[]{:S(2)}, u32[]{:S(2)}) collective-permute-start(bf16[576,384]{1,0:T(8,128)(2,1)S(1)} %get-tuple-element.47), channel_id=1, source_target_pairs={{0,30},{1,31},{2,0},{3,1},{4,2},{5,3},{6,4},{7,5},{8,6},{9,7},{10,... | collective-permute-start | bytes 1327112 | tf_op jit(solution)/shard_map/ppermute | solution.py:22
  13.2 0.3 collective-permute-done.2.c_ref.c0_ref
  13.5 0.5 %collective-permute-start.8 = (bf16[576,384]{1,0:T(8,128)(2,1)S(1)}, bf16[576,384]{1,0:T(8,128)(2,1)S(1)}, u32[]{:S(2)}, u32[]{:S(2)}) collective-permute-start(bf16[576,384]{1,0:T(8,128)(2,1)S(1)} %collective-permute-done.2.c_ref.c0_ref), channel_id=1, source_target_pairs={{0,1},{1,0},{2,3},{3,2},{4,5},{5,4},{6,7},{7,6},{8,9},{9,8},{10,11... | collective-permute-start | bytes 1327112 | tf_op jit(solution)/shard_map/ppermute | solution.py:22
  14.0 1.1 %hidden_cotangent.1.da_ref = f32[384,1536]{1,0:T(8,128)S(1)} custom-call(bf16[576,384]{1,0:T(8,128)(2,1)S(1)} %collective-permute-done.2.c_ref.c0_ref, bf16[576,1536]{1,0:T(8,128)(2,1)S(1)} %get-tuple-element.49.down_ref.refs_3_), custom_call_target="tpu_custom_call" | custom-call | flops 10000000000 | bytes 30000000 | tf_op jit(solution)/shard_map/hidden_cotangent/pallas_call | solution.py:271
  15.1 0.0 collective-permute-done.1.refs_0_
  15.1 3.2 %first_other.1 = (bf16[576,384]{1,0:T(8,128)(2,1)S(1)}, bf16[576,384]{1,0:T(8,128)(2,1)S(1)}, bf16[384,1536]{1,0:T(8,128)(2,1)S(1)}, bf16[384,1536]{1,0:T(8,128)(2,1)S(1)}, bf16[384,1536]{1,0:T(8,128)(2,1)S(1)}) custom-call(bf16[576,384]{1,0:T(8,128)(2,1)S(1)} %collective-permute-done.1.refs_0_, bf16[576,1536]{1,0:T(8,128)(2,1)S(1)} %get-tuple-element.51.refs_1_.gate_ref, ...), custom_call_target="tpu_custom_call" | custom-call | flops 10000000000 | bytes 30000000 | tf_op jit(solution)/shard_map/first_other/pallas_call | solution.py:271
  18.3 4.3 %collective-permute-start.3 = (bf16[576,384]{1,0:T(8,128)(2,1)S(1)}, bf16[576,384]{1,0:T(8,128)(2,1)S(1)}, u32[]{:S(2)}, u32[]{:S(2)}) collective-permute-start(bf16[576,384]{1,0:T(8,128)(2,1)S(1)} %get-tuple-element.53), channel_id=1, source_target_pairs={{0,30},{1,31},{2,0},{3,1},{4,2},{5,3},{6,4},{7,5},{8,6},{9,7},{10,... | collective-permute-start | bytes 1327112 | tf_op jit(solution)/shard_map/ppermute | solution.py:22
  22.6 0.0 collective-permute-done.h_ref
  22.6 4.4 %second_own.1 = (bf16[576,256]{1,0:T(8,128)(2,1)S(1)}, bf16[576,128]{1,0:T(8,128)(2,1)S(1)}, bf16[288,384]{1,0:T(8,128)(2,1)S(1)}, bf16[288,384]{1,0:T(8,128)(2,...) custom-call(bf16[576,384]{1,0:T(8,128)(2,1)S(1)} %collective-permute, ...), custom_call_target="tpu_custom_call" | custom-call | flops 10000000000 | bytes 30000000 | tf_op jit(solution)/shard_map/second_own/pallas_call | solution.py:271
  27.0 0.1 collective-permute-start.6
  27.1 0.1 collective-permute-start.7
  27.1 0.1 collective-permute-start.5
  27.2 1.2 %collective-permute-done.3.h_ref = bf16[576,384]{1,0:T(8,128)(2,1)S(1)} collective-permute-done((bf16[576,384]{1,0:T(8,128)(2,1)S(1)}, bf16[576,384]{1,0:T(8,128)(2,1)S(1)}, u32[]{:S(2)}, u32[]{:S(2)}) %collective-permute-start.3) | collective-permute-done | bytes 442400 | tf_op jit(solution)/shard_map/ppermute | solution.py:22
  28.4 0.0 collective-permute-start.4
  28.4 0.0 collective-permute-done.8.c_ref
  28.4 7.4 %second_grads.1 = (bf16[576,1536]{1,0:T(8,128)(2,1)S(1)}, bf16[576,1536]{1,0:T(8,128)(2,1)S(1)}, bf16[576,1536]{1,0:T(8,128)(2,1)S(1)}) custom-call(bf16[576,384]{1,0:T(8,128)(2,1)S(1)} %collective-permute-done.3.h_ref, bf16[576,384]{1,0:T(8,128)(2,1)S(1)} %collective-permute-done.8.c_ref, bf16[576,1536]{1,0:T(8,128)(2,1)S(1)} %get-tuple-element.51.refs_1_.gate_ref, ...), custom_call_target="tpu_custom_call" | custom-call | flops 10000000000 | bytes 30000000 | tf_op jit(solution)/shard_map/second_grads/pallas_call | solution.py:271
  35.8 0.0 collective-permute-done.6.c_lo_ref.c2_lo_ref
  35.8 1.7 %collective-permute-done.7.c_hi_ref.c2_hi_ref = bf16[288,384]{1,0:T(8,128)(2,1)S(1)} collective-permute-done((bf16[288,384]{1,0:T(8,128)(2,1)S(1)}, bf16[288,384]{1,0:T(8,128)(2,1)S(1)}, u32[]{:S(2)}, u32[]{:S(2)}) %collective-permute-start.7) | collective-permute-done | bytes 221216 | tf_op jit(solution)/shard_map/ppermute | solution.py:22
  37.5 4.7 %first_back_own.1 = (bf16[576,384]{1,0:T(8,128)(2,1)S(1)}, bf16[384,1536]{1,0:T(8,128)(2,1)S(1)}, bf16[384,1536]{1,0:T(8,128)(2,1)S(1)}, bf16[576,1536]{1,0:T(8,...) custom-call(bf16[576,384]{1,0:T(8,128)(2,1)S(1)} %get-tuple-element.62.x_ref, ...), custom_call_target="tpu_custom_call" | custom-call | flops 10000000000 | bytes 30000000 | tf_op jit(solution)/shard_map/first_back_own/pallas_call | solution.py:271
  42.2 0.0 collective-permute-done.5.c_ref
  42.3 2.4 %add_other.1 = (bf16[576,1536]{1,0:T(8,128)(2,1)S(1)}, bf16[576,1536]{1,0:T(8,128)(2,1)S(1)}, bf16[576,1536]{1,0:T(8,128)(2,1)S(1)}) custom-call(bf16[576,256]{1,0:T(8,128)(2,1)S(1)} %collective-permute-done.5.c_ref, bf16[576,384]{1,0:T(8,128)(2,1)S(1)} %get-tuple-element.57.z_ref, bf16[384,1536]{1,0:T(8,128)(2,1)S(1)} %get-tuple-element.58.act_ref, ...), custom_call_target="tpu_custom_call" | custom-call | flops 10000000000 | bytes 30000000 | tf_op jit(solution)/shard_map/add_other/pallas_call | solution.py:271
  44.6 0.0 collective-permute-done.4.c_ref
  44.6 3.0 %final.1 = (bf16[576,1536]{1,0:T(8,128)(2,1)}, bf16[576,1536]{1,0:T(8,128)(2,1)}, bf16[576,1536]{1,0:T(8,128)(2,1)}, bf16[576,384]{1,0:T(8,128)(2,1)}) custom-call(bf16[576,128]{1,0:T(8,128)(2,1)S(1)} %collective-permute-done.4.c_ref, bf16[576,384]{1,0:T(8,128)(2,1)S(1)} %get-tuple-element.57.z_ref, bf16[384,1536]{1,0:T(8,128)(2,1)S(1)} %get-tuple-element.58.act_ref, ...), custom_call_target="tpu_custom_call" | custom-call | flops 10000000000 | bytes 30000000 | tf_op jit(solution)/shard_map/final/pallas_call | solution.py:335
Async XLA Ops:
  0.6 14.5 %collective-permute-start.1 = (bf16[576,384]{1,0:T(8,128)(2,1)}, bf16[576,384]{1,0:T(8,128)(2,1)S(1)}, u32[]{:S(2)}, u32[]{:S(2)}) collective-permute-start(bf16[576,384]{1,0:T(8,128)(2,1)} %bitcast.23), channel_id=1, source_target_pairs={{0,1},{1,0},{2,3},{3,2},{4,5},{5,4},{6,7},{7,6},{8,9},{9,8},{10,11... | collective-permute-start | bytes 1327112 | tf_op jit(solution)/shard_map/ppermute | solution.py:22
  3.6 9.9 %collective-permute-start.2 = (bf16[576,384]{1,0:T(8,128)(2,1)}, bf16[576,384]{1,0:T(8,128)(2,1)S(1)}, u32[]{:S(2)}, u32[]{:S(2)}) collective-permute-start(bf16[576,384]{1,0:T(8,128)(2,1)} %bitcast.22), channel_id=1, source_target_pairs={{0,30},{1,31},{2,0},{3,1},{4,2},{5,3},{6,4},{7,5},{8,6},{9,7},{10,... | collective-permute-start | bytes 1327112 | tf_op jit(solution)/shard_map/ppermute | solution.py:22
  12.2 10.4 %collective-permute-start = (bf16[576,384]{1,0:T(8,128)(2,1)S(1)}, bf16[576,384]{1,0:T(8,128)(2,1)S(1)}, u32[]{:S(2)}, u32[]{:S(2)}) collective-permute-start(bf16[576,384]{1,0:T(8,128)(2,1)S(1)} %get-tuple-element.47), channel_id=1, source_target_pairs={{0,30},{1,31},{2,0},{3,1},{4,2},{5,3},{6,4},{7,5},{8,6},{9,7},{10,... | collective-permute-start | bytes 1327112 | tf_op jit(solution)/shard_map/ppermute | solution.py:22
  13.5 14.9 %collective-permute-start.8 = (bf16[576,384]{1,0:T(8,128)(2,1)S(1)}, bf16[576,384]{1,0:T(8,128)(2,1)S(1)}, u32[]{:S(2)}, u32[]{:S(2)}) collective-permute-start(bf16[576,384]{1,0:T(8,128)(2,1)S(1)} %collective-permute-done.2.c_ref.c0_ref), channel_id=1, source_target_pairs={{0,1},{1,0},{2,3},{3,2},{4,5},{5,4},{6,7},{7,6},{8,9},{9,8},{10,11... | collective-permute-start | bytes 1327112 | tf_op jit(solution)/shard_map/ppermute | solution.py:22
  18.3 10.1 %collective-permute-start.3 = (bf16[576,384]{1,0:T(8,128)(2,1)S(1)}, bf16[576,384]{1,0:T(8,128)(2,1)S(1)}, u32[]{:S(2)}, u32[]{:S(2)}) collective-permute-start(bf16[576,384]{1,0:T(8,128)(2,1)S(1)} %get-tuple-element.53), channel_id=1, source_target_pairs={{0,30},{1,31},{2,0},{3,1},{4,2},{5,3},{6,4},{7,5},{8,6},{9,7},{10,... | collective-permute-start | bytes 1327112 | tf_op jit(solution)/shard_map/ppermute | solution.py:22
  27.0 8.8 %collective-permute-start.6 = (bf16[288,384]{1,0:T(8,128)(2,1)S(1)}, bf16[288,384]{1,0:T(8,128)(2,1)S(1)}, u32[]{:S(2)}, u32[]{:S(2)}) collective-permute-start(bf16[288,384]{1,0:T(8,128)(2,1)S(1)} %get-tuple-element.63), channel_id=1, source_target_pairs={{0,2},{1,3},{2,4},{3,5},{4,6},{5,7},{6,8},{7,9},{8,10},{9,11},{10,... | collective-permute-start | bytes 663560 | tf_op jit(solution)/shard_map/ppermute | solution.py:22
  27.1 10.4 %collective-permute-start.7 = (bf16[288,384]{1,0:T(8,128)(2,1)S(1)}, bf16[288,384]{1,0:T(8,128)(2,1)S(1)}, u32[]{:S(2)}, u32[]{:S(2)}) collective-permute-start(bf16[288,384]{1,0:T(8,128)(2,1)S(1)} %get-tuple-element.64), channel_id=1, source_target_pairs={{0,2},{1,3},{2,4},{3,5},{4,6},{5,7},{6,8},{7,9},{8,10},{9,11},{10,... | collective-permute-start | bytes 663560 | tf_op jit(solution)/shard_map/ppermute | solution.py:22
  27.1 15.1 %collective-permute-start.5 = (bf16[576,256]{1,0:T(8,128)(2,1)S(1)}, bf16[576,256]{1,0:T(8,128)(2,1)S(1)}, u32[]{:S(2)}, u32[]{:S(2)}) collective-permute-start(bf16[576,256]{1,0:T(8,128)(2,1)S(1)} %get-tuple-element.61), channel_id=1, source_target_pairs={{0,3},{1,2},{2,5},{3,4},{4,7},{5,6},{6,9},{7,8},{8,11},{9,10},{10,... | collective-permute-start | bytes 884744 | tf_op jit(solution)/shard_map/ppermute | solution.py:22
  28.4 16.2 %collective-permute-start.4 = (bf16[576,128]{1,0:T(8,128)(2,1)S(1)}, bf16[576,128]{1,0:T(8,128)(2,1)S(1)}, u32[]{:S(2)}, u32[]{:S(2)}) collective-permute-start(bf16[576,128]{1,0:T(8,128)(2,1)S(1)} %get-tuple-element.56), channel_id=1, source_target_pairs={{0,3},{1,2},{2,5},{3,4},{4,7},{5,6},{6,9},{7,8},{8,11},{9,10},{10,... | collective-permute-start | bytes 442376 | tf_op jit(solution)/shard_map/ppermute | solution.py:22

commit v13 on v12

--- a/solution.py
+++ b/solution.py
@@ -308,8 +308,8 @@
 def second(v, c, gate, up, da):
     d, t = v.shape
     h = gate.shape[1]
-    cut = whole_tiles(t)
-    shapes = [(d, cut), (d, t - cut), (d // 2, t), (d - d // 2, t), (d, t), (t, h), (t, h), (t, h)]
+    cut, most = whole_tiles(t), d * 7 // 9
+    shapes = [(d, cut), (d, t - cut), (most, t), (d - most, t), (d, t), (t, h), (t, h), (t, h)]
     return whole(second_kernel, (v, c, gate, up, da), shapes, "second_own")
 
 

time: 48 us -> 52.1 us (1.085)
  waiting for transfers between devices: 3.16 us -> 7.26 us
    ppermute x9, waiting for transfers between devices: 3.16 us -> 7.26 us  [shift(): return lax.ppermute(x, ('blk', 'dp'), pairs)]
  transfers between devices with their start and end apart: 9 -> 9, of which waited for: 3 -> 3; matrix products, arithmetic and copies ran while one was open for 0% -> 0% of each run, Pallas kernels for 59% -> 54%
where the time goes in v13:
time: 52.1 us; the launch traced here: 51.9 us
  Pallas kernels  31 us (60%)
  starting transfers between devices  12.7 us (24%)
  waiting for transfers between devices  7.26 us (14%)
  between operations  0.9 us (2%)
    pallas_call x6, Pallas kernels, whole(): pl.pallas_call(kernel, in_specs=[spec] * len(args), out_specs=[spec] * le...  23.1 us
    ppermute x9, starting transfers between devices, shift(): return lax.ppermute(x, ('blk', 'dp'), pairs)  12.7 us
    ppermute x9, waiting for transfers between devices, shift(): return lax.ppermute(x, ('blk', 'dp'), pairs)  7.26 us
    pallas_call x1, Pallas kernels, loading_first(): pl.pallas_call(loading_forward_kernel, in_specs=[pl.BlockSpec(memory_spac...  4.86 us
    pallas_call x1, Pallas kernels, final(): pl.pallas_call(final_kernel, in_specs=[pl.BlockSpec(memory_space=pltpu.VM...  3.04 us
  transfers between devices with their start and end apart: 9, of which 3 were waited for; matrix products, arithmetic and copies ran while one was open for 0% of the time, Pallas kernels for 54%

profile of v13, /device:TPU:0, one launch (start us, length us, event | category | flops | bytes accessed | tf_op | source)
XLA Modules:
  0.0 51.9 jit_solution(1787997837074431633)
XLA Ops:
  0.6 3.0 %collective-permute-start.1 = (bf16[576,384]{1,0:T(8,128)(2,1)}, bf16[576,384]{1,0:T(8,128)(2,1)S(1)}, u32[]{:S(2)}, u32[]{:S(2)}) collective-permute-start(bf16[576,384]{1,0:T(8,128)(2,1)} %bitcast.23), channel_id=1, source_target_pairs={{0,1},{1,0},{2,3},{3,2},{4,5},{5,4},{6,7},{7,6},{8,9},{9,8},{10,11... | collective-permute-start | bytes 1327112 | tf_op jit(solution)/shard_map/ppermute | solution.py:22
  3.6 3.7 %collective-permute-start.2 = (bf16[576,384]{1,0:T(8,128)(2,1)}, bf16[576,384]{1,0:T(8,128)(2,1)S(1)}, u32[]{:S(2)}, u32[]{:S(2)}) collective-permute-start(bf16[576,384]{1,0:T(8,128)(2,1)} %bitcast.22), channel_id=1, source_target_pairs={{0,30},{1,31},{2,0},{3,1},{4,2},{5,3},{6,4},{7,5},{8,6},{9,7},{10,... | collective-permute-start | bytes 1327112 | tf_op jit(solution)/shard_map/ppermute | solution.py:22
  7.4 4.9 %first_own.1 = (bf16[576,384]{1,0:T(8,128)(2,1)S(1)}, bf16[576,384]{1,0:T(8,128)(2,1)S(1)}, bf16[384,1536]{1,0:T(8,128)(2,1)S(1)}, bf16[384,1536]{1,0:T(8,128)(2...) custom-call(bf16[576,384]{1,0:T(8,128)(2,1)} %bitcast.24, ...), custom_call_target="tpu_custom_call" | custom-call | flops 10000000000 | bytes 30000000 | tf_op jit(solution)/shard_map/first_own/pallas_call | solution.py:292
  12.2 1.0 %collective-permute-start = (bf16[576,384]{1,0:T(8,128)(2,1)S(1)}, bf16[576,384]{1,0:T(8,128)(2,1)S(1)}, u32[]{:S(2)}, u32[]{:S(2)}) collective-permute-start(bf16[576,384]{1,0:T(8,128)(2,1)S(1)} %get-tuple-element.47), channel_id=1, source_target_pairs={{0,30},{1,31},{2,0},{3,1},{4,2},{5,3},{6,4},{7,5},{8,6},{9,7},{10,... | collective-permute-start | bytes 1327112 | tf_op jit(solution)/shard_map/ppermute | solution.py:22
  13.2 0.3 collective-permute-done.2.c_ref.c0_ref
  13.5 0.5 %collective-permute-start.8 = (bf16[576,384]{1,0:T(8,128)(2,1)S(1)}, bf16[576,384]{1,0:T(8,128)(2,1)S(1)}, u32[]{:S(2)}, u32[]{:S(2)}) collective-permute-start(bf16[576,384]{1,0:T(8,128)(2,1)S(1)} %collective-permute-done.2.c_ref.c0_ref), channel_id=1, source_target_pairs={{0,1},{1,0},{2,3},{3,2},{4,5},{5,4},{6,7},{7,6},{8,9},{9,8},{10,11... | collective-permute-start | bytes 1327112 | tf_op jit(solution)/shard_map/ppermute | solution.py:22
  14.0 1.1 %hidden_cotangent.1.da_ref = f32[384,1536]{1,0:T(8,128)S(1)} custom-call(bf16[576,384]{1,0:T(8,128)(2,1)S(1)} %collective-permute-done.2.c_ref.c0_ref, bf16[576,1536]{1,0:T(8,128)(2,1)S(1)} %get-tuple-element.49.down_ref.refs_3_), custom_call_target="tpu_custom_call" | custom-call | flops 10000000000 | bytes 30000000 | tf_op jit(solution)/shard_map/hidden_cotangent/pallas_call | solution.py:271
  15.1 0.0 collective-permute-done.1.refs_0_
  15.1 3.2 %first_other.1 = (bf16[576,384]{1,0:T(8,128)(2,1)S(1)}, bf16[576,384]{1,0:T(8,128)(2,1)S(1)}, bf16[384,1536]{1,0:T(8,128)(2,1)S(1)}, bf16[384,1536]{1,0:T(8,128)(2,1)S(1)}, bf16[384,1536]{1,0:T(8,128)(2,1)S(1)}) custom-call(bf16[576,384]{1,0:T(8,128)(2,1)S(1)} %collective-permute-done.1.refs_0_, bf16[576,1536]{1,0:T(8,128)(2,1)S(1)} %get-tuple-element.51.refs_1_.gate_ref, ...), custom_call_target="tpu_custom_call" | custom-call | flops 10000000000 | bytes 30000000 | tf_op jit(solution)/shard_map/first_other/pallas_call | solution.py:271
  18.3 4.3 %collective-permute-start.3 = (bf16[576,384]{1,0:T(8,128)(2,1)S(1)}, bf16[576,384]{1,0:T(8,128)(2,1)S(1)}, u32[]{:S(2)}, u32[]{:S(2)}) collective-permute-start(bf16[576,384]{1,0:T(8,128)(2,1)S(1)} %get-tuple-element.53), channel_id=1, source_target_pairs={{0,30},{1,31},{2,0},{3,1},{4,2},{5,3},{6,4},{7,5},{8,6},{9,7},{10,... | collective-permute-start | bytes 1327112 | tf_op jit(solution)/shard_map/ppermute | solution.py:22
  22.6 0.0 collective-permute-done.h_ref
  22.6 4.4 %second_own.1 = (bf16[576,256]{1,0:T(8,128)(2,1)S(1)}, bf16[576,128]{1,0:T(8,128)(2,1)S(1)}, bf16[448,384]{1,0:T(8,128)(2,1)S(1)}, bf16[128,384]{1,0:T(8,128)(2,...) custom-call(bf16[576,384]{1,0:T(8,128)(2,1)S(1)} %collective-permute, ...), custom_call_target="tpu_custom_call" | custom-call | flops 10000000000 | bytes 30000000 | tf_op jit(solution)/shard_map/second_own/pallas_call | solution.py:271
  27.0 0.1 collective-permute-start.7
  27.1 0.1 collective-permute-start.5
  27.1 0.1 collective-permute-start.6
  27.2 1.2 %collective-permute-done.3.h_ref = bf16[576,384]{1,0:T(8,128)(2,1)S(1)} collective-permute-done((bf16[576,384]{1,0:T(8,128)(2,1)S(1)}, bf16[576,384]{1,0:T(8,128)(2,1)S(1)}, u32[]{:S(2)}, u32[]{:S(2)}) %collective-permute-start.3) | collective-permute-done | bytes 442400 | tf_op jit(solution)/shard_map/ppermute | solution.py:22
  28.4 0.0 collective-permute-start.4
  28.4 0.0 collective-permute-done.8.c_ref
  28.4 7.4 %second_grads.1 = (bf16[576,1536]{1,0:T(8,128)(2,1)S(1)}, bf16[576,1536]{1,0:T(8,128)(2,1)S(1)}, bf16[576,1536]{1,0:T(8,128)(2,1)S(1)}) custom-call(bf16[576,384]{1,0:T(8,128)(2,1)S(1)} %collective-permute-done.3.h_ref, bf16[576,384]{1,0:T(8,128)(2,1)S(1)} %collective-permute-done.8.c_ref, bf16[576,1536]{1,0:T(8,128)(2,1)S(1)} %get-tuple-element.51.refs_1_.gate_ref, ...), custom_call_target="tpu_custom_call" | custom-call | flops 10000000000 | bytes 30000000 | tf_op jit(solution)/shard_map/second_grads/pallas_call | solution.py:271
  35.8 0.0 collective-permute-done.7.c_hi_ref.c2_hi_ref
  35.8 5.8 %collective-permute-done.6.c_lo_ref.c2_lo_ref = bf16[448,384]{1,0:T(8,128)(2,1)S(1)} collective-permute-done((bf16[448,384]{1,0:T(8,128)(2,1)S(1)}, bf16[448,384]{1,0:T(8,128)(2,1)S(1)}, u32[]{:S(2)}, u32[]{:S(2)}) %collective-permute-start.6) | collective-permute-done | bytes 344096 | tf_op jit(solution)/shard_map/ppermute | solution.py:22
  41.6 4.7 %first_back_own.1 = (bf16[576,384]{1,0:T(8,128)(2,1)S(1)}, bf16[384,1536]{1,0:T(8,128)(2,1)S(1)}, bf16[384,1536]{1,0:T(8,128)(2,1)S(1)}, bf16[576,1536]{1,0:T(8,...) custom-call(bf16[576,384]{1,0:T(8,128)(2,1)S(1)} %get-tuple-element.62.x_ref, ...), custom_call_target="tpu_custom_call" | custom-call | flops 10000000000 | bytes 30000000 | tf_op jit(solution)/shard_map/first_back_own/pallas_call | solution.py:271
  46.3 0.0 collective-permute-done.5.c_ref
  46.3 2.4 %add_other.1 = (bf16[576,1536]{1,0:T(8,128)(2,1)S(1)}, bf16[576,1536]{1,0:T(8,128)(2,1)S(1)}, bf16[576,1536]{1,0:T(8,128)(2,1)S(1)}) custom-call(bf16[576,256]{1,0:T(8,128)(2,1)S(1)} %collective-permute-done.5.c_ref, bf16[576,384]{1,0:T(8,128)(2,1)S(1)} %get-tuple-element.57.z_ref, bf16[384,1536]{1,0:T(8,128)(2,1)S(1)} %get-tuple-element.58.act_ref, ...), custom_call_target="tpu_custom_call" | custom-call | flops 10000000000 | bytes 30000000 | tf_op jit(solution)/shard_map/add_other/pallas_call | solution.py:271
  48.7 0.0 collective-permute-done.4.c_ref
  48.7 3.0 %final.1 = (bf16[576,1536]{1,0:T(8,128)(2,1)}, bf16[576,1536]{1,0:T(8,128)(2,1)}, bf16[576,1536]{1,0:T(8,128)(2,1)}, bf16[576,384]{1,0:T(8,128)(2,1)}) custom-call(bf16[576,128]{1,0:T(8,128)(2,1)S(1)} %collective-permute-done.4.c_ref, bf16[576,384]{1,0:T(8,128)(2,1)S(1)} %get-tuple-element.57.z_ref, bf16[384,1536]{1,0:T(8,128)(2,1)S(1)} %get-tuple-element.58.act_ref, ...), custom_call_target="tpu_custom_call" | custom-call | flops 10000000000 | bytes 30000000 | tf_op jit(solution)/shard_map/final/pallas_call | solution.py:335
Async XLA Ops:
  0.6 14.5 %collective-permute-start.1 = (bf16[576,384]{1,0:T(8,128)(2,1)}, bf16[576,384]{1,0:T(8,128)(2,1)S(1)}, u32[]{:S(2)}, u32[]{:S(2)}) collective-permute-start(bf16[576,384]{1,0:T(8,128)(2,1)} %bitcast.23), channel_id=1, source_target_pairs={{0,1},{1,0},{2,3},{3,2},{4,5},{5,4},{6,7},{7,6},{8,9},{9,8},{10,11... | collective-permute-start | bytes 1327112 | tf_op jit(solution)/shard_map/ppermute | solution.py:22
  3.6 9.9 %collective-permute-start.2 = (bf16[576,384]{1,0:T(8,128)(2,1)}, bf16[576,384]{1,0:T(8,128)(2,1)S(1)}, u32[]{:S(2)}, u32[]{:S(2)}) collective-permute-start(bf16[576,384]{1,0:T(8,128)(2,1)} %bitcast.22), channel_id=1, source_target_pairs={{0,30},{1,31},{2,0},{3,1},{4,2},{5,3},{6,4},{7,5},{8,6},{9,7},{10,... | collective-permute-start | bytes 1327112 | tf_op jit(solution)/shard_map/ppermute | solution.py:22
  12.2 10.4 %collective-permute-start = (bf16[576,384]{1,0:T(8,128)(2,1)S(1)}, bf16[576,384]{1,0:T(8,128)(2,1)S(1)}, u32[]{:S(2)}, u32[]{:S(2)}) collective-permute-start(bf16[576,384]{1,0:T(8,128)(2,1)S(1)} %get-tuple-element.47), channel_id=1, source_target_pairs={{0,30},{1,31},{2,0},{3,1},{4,2},{5,3},{6,4},{7,5},{8,6},{9,7},{10,... | collective-permute-start | bytes 1327112 | tf_op jit(solution)/shard_map/ppermute | solution.py:22
  13.5 14.9 %collective-permute-start.8 = (bf16[576,384]{1,0:T(8,128)(2,1)S(1)}, bf16[576,384]{1,0:T(8,128)(2,1)S(1)}, u32[]{:S(2)}, u32[]{:S(2)}) collective-permute-start(bf16[576,384]{1,0:T(8,128)(2,1)S(1)} %collective-permute-done.2.c_ref.c0_ref), channel_id=1, source_target_pairs={{0,1},{1,0},{2,3},{3,2},{4,5},{5,4},{6,7},{7,6},{8,9},{9,8},{10,11... | collective-permute-start | bytes 1327112 | tf_op jit(solution)/shard_map/ppermute | solution.py:22
  18.3 10.1 %collective-permute-start.3 = (bf16[576,384]{1,0:T(8,128)(2,1)S(1)}, bf16[576,384]{1,0:T(8,128)(2,1)S(1)}, u32[]{:S(2)}, u32[]{:S(2)}) collective-permute-start(bf16[576,384]{1,0:T(8,128)(2,1)S(1)} %get-tuple-element.53), channel_id=1, source_target_pairs={{0,30},{1,31},{2,0},{3,1},{4,2},{5,3},{6,4},{7,5},{8,6},{9,7},{10,... | collective-permute-start | bytes 1327112 | tf_op jit(solution)/shard_map/ppermute | solution.py:22
  27.0 8.8 %collective-permute-start.7 = (bf16[128,384]{1,0:T(8,128)(2,1)S(1)}, bf16[128,384]{1,0:T(8,128)(2,1)S(1)}, u32[]{:S(2)}, u32[]{:S(2)}) collective-permute-start(bf16[128,384]{1,0:T(8,128)(2,1)S(1)} %get-tuple-element.64), channel_id=1, source_target_pairs={{0,2},{1,3},{2,4},{3,5},{4,6},{5,7},{6,8},{7,9},{8,10},{9,11},{10,... | collective-permute-start | bytes 294920 | tf_op jit(solution)/shard_map/ppermute | solution.py:22
  27.1 19.2 %collective-permute-start.5 = (bf16[576,256]{1,0:T(8,128)(2,1)S(1)}, bf16[576,256]{1,0:T(8,128)(2,1)S(1)}, u32[]{:S(2)}, u32[]{:S(2)}) collective-permute-start(bf16[576,256]{1,0:T(8,128)(2,1)S(1)} %get-tuple-element.61), channel_id=1, source_target_pairs={{0,3},{1,2},{2,5},{3,4},{4,7},{5,6},{6,9},{7,8},{8,11},{9,10},{10,... | collective-permute-start | bytes 884744 | tf_op jit(solution)/shard_map/ppermute | solution.py:22
  27.1 14.4 %collective-permute-start.6 = (bf16[448,384]{1,0:T(8,128)(2,1)S(1)}, bf16[448,384]{1,0:T(8,128)(2,1)S(1)}, u32[]{:S(2)}, u32[]{:S(2)}) collective-permute-start(bf16[448,384]{1,0:T(8,128)(2,1)S(1)} %get-tuple-element.63), channel_id=1, source_target_pairs={{0,2},{1,3},{2,4},{3,5},{4,6},{5,7},{6,8},{7,9},{8,10},{9,11},{10,... | collective-permute-start | bytes 1032200 | tf_op jit(solution)/shard_map/ppermute | solution.py:22
  28.4 20.3 %collective-permute-start.4 = (bf16[576,128]{1,0:T(8,128)(2,1)S(1)}, bf16[576,128]{1,0:T(8,128)(2,1)S(1)}, u32[]{:S(2)}, u32[]{:S(2)}) collective-permute-start(bf16[576,128]{1,0:T(8,128)(2,1)S(1)} %get-tuple-element.56), channel_id=1, source_target_pairs={{0,3},{1,2},{2,5},{3,4},{4,7},{5,6},{6,9},{7,8},{8,11},{9,10},{10,... | collective-permute-start | bytes 442376 | tf_op jit(solution)/shard_map/ppermute | solution.py:22
